TPU v7x, 32 devices: a whole 2x2x4 slice. The times are simulated.
32 devices in a mesh: grp: 2 (over y), anim: 8 (over z, x), mark: 2 (over core).
Axes of the slice: x: 2, y: 2, z: 4, core: 2. Of those that a mesh axis runs over, the one named last changes fastest.
Arguments:
- noncore_geno: int32 [2048, 512], P(('grp', 'anim'), 'mark'), parts along dimension 0, may hold values from 0 to 2
- noncore_codes: int32 [5, 2048], P(None, ('grp', 'anim')), parts along dimension 1, may hold values from 0 to 32, as said below
- core_geno: int32 [8192, 512], P('anim', 'mark'), may hold values from 0 to 2
- core_codes: int32 [5, 8192], P(None, 'anim'), may hold values from 0 to 32, as said below
- breed_freqs: float32 [5, 512], P(None, 'mark'), may hold values from 0.05 to 0.95
- core_inverse: bfloat16 [8192, 8192], P(None, 'anim'), may hold values from -0.25 to 0.25
Outputs:
- kinship_entries: bfloat16 [2048, 8192], P(('grp', 'anim'), 'mark'), parts along dimension 0
- inverse_weighted_kinship: bfloat16 [2048, 8192], P(('grp', 'anim'), 'mark'), parts along dimension 0
There are 2 independent parts, one for each index of `grp`. A program takes and returns all parts, laid end to end along the dimension named above; an argument that names none is the same for every part. Nothing has to cross between parts.
Inputs may be any that keep to these rules, and one draw needn't show every extreme that they name: `noncore_codes`: each animal's 5 codes sum to 32. `core_codes`: each animal's 5 codes sum to 32.
All inputs are finite; a program needn't handle non-finite values.
Results may differ from a plain program's by a relative error of at most 0.0055.
Values may be sent and summed in bfloat16 or wider, within the bound.
No kernel may reach another device: no remote copies, remote signals or barrier semaphores. Data moves between devices by JAX's collectives and lax.ppermute only.
A program may use at most 64 MiB of HBM per device.

v0:
```python
import jax
import jax.numpy as jnp
from jax import lax
from jax.sharding import PartitionSpec as P

SLAB_MARKERS = 512


def centre_value(genotypes, breed_codes, breed_freqs):
    fractions = breed_codes.astype(jnp.float32) / 32.0
    expected = lax.dot_general(
        fractions, breed_freqs, (((0,), (0,)), ((), ())), precision=lax.Precision.HIGHEST
    )
    return (genotypes.astype(jnp.float32) - 2.0 * expected).astype(jnp.bfloat16)


def body(noncore_geno, noncore_codes, core_geno, core_codes, breed_freqs, core_inverse):
    noncore_z = centre_value(noncore_geno, noncore_codes, breed_freqs)
    core_z = centre_value(core_geno, core_codes, breed_freqs)
    shard_rows = lax.all_gather(core_z, "anim", axis=0, tiled=True)
    incomplete_submatrix = (
        lax.dot_general(
            noncore_z, shard_rows, (((1,), (1,)), ((), ())), preferred_element_type=jnp.float32
        )
        / SLAB_MARKERS
    )
    related = incomplete_submatrix
    marker_loading = lax.dot_general(
        shard_rows, core_inverse, (((0,), (0,)), ((), ())), preferred_element_type=jnp.float32
    )
    related, marker_loading = (related, marker_loading)
    loading_low = marker_loading.astype(jnp.bfloat16)
    scores = (
        jnp.dot(
            noncore_z,
            lax.all_gather(loading_low, "anim", axis=1, tiled=True),
            preferred_element_type=jnp.float32,
        )
        / SLAB_MARKERS
    )
    related_sum, score_sum = (
        lax.psum_scatter(
            related.astype(jnp.bfloat16), "mark", scatter_dimension=1, tiled=True
        ).astype(jnp.float32),
        lax.psum_scatter(
            scores.astype(jnp.bfloat16), "mark", scatter_dimension=1, tiled=True
        ).astype(jnp.float32),
    )
    return (related_sum.astype(jnp.bfloat16), score_sum.astype(jnp.bfloat16))


def solution(mesh):
    in_specs = (
        P(("grp", "anim"), "mark"),
        P(None, ("grp", "anim")),
        P("anim", "mark"),
        P(None, "anim"),
        P(None, "mark"),
        P(None, "anim"),
    )
    out_specs = (P(("grp", "anim"), "mark"), P(("grp", "anim"), "mark"))
    return jax.shard_map(body, mesh=mesh, in_specs=in_specs, out_specs=out_specs, check_vma=False)
```

profile of v0, /device:TPU:0, one launch (start us, length us, event | category | flops | bytes accessed | tf_op | source)
XLA Modules:
  0.0 202.3 jit_solution(9231878696982391324)
XLA Ops:
  7.2 0.0 copy-start
  7.2 0.0 all-gather.3.cloned.1.call-start
  7.2 0.6 copy-done
  7.9 3.1 %fusion.3 = bf16[1024,256]{1,0:T(8,128)(2,1)} fusion(f32[5,256]{1,0:T(8,128)S(1)} %copy-done, s32[1024,256]{1,0:T(8,128)} %param.8, s32[5,1024]{1,0:T(8,128)} %param.9), kind=kOutput, calls=%fused_computation.6 | convolution fusion | flops 16787456 | bytes 1598464 | tf_op jit(solution)/shard_map/dot_general | solution.py:11
  11.0 0.0 all-gather.3.cloned.1.call-update
  11.0 0.0 copy-start.1
  11.0 0.0 copy-start.2
  11.0 0.0 all-gather.5.cloned.1.call-start
  11.1 76.2 %all-gather.3.cloned.1.call-done = bf16[8192,256]{1,0:T(8,128)(2,1)} async-done(((bf16[1024,256]{1,0:T(8,128)(2,1)}), bf16[8192,256]{1,0:T(8,128)(2,1)}) %all-gather.3.cloned.1.call-update) | async-done | bytes 4194320 | tf_op jit(solution)/shard_map/all_gather | solution.py:20
  87.2 12.4 %convolution_convert_fusion = bf16[256,1024]{1,0:T(8,128)(2,1)} fusion(bf16[8192,256]{1,0:T(8,128)(2,1)} %all-gather.3.cloned.1.call-done, bf16[8192,1024]{1,0:T(8,128)(2,1)} %param.11), kind=kOutput, calls=%fused_computation.7 | convolution fusion | flops 4295229440 | bytes 21495808 | tf_op jit(solution)/shard_map/dot_general | solution.py:28
  99.6 0.0 all-gather.5.cloned.1.call-update
  99.6 0.0 reduce-scatter.3.cloned.1.call-start
  99.7 0.0 copy-done.1
  99.7 0.0 copy-done.2
  99.7 0.3 fusion.5
  100.0 5.1 %fusion = bf16[128,8192]{1,0:T(8,128)(2,1)} fusion(bf16[128,256]{1,0:T(8,128)(2,1)S(1)} %fusion.5, bf16[8192,256]{1,0:T(8,128)(2,1)} %all-gather.3.cloned.1.call-done), kind=kOutput, calls=%fused_computation.2 | convolution fusion | flops 538968064 | bytes 6356992 | tf_op jit(solution)/shard_map/dot_general | solution.py:22
  105.1 0.0 reduce-scatter.3.cloned.1.call-update
  105.1 0.0 reduce-scatter.5.cloned.1.call-start
  105.2 66.2 %all-gather.5.cloned.1.call-done = bf16[256,8192]{1,0:T(8,128)(2,1)} async-done(((bf16[256,1024]{1,0:T(8,128)(2,1)}), bf16[256,8192]{1,0:T(8,128)(2,1)}) %all-gather.5.cloned.1.call-update) | async-done | bytes 4194320 | tf_op jit(solution)/shard_map/all_gather | solution.py:36
  171.4 4.3 %fusion.1 = bf16[128,8192]{1,0:T(8,128)(2,1)} fusion(bf16[128,256]{1,0:T(8,128)(2,1)S(1)} %fusion.5, bf16[256,8192]{1,0:T(8,128)(2,1)} %all-gather.5.cloned.1.call-done), kind=kOutput, calls=%fused_computation.3 | convolution fusion | flops 538968064 | bytes 6356992 | tf_op jit(solution)/shard_map/dot_general | solution.py:34
  175.7 0.0 reduce-scatter.5.cloned.1.call-update
  175.7 6.4 %reduce-scatter.3.cloned.1.call-done = bf16[128,4096]{1,0:T(8,128)(2,1)} async-done(((bf16[128,8192]{1,0:T(8,128)(2,1)}), bf16[128,4096]{1,0:T(8,128)(2,1)}) %reduce-scatter.3.cloned.1.call-update) | async-done | bytes 1048592 | tf_op jit(solution)/shard_map/reduce_scatter | solution.py:42
  182.1 13.6 %reduce-scatter.5.cloned.1.call-done = bf16[128,4096]{1,0:T(8,128)(2,1)} async-done(((bf16[128,8192]{1,0:T(8,128)(2,1)}), bf16[128,4096]{1,0:T(8,128)(2,1)}) %reduce-scatter.5.cloned.1.call-update) | async-done | bytes 1048592 | tf_op jit(solution)/shard_map/reduce_scatter | solution.py:45
Async XLA Ops:
  7.2 0.7 copy-start
  7.2 80.1 %all-gather.3.cloned.1.call-start = ((), (), s32[]{:S(2)}) async-start(), calls=%async_computation.2 | async-start | bytes 4718592 | tf_op jit(solution)/shard_map/all_gather | solution.py:20
  11.0 88.7 %copy-start.1 = (s32[128,256]{1,0:T(8,128)S(1)}, s32[128,256]{1,0:T(8,128)}, u32[]{:S(2)}) copy-start(s32[128,256]{1,0:T(8,128)} %param.6) | copy-start | bytes 393220
  11.0 88.7 %copy-start.2 = (s32[5,128]{1,0:T(8,128)S(1)}, s32[5,128]{1,0:T(8,128)}, u32[]{:S(2)}) copy-start(s32[5,128]{1,0:T(8,128)} %param.7) | copy-start | bytes 7684
  11.0 160.4 %all-gather.5.cloned.1.call-start = ((), (), s32[]{:S(2)}) async-start(), calls=%async_computation.4 | async-start | bytes 4718592 | tf_op jit(solution)/shard_map/all_gather | solution.py:36
  99.6 82.5 %reduce-scatter.3.cloned.1.call-start = ((), (), s32[]{:S(2)}) async-start(), calls=%async_computation.3 | async-start | bytes 3145728 | tf_op jit(solution)/shard_map/reduce_scatter | solution.py:42
  105.1 90.6 %reduce-scatter.5.cloned.1.call-start = ((), (), s32[]{:S(2)}) async-start(), calls=%async_computation.5 | async-start | bytes 3145728 | tf_op jit(solution)/shard_map/reduce_scatter | solution.py:45
Sparse Core Ops, SparseCore 0:
  11.1 76.0 all-gather.2
  99.7 71.6 all-gather.4
  174.2 7.8 reduce-scatter.2
  184.9 10.7 reduce-scatter.4
where the time goes:
time: 203 us; the launch traced here: 202 us
  waiting for transfers between devices  163 us (80%)
  matrix products  25.1 us (12%)
  between operations  13.8 us (7%)
    all_gather x1, waiting for transfers between devices, body(): shard_rows = lax.all_gather(core_z, 'anim', axis=0, tiled=True)  76.2 us
    all_gather x1, waiting for transfers between devices, body(): lax.all_gather(loading_low, 'anim', axis=1, tiled=True)  66.2 us
    reduce_scatter x1, waiting for transfers between devices, body(): lax.psum_scatter(scores.astype(jnp.bfloat16), 'mark', scatter_dimension=1...  13.6 us
    dot_general x1, matrix products, body(): lax.dot_general(shard_rows, core_inverse, (((0,), (0,)), ((), ())), prefe...  12.4 us
    reduce_scatter x1, waiting for transfers between devices, body(): lax.psum_scatter(related.astype(jnp.bfloat16), 'mark', scatter_dimension=...  6.44 us
    dot_general x1, matrix products, body(): lax.dot_general(noncore_z, shard_rows, (((1,), (1,)), ((), ())), preferre...  5.06 us
    dot_general x1, matrix products, body(): jnp.dot(noncore_z, lax.all_gather(loading_low, 'anim', axis=1, tiled=True...  4.26 us
  transfers between devices with their start and end apart: 4, of which 4 were waited for; matrix products, arithmetic and copies ran while one was open for 5% of the time, Pallas kernels for 0%

commit v1 on v0

v1 whole, which is shorter than its diff:
```python
import functools

import jax
import jax.numpy as jnp
from jax import lax
from jax.experimental import pallas as pl
from jax.experimental.pallas import tpu as pltpu
from jax.sharding import PartitionSpec as P

AXES = ("grp", "anim", "mark")
VMEM_LIMIT = 48 * 1024 * 1024


def whole():
    return pl.BlockSpec(memory_space=pltpu.VMEM)


def params(**more):
    return pltpu.CompilerParams(vmem_limit_bytes=VMEM_LIMIT, **more)


def shape(dims, dtype=jnp.bfloat16):
    return jax.ShapeDtypeStruct(dims, dtype)


def expected_dot(left, right):
    return lax.dot_general(
        left, right, (((0,), (0,)), ((), ())), precision=lax.Precision.HIGHEST,
        preferred_element_type=jnp.float32,
    )


def matmul(left, right):
    return jnp.dot(left, right, preferred_element_type=jnp.float32)


def centre_value(genotypes, breed_codes, breed_freqs):
    fractions = breed_codes.astype(jnp.float32) / 32.0
    expected = expected_dot(fractions, breed_freqs)
    return (genotypes.astype(jnp.float32) - 2.0 * expected).astype(jnp.bfloat16)


def gather_body(noncore_geno, noncore_codes, core_geno, core_codes, breed_freqs, core_inverse, *, n_mark):
    slab = breed_freqs.shape[1] * n_mark
    noncore_z = centre_value(noncore_geno, noncore_codes, breed_freqs)
    core_z = centre_value(core_geno, core_codes, breed_freqs)
    shard_rows = lax.all_gather(core_z, "anim", axis=0, tiled=True)
    related = (
        lax.dot_general(
            noncore_z, shard_rows, (((1,), (1,)), ((), ())), preferred_element_type=jnp.float32
        )
        / slab
    )
    loading = lax.dot_general(
        shard_rows, core_inverse, (((0,), (0,)), ((), ())), preferred_element_type=jnp.float32
    ).astype(jnp.bfloat16)
    scores = matmul(noncore_z, lax.all_gather(loading, "anim", axis=1, tiled=True)) / slab
    return tuple(
        lax.psum_scatter(part.astype(jnp.bfloat16), "mark", scatter_dimension=1, tiled=True)
        for part in (related, scores)
    )


def centre_kernel(place, geno, codes, freqs, out):
    fractions = codes[...].astype(jnp.float32) / 32.0
    expected = expected_dot(freqs[...], fractions)
    dosage = geno[...].astype(jnp.float32).T
    out[...] = (dosage - 2.0 * expected).astype(jnp.bfloat16)


def centre_core(part, core_geno, core_codes, breed_freqs):
    rows, markers = core_geno.shape[0] // 2, core_geno.shape[1]
    breeds = core_codes.shape[0]
    return pl.pallas_call(
        centre_kernel,
        grid_spec=pltpu.PrefetchScalarGridSpec(
            num_scalar_prefetch=1,
            grid=(1,),
            in_specs=[
                pl.BlockSpec((rows, markers), lambda i, place: (place[0], 0)),
                pl.BlockSpec((breeds, rows), lambda i, place: (0, place[0])),
                pl.BlockSpec((breeds, markers), lambda i, place: (0, 0)),
            ],
            out_specs=pl.BlockSpec((markers, rows), lambda i, place: (0, 0)),
        ),
        out_shape=shape((markers, rows)),
        compiler_params=params(),
        name="centre_core",
    )(part[None], core_geno, core_codes, breed_freqs)


def loading_kernel(count, first, last, place, *refs):
    pieces, refs = refs[:count], refs[count:]
    inverse, refs = refs[0], refs[1:]
    if not first:
        before, refs = refs[0], refs[1:]
    if last:
        keep, send, total = refs
    else:
        (total,) = refs
    step = pl.program_id(0)
    for i in range(count):
        @pl.when(step == i)
        def _(i=i):
            product = matmul(pieces[i][...], inverse[...])
            if i > 0:
                total[...] += product
            elif first:
                total[...] = product
            else:
                total[...] = before[...] + product

    if last:
        @pl.when(step == count - 1)
        def _():
            half = keep.shape[1]
            mine = pl.ds(pl.multiple_of(place[count] * half, half), half)
            other = pl.ds(pl.multiple_of((1 - place[count]) * half, half), half)
            keep[...] = total[:, mine]
            send[...] = total[:, other].astype(jnp.bfloat16)


def add_loadings(pieces, blocks, part, core_inverse, before, last):
    count, (markers, rows), columns = len(pieces), pieces[0].shape, core_inverse.shape[1]
    first = before is None
    fixed = lambda i, place: (0, 0)
    in_specs = [pl.BlockSpec((markers, rows), fixed) for _ in pieces]
    in_specs.append(pl.BlockSpec((rows, columns), lambda i, place: (place[i], 0)))
    operands = list(pieces) + [core_inverse]
    if not first:
        in_specs.append(pl.BlockSpec((markers, columns), fixed))
        operands.append(before)
    if last:
        half = columns // 2
        out_shape = (shape((markers, half), jnp.float32), shape((markers, half)))
        out_specs = [pl.BlockSpec((markers, half), fixed)] * 2
        scratch = [pltpu.VMEM((markers, columns), jnp.float32)]
    else:
        out_shape = shape((markers, columns), jnp.float32)
        out_specs = pl.BlockSpec((markers, columns), fixed)
        scratch = []
    place = jnp.stack(list(blocks) + [part]).astype(jnp.int32)
    return pl.pallas_call(
        functools.partial(loading_kernel, count, first, last),
        grid_spec=pltpu.PrefetchScalarGridSpec(
            num_scalar_prefetch=1, grid=(count,), in_specs=in_specs, out_specs=out_specs,
            scratch_shapes=scratch,
        ),
        out_shape=out_shape,
        compiler_params=params(),
        cost_estimate=pl.CostEstimate(
            flops=2 * count * markers * rows * columns,
            bytes_accessed=2 * count * rows * (columns + markers) + 8 * markers * columns,
            transcendentals=0,
        ),
        name="add_loadings",
    )(place, *operands)


def relation_kernel(count, scale, place, noncore, *refs):
    pieces, (own, send) = refs[:count], refs[count:]
    width = pieces[0].shape[1]
    for k in range(count):
        value = (matmul(noncore[...], pieces[k][...]) * scale).astype(jnp.bfloat16)
        columns = pl.ds(pl.multiple_of(place[2 * k + 1] * width, width), width)

        @pl.when(place[2 * k] == 1)
        def _(value=value, columns=columns):
            own[:, columns] = value

        @pl.when(place[2 * k] == 0)
        def _(value=value, columns=columns):
            send[:, columns] = value


def relate(noncore, pieces, own_flags, slots, scale):
    count, width, rows = len(pieces), pieces[0].shape[1], noncore.shape[0]
    place = jnp.stack([v for pair in zip(own_flags, slots) for v in pair]).astype(jnp.int32)
    out = shape((rows, width * count // 2))
    return pl.pallas_call(
        functools.partial(relation_kernel, count, scale),
        in_specs=[pl.BlockSpec(memory_space=pltpu.SMEM)] + [whole()] * (count + 1),
        out_specs=(whole(), whole()),
        out_shape=(out, out),
        compiler_params=params(),
        cost_estimate=pl.CostEstimate(
            flops=2 * count * rows * width * noncore.shape[1],
            bytes_accessed=4 * count * width * rows,
            transcendentals=0,
        ),
        name="relate",
    )(place, noncore, *pieces)


def regression_kernel(count, scale, place, first, second, mine, other, *outs):
    rows = outs[0].shape[0]
    for k in range(count):
        block = pl.ds(pl.multiple_of(place[k] * rows, rows), rows)
        value = matmul(first[block, :], mine[...]) + matmul(second[block, :], other[...])
        outs[k][...] = (value * scale).astype(jnp.bfloat16)


def regress(first, second, mine, other, row_blocks, scale):
    count, width = len(row_blocks), mine.shape[1]
    rows = first.shape[0] // count
    return pl.pallas_call(
        functools.partial(regression_kernel, count, scale),
        in_specs=[pl.BlockSpec(memory_space=pltpu.SMEM)] + [whole()] * 4,
        out_specs=[whole()] * count,
        out_shape=[shape((rows, width))] * count,
        compiler_params=params(),
        cost_estimate=pl.CostEstimate(
            flops=4 * first.size * width, bytes_accessed=2 * (4 * first.size + 2 * mine.size),
            transcendentals=0,
        ),
        name="regress",
    )(jnp.stack(row_blocks).astype(jnp.int32), first, second, mine, other)


def assemble_kernel(width, place, *refs):
    parts, out = refs[:-1], refs[-1]
    slot = 0
    for part in parts:
        for start in range(0, part.shape[1], width):
            columns = pl.ds(pl.multiple_of(place[slot] * width, width), width)
            out[:, columns] = part[:, start:start + width]
            slot += 1


def assemble(parts, slots, width):
    rows = parts[0].shape[0]
    return pl.pallas_call(
        functools.partial(assemble_kernel, width),
        in_specs=[pl.BlockSpec(memory_space=pltpu.SMEM)] + [whole()] * len(parts),
        out_specs=whole(),
        out_shape=shape((rows, width * len(slots))),
        compiler_params=params(),
        name="assemble",
    )(jnp.stack(slots).astype(jnp.int32), *parts)


def permute_body(
    noncore_geno, noncore_codes, core_geno, core_codes, breed_freqs, core_inverse, *, n_anim, n_mark
):
    markers = breed_freqs.shape[1]
    scale = 1.0 / (markers * n_mark)
    top = n_anim // 2
    grp, anim, mark = (lax.axis_index(name) for name in AXES)

    def move(array, target):
        pairs = []
        for g in range(2):
            for a in range(n_anim):
                for m in range(2):
                    tg, ta, tm = target(g, a, m)
                    pairs.append(((g * n_anim + a) * 2 + m, (tg * n_anim + ta) * 2 + tm))
        return lax.ppermute(array, AXES, pairs)

    def along_anim(array, bits):
        return move(array, lambda g, a, m: (g, a ^ bits, m))

    def across_grp(array):
        return move(array, lambda g, a, m: (1 - g, a, m))

    def across_mark(array):
        return move(array, lambda g, a, m: (g, a, 1 - m))

    own = centre_core(grp, core_geno, core_codes, breed_freqs)
    pieces = {0: own}
    far = [top] + [b for b in range(2, n_anim, 2) if b != top]
    for bits in far:
        pieces[bits] = along_anim(own, bits)
    pieces[1] = along_anim(own, 1)
    for bits in far:
        pieces[bits + 1] = along_anim(pieces[bits], 1)

    noncore_z = centre_value(noncore_geno, noncore_codes, breed_freqs)
    both = jnp.concatenate([noncore_z, across_grp(noncore_z)], axis=0)
    gathered = noncore_z
    bit = 1
    while bit < n_anim:
        gathered = jnp.concatenate([gathered, along_anim(gathered, bit)], axis=0)
        bit *= 2
    one = move(gathered, lambda g, a, m: (1 - g, a, m) if m == g else (g, a, 1 - m))
    two = move(gathered, lambda g, a, m: (1 - g, a, 1 - m))
    at_home = mark == grp
    first = jnp.where(at_home, gathered, one)
    second = jnp.where(at_home, one, two)

    early = [0, 1] + [b for b in far[:1]]
    late = [b for b in range(n_anim) if b not in early]
    block = lambda bits: (anim ^ bits) * 2 + grp
    total = add_loadings(
        [pieces[b] for b in early], [block(b) for b in early], grp, core_inverse, None, False
    )
    keep, send = add_loadings(
        [pieces[b] for b in late], [block(b) for b in late], grp, core_inverse, total, True
    )
    mine = (keep + across_grp(send).astype(jnp.float32)).astype(jnp.bfloat16)
    other = across_mark(mine)

    high = (anim // top) ^ grp
    row_blocks = [(high ^ (k // top)) * top + k % top for k in range(n_anim)]
    results = regress(first, second, mine, other, row_blocks, scale)
    arrived = [
        move(
            results[k],
            lambda g, a, m, k=k: (m, (g * top + a % top) ^ k, a // top),
        )
        for k in range(n_anim)
    ]
    slots = [((anim ^ k) % top) * 2 + (anim ^ k) // top for k in range(n_anim)]
    weighted = assemble(arrived, slots, own.shape[1])

    own_part, send_part = relate(
        both,
        [pieces[k] for k in range(n_anim)],
        [((anim ^ k) // top == mark).astype(jnp.int32) for k in range(n_anim)],
        [(anim ^ k) % top for k in range(n_anim)],
        scale,
    )
    summed = (
        own_part.astype(jnp.float32) + across_mark(send_part).astype(jnp.float32)
    ).astype(jnp.bfloat16)
    rows = noncore_z.shape[0]
    kept, from_other = summed[:rows], across_grp(summed[rows:])
    slots = [2 * i + grp for i in range(top)] + [2 * i + 1 - grp for i in range(top)]
    kinship = assemble([kept, from_other], slots, own.shape[1])
    return kinship, weighted


def solution(mesh):
    in_specs = (
        P(("grp", "anim"), "mark"),
        P(None, ("grp", "anim")),
        P("anim", "mark"),
        P(None, "anim"),
        P(None, "mark"),
        P(None, "anim"),
    )
    out_specs = (P(("grp", "anim"), "mark"), P(("grp", "anim"), "mark"))
    n_grp, n_anim, n_mark = (mesh.shape[name] for name in AXES)
    if n_grp == 2 and n_mark == 2 and n_anim in (4, 8, 16):
        body = functools.partial(permute_body, n_anim=n_anim, n_mark=n_mark)
    else:
        body = functools.partial(gather_body, n_mark=n_mark)
    return jax.shard_map(body, mesh=mesh, in_specs=in_specs, out_specs=out_specs, check_vma=False)
```

time: 203 us -> 145 us (0.71)
  waiting for transfers between devices: 163 us -> 66 us
  starting transfers between devices: 0.16 us -> 49.7 us
  matrix products: 25.1 us -> 1.25 us
  Pallas kernels: 0 us -> 18.2 us
  between operations: 13.8 us -> 0.81 us
  other arithmetic: 0 us -> 4.71 us
  local copies, waits for them, and re-layouts: 0.66 us -> 3.98 us
    all_gather x2 -> x0, waiting for transfers between devices: 142 us -> none  [the longest x1 76.2 us: body(): shard_rows = lax.all_gather(core_z, 'anim', axis=0, tiled=True)]
    ppermute x0 -> x25, waiting for transfers between devices: none -> 66 us  [move(): return lax.ppermute(array, AXES, pairs)]
    ppermute x0 -> x25, starting transfers between devices: none -> 49.7 us  [move(): return lax.ppermute(array, AXES, pairs)]
    dot_general x5 -> x1, matrix products: 25.1 us -> 1.25 us  [expected_dot(): lax.dot_general(left, right, (((0,), (0,)), ((), ())), precision=lax.Prec...]
    reduce_scatter x2 -> x0, waiting for transfers between devices: 20 us -> none  [the longest x1 13.6 us: body(): lax.psum_scatter(scores.astype(jnp.bfloat16), 'mark', scatter_dimension=1...]
    pallas_call x0 -> x7, Pallas kernels: none -> 18.2 us  [the longest x2 9.62 us: add_loadings(): pl.pallas_call(functools.partial(loading_kernel, count, first, last), gri...]
  transfers between devices with their start and end apart: 4 -> 25, of which waited for: 4 -> 11; matrix products, arithmetic and copies ran while one was open for 5% -> 5% of each run, Pallas kernels for 0% -> 9%
where the time goes in v1:
time: 145 us
  waiting for transfers between devices  66 us (46%)
  starting transfers between devices  49.7 us (34%)
  Pallas kernels  18.2 us (13%)
  other arithmetic  4.71 us (3%)
  local copies, waits for them, and re-layouts  3.98 us (3%)
    ppermute x25, waiting for transfers between devices, move(): return lax.ppermute(array, AXES, pairs)  66 us
    ppermute x25, starting transfers between devices, move(): return lax.ppermute(array, AXES, pairs)  49.7 us
    pallas_call x2, Pallas kernels, add_loadings(): pl.pallas_call(functools.partial(loading_kernel, count, first, last), gri...  9.62 us
    pallas_call x1, Pallas kernels, relate(): pl.pallas_call(functools.partial(relation_kernel, count, scale), in_specs...  3.57 us
    pallas_call x2, Pallas kernels, assemble(): pl.pallas_call(functools.partial(assemble_kernel, width), in_specs=[pl.Bl...  3.18 us
  transfers between devices with their start and end apart: 25, of which 11 were waited for; matrix products, arithmetic and copies ran while one was open for 5% of the time, Pallas kernels for 9%

profile of v1, /device:TPU:0, one launch (start us, length us, event | category | flops | bytes accessed | tf_op | source)
XLA Modules:
  0.0 144.7 jit_solution(1839380892899073844)
XLA Ops:
  3.9 3.1 %collective-permute-start.2 = (bf16[256,512]{1,0:T(8,128)(2,1)S(1)}, bf16[256,512]{1,0:T(8,128)(2,1)S(1)}, u32[]{:S(2)}, u32[]{:S(2)}) collective-permute-start(bf16[256,512]{1,0:T(8,128)(2,1)S(1)} %centre_core.1.refs_0_), channel_id=1, source_target_pairs={{0,4},{1,5},{2,6},{3,7},{4,0},{5,1},{6,2},{7,3},{8,12},{9,13},{10,... | collective-permute-start | bytes 786440 | tf_op jit(solution)/shard_map/ppermute | solution.py:257
  7.0 2.6 %collective-permute-start.4 = (bf16[256,512]{1,0:T(8,128)(2,1)S(1)}, bf16[256,512]{1,0:T(8,128)(2,1)S(1)}, u32[]{:S(2)}, u32[]{:S(2)}) collective-permute-start(bf16[256,512]{1,0:T(8,128)(2,1)S(1)} %centre_core.1.refs_0_), channel_id=1, source_target_pairs={{0,8},{1,9},{2,10},{3,11},{4,12},{5,13},{6,14},{7,15},{8,0},{9,1},... | collective-permute-start | bytes 786440 | tf_op jit(solution)/shard_map/ppermute | solution.py:257
  9.6 1.7 %collective-permute-start.1 = (bf16[256,512]{1,0:T(8,128)(2,1)S(1)}, bf16[256,512]{1,0:T(8,128)(2,1)S(1)}, u32[]{:S(2)}, u32[]{:S(2)}) collective-permute-start(bf16[256,512]{1,0:T(8,128)(2,1)S(1)} %centre_core.1.refs_0_), channel_id=1, source_target_pairs={{0,2},{1,3},{2,0},{3,1},{4,6},{5,7},{6,4},{7,5},{8,10},{9,11},{10,... | collective-permute-start | bytes 786440 | tf_op jit(solution)/shard_map/ppermute | solution.py:257
  11.3 6.8 %collective-permute-done.2.refs_2_.refs_0_ = bf16[256,512]{1,0:T(8,128)(2,1)S(1)} collective-permute-done((bf16[256,512]{1,0:T(8,128)(2,1)S(1)}, bf16[256,512]{1,0:T(8,128)(2,1)S(1)}, u32[]{:S(2)}, u32[]{:S(2)}) %collective-permute-start.2) | collective-permute-done | bytes 262176 | tf_op jit(solution)/shard_map/ppermute | solution.py:257
  18.2 1.7 %collective-permute-start.3 = (bf16[256,512]{1,0:T(8,128)(2,1)S(1)}, bf16[256,512]{1,0:T(8,128)(2,1)S(1)}, u32[]{:S(2)}, u32[]{:S(2)}) collective-permute-start(bf16[256,512]{1,0:T(8,128)(2,1)S(1)} %collective-permute-done.2.refs_2_.refs_0_), channel_id=1, source_target_pairs={{0,2},{1,3},{2,0},{3,1},{4,6},{5,7},{6,4},{7,5},{8,10},{9,11},{10,... | collective-permute-start | bytes 786440 | tf_op jit(solution)/shard_map/ppermute | solution.py:257
  19.8 8.6 %collective-permute-done.4.refs_4_.refs_2_ = bf16[256,512]{1,0:T(8,128)(2,1)S(1)} collective-permute-done((bf16[256,512]{1,0:T(8,128)(2,1)S(1)}, bf16[256,512]{1,0:T(8,128)(2,1)S(1)}, u32[]{:S(2)}, u32[]{:S(2)}) %collective-permute-start.4) | collective-permute-done | bytes 262176 | tf_op jit(solution)/shard_map/ppermute | solution.py:257
  28.4 1.5 %collective-permute-start.5 = (bf16[256,512]{1,0:T(8,128)(2,1)S(1)}, bf16[256,512]{1,0:T(8,128)(2,1)S(1)}, u32[]{:S(2)}, u32[]{:S(2)}) collective-permute-start(bf16[256,512]{1,0:T(8,128)(2,1)S(1)} %collective-permute-done.4.refs_4_.refs_2_), channel_id=1, source_target_pairs={{0,2},{1,3},{2,0},{3,1},{4,6},{5,7},{6,4},{7,5},{8,10},{9,11},{10,... | collective-permute-start | bytes 786440 | tf_op jit(solution)/shard_map/ppermute | solution.py:257
  31.7 1.6 %collective-permute-start.10 = (bf16[128,256]{1,0:T(8,128)(2,1)S(1)}, bf16[128,256]{1,0:T(8,128)(2,1)S(1)}, u32[]{:S(2)}, u32[]{:S(2)}) collective-permute-start(bf16[128,256]{1,0:T(8,128)(2,1)S(1)} %fusion.1), channel_id=1, source_target_pairs={{0,2},{1,3},{2,0},{3,1},{4,6},{5,7},{6,4},{7,5},{8,10},{9,11},{10,... | collective-permute-start | bytes 196616 | tf_op jit(solution)/shard_map/ppermute | solution.py:257
  33.2 5.1 %collective-permute-done.10 = bf16[128,256]{1,0:T(8,128)(2,1)S(1)} collective-permute-done((bf16[128,256]{1,0:T(8,128)(2,1)S(1)}, bf16[128,256]{1,0:T(8,128)(2,1)S(1)}, u32[]{:S(2)}, u32[]{:S(2)}) %collective-permute-start.10) | collective-permute-done | bytes 65568 | tf_op jit(solution)/shard_map/ppermute | solution.py:257
  38.3 1.5 %collective-permute-start = (bf16[128,256]{1,0:T(8,128)(2,1)S(1)}, bf16[128,256]{1,0:T(8,128)(2,1)S(1)}, u32[]{:S(2)}, u32[]{:S(2)}) collective-permute-start(bf16[128,256]{1,0:T(8,128)(2,1)S(1)} %fusion.1), channel_id=1, source_target_pairs={{0,16},{1,17},{2,18},{3,19},{4,20},{5,21},{6,22},{7,23},{8,24},{9,... | collective-permute-start | bytes 196616 | tf_op jit(solution)/shard_map/ppermute | solution.py:257
  39.9 2.7 %collective-permute-done = bf16[128,256]{1,0:T(8,128)(2,1)S(1)} collective-permute-done((bf16[128,256]{1,0:T(8,128)(2,1)S(1)}, bf16[128,256]{1,0:T(8,128)(2,1)S(1)}, u32[]{:S(2)}, u32[]{:S(2)}) %collective-permute-start) | collective-permute-done | bytes 65568 | tf_op jit(solution)/shard_map/ppermute | solution.py:257
  42.7 3.6 %relate.1 = (bf16[256,2048]{1,0:T(8,128)(2,1)S(1)}, bf16[256,2048]{1,0:T(8,128)(2,1)}) custom-call(s32[16]{0:T(128)S(1)} %stack.221.place, bf16[256,256]{1,0:T(8,128)(2,1)S(1)} %get-tuple-element.31.noncore, bf16[256,512]{1,0:T(8,128)(2,1)S(1)} %centre_core.1.refs_0_, bf16[256,512]{1,0:T(8,128)(2,1)S(1)} %collective-permute-done.1.refs_1_, ...), custom_call_target="tpu_custom_call" | custom-call | flops 536870912 | bytes 4194304 | tf_op jit(solution)/shard_map/relate/pallas_call | solution.py:180
  46.2 3.1 %collective-permute-start.11 = (bf16[256,256]{1,0:T(8,128)(2,1)S(1)}, bf16[256,256]{1,0:T(8,128)(2,1)S(1)}, u32[]{:S(2)}, u32[]{:S(2)}) collective-permute-start(bf16[256,256]{1,0:T(8,128)(2,1)S(1)} %get-tuple-element.30), channel_id=1, source_target_pairs={{0,4},{1,5},{2,6},{3,7},{4,0},{5,1},{6,2},{7,3},{8,12},{9,13},{10,... | collective-permute-start | bytes 393224 | tf_op jit(solution)/shard_map/ppermute | solution.py:257
  49.5 4.0 %collective-permute-done.11 = bf16[256,256]{1,0:T(8,128)(2,1)S(1)} collective-permute-done((bf16[256,256]{1,0:T(8,128)(2,1)S(1)}, bf16[256,256]{1,0:T(8,128)(2,1)S(1)}, u32[]{:S(2)}, u32[]{:S(2)}) %collective-permute-start.11) | collective-permute-done | bytes 131104 | tf_op jit(solution)/shard_map/ppermute | solution.py:257
  54.2 2.8 %collective-permute-start.12 = (bf16[512,256]{1,0:T(8,128)(2,1)}, bf16[512,256]{1,0:T(8,128)(2,1)}, u32[]{:S(2)}, u32[]{:S(2)}) collective-permute-start(bf16[512,256]{1,0:T(8,128)(2,1)} %pad_maximum_fusion.1), channel_id=1, source_target_pairs={{0,8},{1,9},{2,10},{3,11},{4,12},{5,13},{6,14},{7,15},{8,0},{9,1},... | collective-permute-start | bytes 786440 | tf_op jit(solution)/shard_map/ppermute | solution.py:257
  57.0 3.9 %add_loadings.2.refs_6_ = f32[256,1024]{1,0:T(8,128)S(1)} custom-call(s32[4]{0:T(128)S(1)} %pad_add_fusion.place, bf16[256,512]{1,0:T(8,128)(2,1)S(1)} %centre_core.1.refs_0_, bf16[256,512]{1,0:T(8,128)(2,1)S(1)} %collective-permute-done.1.refs_1_, bf16[256,512]{1,0:T(8,128)(2,1)S(1)} %collective-permute-done.4.refs_4_.refs_2_, bf16[8192,1024]{1,0:T(8,128)(2,1)} %refs_5_.1), custom_call_target="tpu_custom_call" | custom-call | flops 805306368 | bytes 6029312 | tf_op jit(solution)/shard_map/add_loadings/pallas_call | solution.py:143
  61.0 5.7 %add_loadings.3 = (f32[256,512]{1,0:T(8,128)S(1)}, bf16[256,512]{1,0:T(8,128)(2,1)S(1)}) custom-call(s32[6]{0:T(128)S(1)} %stack.245.place, bf16[256,512]{1,0:T(8,128)(2,1)S(1)} %collective-permute-done.2.refs_2_.refs_0_, bf16[256,512]{1,0:T(8,128)(2,1)S(1)} %collective-permute-done.3.refs_3_.refs_1_, ...), custom_call_target="tpu_custom_call" | custom-call | flops 1342177280 | bytes 8650752 | tf_op jit(solution)/shard_map/add_loadings/pallas_call | solution.py:143
  66.7 1.6 %collective-permute-start.15 = (bf16[256,512]{1,0:T(8,128)(2,1)S(1)}, bf16[256,512]{1,0:T(8,128)(2,1)S(1)}, u32[]{:S(2)}, u32[]{:S(2)}) collective-permute-start(bf16[256,512]{1,0:T(8,128)(2,1)S(1)} %get-tuple-element.17), channel_id=1, source_target_pairs={{0,16},{1,17},{2,18},{3,19},{4,20},{5,21},{6,22},{7,23},{8,24},{9,... | collective-permute-start | bytes 786440 | tf_op jit(solution)/shard_map/ppermute | solution.py:257
  70.2 1.6 %collective-permute-start.13 = (bf16[1024,256]{1,0:T(8,128)(2,1)S(1)}, bf16[1024,256]{1,0:T(8,128)(2,1)S(1)}, u32[]{:S(2)}, u32[]{:S(2)}) collective-permute-start(bf16[1024,256]{1,0:T(8,128)(2,1)S(1)} %pad_maximum_fusion), channel_id=1, source_target_pairs={{0,16},{1,0},{2,18},{3,2},{4,20},{5,4},{6,22},{7,6},{8,24},{9,8},{... | collective-permute-start | bytes 1572872 | tf_op jit(solution)/shard_map/ppermute | solution.py:257
  71.8 4.2 %collective-permute-done.15 = bf16[256,512]{1,0:T(8,128)(2,1)S(1)} collective-permute-done((bf16[256,512]{1,0:T(8,128)(2,1)S(1)}, bf16[256,512]{1,0:T(8,128)(2,1)S(1)}, u32[]{:S(2)}, u32[]{:S(2)}) %collective-permute-start.15) | collective-permute-done | bytes 262176 | tf_op jit(solution)/shard_map/ppermute | solution.py:257
  76.1 1.6 %add_convert_fusion = bf16[256,2048]{1,0:T(8,128)(2,1)S(1)} fusion(bf16[256,2048]{1,0:T(8,128)(2,1)} %collective-permute-done.8, bf16[256,2048]{1,0:T(8,128)(2,1)S(1)} %get-tuple-element.14), kind=kLoop, calls=%fused_computation | loop fusion | flops 2097152 | bytes 3145728 | tf_op jit(solution)/shard_map/convert_element_type | solution.py:324
  79.6 6.1 %collective-permute-done.13 = bf16[1024,256]{1,0:T(8,128)(2,1)S(1)} collective-permute-done((bf16[1024,256]{1,0:T(8,128)(2,1)S(1)}, bf16[1024,256]{1,0:T(8,128)(2,1)S(1)}, u32[]{:S(2)}, u32[]{:S(2)}) %collective-permute-start.13) | collective-permute-done | bytes 524320 | tf_op jit(solution)/shard_map/ppermute | solution.py:257
  85.6 11.2 %collective-permute-done.14 = bf16[1024,256]{1,0:T(8,128)(2,1)S(1)} collective-permute-done((bf16[1024,256]{1,0:T(8,128)(2,1)S(1)}, bf16[1024,256]{1,0:T(8,128)(2,1)S(1)}, u32[]{:S(2)}, u32[]{:S(2)}) %collective-permute-start.14) | collective-permute-done | bytes 524320 | tf_op jit(solution)/shard_map/ppermute | solution.py:257
  98.1 1.3 regress.1
  100.0 1.5 %collective-permute-start.18 = (bf16[128,512]{1,0:T(8,128)(2,1)S(1)}, bf16[128,512]{1,0:T(8,128)(2,1)S(1)}, u32[]{:S(2)}, u32[]{:S(2)}) collective-permute-start(bf16[128,512]{1,0:T(8,128)(2,1)S(1)} %get-tuple-element.19), channel_id=1, source_target_pairs={{0,2},{1,18},{2,0},{3,16},{4,6},{5,22},{6,4},{7,20},{8,3},{9,19},{... | collective-permute-start | bytes 393224 | tf_op jit(solution)/shard_map/ppermute | solution.py:257
  103.6 4.3 %collective-permute-start.21 = (bf16[128,512]{1,0:T(8,128)(2,1)S(1)}, bf16[128,512]{1,0:T(8,128)(2,1)S(1)}, u32[]{:S(2)}, u32[]{:S(2)}) collective-permute-start(bf16[128,512]{1,0:T(8,128)(2,1)S(1)} %get-tuple-element.22), channel_id=1, source_target_pairs={{0,8},{1,24},{2,10},{3,26},{4,12},{5,28},{6,14},{7,30},{8,9},{9,25... | collective-permute-start | bytes 393224 | tf_op jit(solution)/shard_map/ppermute | solution.py:257
  107.9 10.8 %collective-permute-start.22 = (bf16[128,512]{1,0:T(8,128)(2,1)S(1)}, bf16[128,512]{1,0:T(8,128)(2,1)S(1)}, u32[]{:S(2)}, u32[]{:S(2)}) collective-permute-start(bf16[128,512]{1,0:T(8,128)(2,1)S(1)} %get-tuple-element.23), channel_id=1, source_target_pairs={{0,10},{1,26},{2,8},{3,24},{4,14},{5,30},{6,12},{7,28},{8,11},{9,2... | collective-permute-start | bytes 393224 | tf_op jit(solution)/shard_map/ppermute | solution.py:257
  118.7 6.1 %collective-permute-start.23 = (bf16[128,512]{1,0:T(8,128)(2,1)S(1)}, bf16[128,512]{1,0:T(8,128)(2,1)S(1)}, u32[]{:S(2)}, u32[]{:S(2)}) collective-permute-start(bf16[128,512]{1,0:T(8,128)(2,1)S(1)} %get-tuple-element.24), channel_id=1, source_target_pairs={{0,12},{1,28},{2,14},{3,30},{4,8},{5,24},{6,10},{7,26},{8,13},{9,2... | collective-permute-start | bytes 393224 | tf_op jit(solution)/shard_map/ppermute | solution.py:257
  125.1 11.0 %collective-permute-done.23.refs_6_ = bf16[128,512]{1,0:T(8,128)(2,1)S(1)} collective-permute-done((bf16[128,512]{1,0:T(8,128)(2,1)S(1)}, bf16[128,512]{1,0:T(8,128)(2,1)S(1)}, u32[]{:S(2)}, u32[]{:S(2)}) %collective-permute-start.23) | collective-permute-done | bytes 131104 | tf_op jit(solution)/shard_map/ppermute | solution.py:257
  136.1 5.4 %collective-permute-done.24.refs_7_ = bf16[128,512]{1,0:T(8,128)(2,1)S(1)} collective-permute-done((bf16[128,512]{1,0:T(8,128)(2,1)S(1)}, bf16[128,512]{1,0:T(8,128)(2,1)S(1)}, u32[]{:S(2)}, u32[]{:S(2)}) %collective-permute-start.24) | collective-permute-done | bytes 131104 | tf_op jit(solution)/shard_map/ppermute | solution.py:257
  141.5 1.6 %assemble.3 = bf16[128,4096]{1,0:T(8,128)(2,1)} custom-call(s32[8]{0:T(128)S(1)} %stack.230.place, bf16[128,512]{1,0:T(8,128)(2,1)S(1)} %collective-permute-done.17.refs_0_, bf16[128,512]{1,0:T(8,128)(2,1)S(1)} %collective-permute-done.18.refs_1_, bf16[128,512]{1,0:T(8,128)(2,1)S(1)} %collective-permute-done.19.refs_2_, ...), custom_call_target="tpu_custom_call" | custom-call | tf_op jit(solution)/shard_map/assemble/pallas_call | solution.py:232
  143.1 1.6 %assemble.2 = bf16[128,4096]{1,0:T(8,128)(2,1)} custom-call(s32[8]{0:T(128)S(1)} %stack.196.place, bf16[128,2048]{1,0:T(8,128)(2,1)S(1)} %get-tuple-element.27.refs_0_, bf16[128,2048]{1,0:T(8,128)(2,1)S(1)} %collective-permute-done.9.refs_1_), custom_call_target="tpu_custom_call" | custom-call | tf_op jit(solution)/shard_map/assemble/pallas_call | solution.py:232
  (45 shorter events, 14.2 us)
Async XLA Ops:
  0.6 1.2 copy-start
  1.9 0.7 copy-start.1
  2.6 0.8 copy-start.2
  3.9 14.2 %collective-permute-start.2 = (bf16[256,512]{1,0:T(8,128)(2,1)S(1)}, bf16[256,512]{1,0:T(8,128)(2,1)S(1)}, u32[]{:S(2)}, u32[]{:S(2)}) collective-permute-start(bf16[256,512]{1,0:T(8,128)(2,1)S(1)} %centre_core.1.refs_0_), channel_id=1, source_target_pairs={{0,4},{1,5},{2,6},{3,7},{4,0},{5,1},{6,2},{7,3},{8,12},{9,13},{10,... | collective-permute-start | bytes 786440 | tf_op jit(solution)/shard_map/ppermute | solution.py:257
  7.0 21.4 %collective-permute-start.4 = (bf16[256,512]{1,0:T(8,128)(2,1)S(1)}, bf16[256,512]{1,0:T(8,128)(2,1)S(1)}, u32[]{:S(2)}, u32[]{:S(2)}) collective-permute-start(bf16[256,512]{1,0:T(8,128)(2,1)S(1)} %centre_core.1.refs_0_), channel_id=1, source_target_pairs={{0,8},{1,9},{2,10},{3,11},{4,12},{5,13},{6,14},{7,15},{8,0},{9,1},... | collective-permute-start | bytes 786440 | tf_op jit(solution)/shard_map/ppermute | solution.py:257
  9.6 20.3 %collective-permute-start.6 = (bf16[256,512]{1,0:T(8,128)(2,1)S(1)}, bf16[256,512]{1,0:T(8,128)(2,1)S(1)}, u32[]{:S(2)}, u32[]{:S(2)}) collective-permute-start(bf16[256,512]{1,0:T(8,128)(2,1)S(1)} %centre_core.1.refs_0_), channel_id=1, source_target_pairs={{0,12},{1,13},{2,14},{3,15},{4,8},{5,9},{6,10},{7,11},{8,4},{9,5},... | collective-permute-start | bytes 786440 | tf_op jit(solution)/shard_map/ppermute | solution.py:257
  9.6 33.0 %collective-permute-start.1 = (bf16[256,512]{1,0:T(8,128)(2,1)S(1)}, bf16[256,512]{1,0:T(8,128)(2,1)S(1)}, u32[]{:S(2)}, u32[]{:S(2)}) collective-permute-start(bf16[256,512]{1,0:T(8,128)(2,1)S(1)} %centre_core.1.refs_0_), channel_id=1, source_target_pairs={{0,2},{1,3},{2,0},{3,1},{4,6},{5,7},{6,4},{7,5},{8,10},{9,11},{10,... | collective-permute-start | bytes 786440 | tf_op jit(solution)/shard_map/ppermute | solution.py:257
  18.2 24.4 %collective-permute-start.3 = (bf16[256,512]{1,0:T(8,128)(2,1)S(1)}, bf16[256,512]{1,0:T(8,128)(2,1)S(1)}, u32[]{:S(2)}, u32[]{:S(2)}) collective-permute-start(bf16[256,512]{1,0:T(8,128)(2,1)S(1)} %collective-permute-done.2.refs_2_.refs_0_), channel_id=1, source_target_pairs={{0,2},{1,3},{2,0},{3,1},{4,6},{5,7},{6,4},{7,5},{8,10},{9,11},{10,... | collective-permute-start | bytes 786440 | tf_op jit(solution)/shard_map/ppermute | solution.py:257
  28.4 14.2 %collective-permute-start.5 = (bf16[256,512]{1,0:T(8,128)(2,1)S(1)}, bf16[256,512]{1,0:T(8,128)(2,1)S(1)}, u32[]{:S(2)}, u32[]{:S(2)}) collective-permute-start(bf16[256,512]{1,0:T(8,128)(2,1)S(1)} %collective-permute-done.4.refs_4_.refs_2_), channel_id=1, source_target_pairs={{0,2},{1,3},{2,0},{3,1},{4,6},{5,7},{6,4},{7,5},{8,10},{9,11},{10,... | collective-permute-start | bytes 786440 | tf_op jit(solution)/shard_map/ppermute | solution.py:257
  29.9 12.7 %collective-permute-start.7 = (bf16[256,512]{1,0:T(8,128)(2,1)S(1)}, bf16[256,512]{1,0:T(8,128)(2,1)S(1)}, u32[]{:S(2)}, u32[]{:S(2)}) collective-permute-start(bf16[256,512]{1,0:T(8,128)(2,1)S(1)} %collective-permute-done.6.refs_6_.refs_3_), channel_id=1, source_target_pairs={{0,2},{1,3},{2,0},{3,1},{4,6},{5,7},{6,4},{7,5},{8,10},{9,11},{10,... | collective-permute-start | bytes 786440 | tf_op jit(solution)/shard_map/ppermute | solution.py:257
  31.7 6.6 %collective-permute-start.10 = (bf16[128,256]{1,0:T(8,128)(2,1)S(1)}, bf16[128,256]{1,0:T(8,128)(2,1)S(1)}, u32[]{:S(2)}, u32[]{:S(2)}) collective-permute-start(bf16[128,256]{1,0:T(8,128)(2,1)S(1)} %fusion.1), channel_id=1, source_target_pairs={{0,2},{1,3},{2,0},{3,1},{4,6},{5,7},{6,4},{7,5},{8,10},{9,11},{10,... | collective-permute-start | bytes 196616 | tf_op jit(solution)/shard_map/ppermute | solution.py:257
  38.3 4.3 %collective-permute-start = (bf16[128,256]{1,0:T(8,128)(2,1)S(1)}, bf16[128,256]{1,0:T(8,128)(2,1)S(1)}, u32[]{:S(2)}, u32[]{:S(2)}) collective-permute-start(bf16[128,256]{1,0:T(8,128)(2,1)S(1)} %fusion.1), channel_id=1, source_target_pairs={{0,16},{1,17},{2,18},{3,19},{4,20},{5,21},{6,22},{7,23},{8,24},{9,... | collective-permute-start | bytes 196616 | tf_op jit(solution)/shard_map/ppermute | solution.py:257
  46.2 29.9 %collective-permute-start.8 = (bf16[256,2048]{1,0:T(8,128)(2,1)}, bf16[256,2048]{1,0:T(8,128)(2,1)}, u32[]{:S(2)}, u32[]{:S(2)}) collective-permute-start(bf16[256,2048]{1,0:T(8,128)(2,1)} %get-tuple-element.15), channel_id=1, source_target_pairs={{0,1},{1,0},{2,3},{3,2},{4,5},{5,4},{6,7},{7,6},{8,9},{9,8},{10,11... | collective-permute-start | bytes 3145736 | tf_op jit(solution)/shard_map/ppermute | solution.py:257
  46.2 7.3 %collective-permute-start.11 = (bf16[256,256]{1,0:T(8,128)(2,1)S(1)}, bf16[256,256]{1,0:T(8,128)(2,1)S(1)}, u32[]{:S(2)}, u32[]{:S(2)}) collective-permute-start(bf16[256,256]{1,0:T(8,128)(2,1)S(1)} %get-tuple-element.30), channel_id=1, source_target_pairs={{0,4},{1,5},{2,6},{3,7},{4,0},{5,1},{6,2},{7,3},{8,12},{9,13},{10,... | collective-permute-start | bytes 393224 | tf_op jit(solution)/shard_map/ppermute | solution.py:257
  54.2 15.0 %collective-permute-start.12 = (bf16[512,256]{1,0:T(8,128)(2,1)}, bf16[512,256]{1,0:T(8,128)(2,1)}, u32[]{:S(2)}, u32[]{:S(2)}) collective-permute-start(bf16[512,256]{1,0:T(8,128)(2,1)} %pad_maximum_fusion.1), channel_id=1, source_target_pairs={{0,8},{1,9},{2,10},{3,11},{4,12},{5,13},{6,14},{7,15},{8,0},{9,1},... | collective-permute-start | bytes 786440 | tf_op jit(solution)/shard_map/ppermute | solution.py:257
  66.7 9.3 %collective-permute-start.15 = (bf16[256,512]{1,0:T(8,128)(2,1)S(1)}, bf16[256,512]{1,0:T(8,128)(2,1)S(1)}, u32[]{:S(2)}, u32[]{:S(2)}) collective-permute-start(bf16[256,512]{1,0:T(8,128)(2,1)S(1)} %get-tuple-element.17), channel_id=1, source_target_pairs={{0,16},{1,17},{2,18},{3,19},{4,20},{5,21},{6,22},{7,23},{8,24},{9,... | collective-permute-start | bytes 786440 | tf_op jit(solution)/shard_map/ppermute | solution.py:257
  70.2 15.4 %collective-permute-start.13 = (bf16[1024,256]{1,0:T(8,128)(2,1)S(1)}, bf16[1024,256]{1,0:T(8,128)(2,1)S(1)}, u32[]{:S(2)}, u32[]{:S(2)}) collective-permute-start(bf16[1024,256]{1,0:T(8,128)(2,1)S(1)} %pad_maximum_fusion), channel_id=1, source_target_pairs={{0,16},{1,0},{2,18},{3,2},{4,20},{5,4},{6,22},{7,6},{8,24},{9,8},{... | collective-permute-start | bytes 1572872 | tf_op jit(solution)/shard_map/ppermute | solution.py:257
  71.8 25.1 %collective-permute-start.14 = (bf16[1024,256]{1,0:T(8,128)(2,1)S(1)}, bf16[1024,256]{1,0:T(8,128)(2,1)S(1)}, u32[]{:S(2)}, u32[]{:S(2)}) collective-permute-start(bf16[1024,256]{1,0:T(8,128)(2,1)S(1)} %pad_maximum_fusion), channel_id=1, source_target_pairs={{0,17},{1,16},{2,19},{3,18},{4,21},{5,20},{6,23},{7,22},{8,25},{9,... | collective-permute-start | bytes 1572872 | tf_op jit(solution)/shard_map/ppermute | solution.py:257
  76.1 22.0 %collective-permute-start.16 = (bf16[256,512]{1,0:T(8,128)(2,1)S(1)}, bf16[256,512]{1,0:T(8,128)(2,1)S(1)}, u32[]{:S(2)}, u32[]{:S(2)}) collective-permute-start(bf16[256,512]{1,0:T(8,128)(2,1)S(1)} %add_convert_fusion.1.mine), channel_id=1, source_target_pairs={{0,1},{1,0},{2,3},{3,2},{4,5},{5,4},{6,7},{7,6},{8,9},{9,8},{10,11... | collective-permute-start | bytes 786440 | tf_op jit(solution)/shard_map/ppermute | solution.py:257
  78.7 64.5 %collective-permute-start.9 = (bf16[128,2048]{1,0:T(8,128)(2,1)}, bf16[128,2048]{1,0:T(8,128)(2,1)S(1)}, u32[]{:S(2)}, u32[]{:S(2)}) collective-permute-start(bf16[128,2048]{1,0:T(8,128)(2,1)} %get-tuple-element.26), channel_id=1, source_target_pairs={{0,16},{1,17},{2,18},{3,19},{4,20},{5,21},{6,22},{7,23},{8,24},{9,... | collective-permute-start | bytes 1572872 | tf_op jit(solution)/shard_map/ppermute | solution.py:257
  99.3 4.2 %collective-permute-start.17 = (bf16[128,512]{1,0:T(8,128)(2,1)S(1)}, bf16[128,512]{1,0:T(8,128)(2,1)S(1)}, u32[]{:S(2)}, u32[]{:S(2)}) collective-permute-start(bf16[128,512]{1,0:T(8,128)(2,1)S(1)} %get-tuple-element.18), channel_id=1, source_target_pairs={{0,0},{1,16},{2,2},{3,18},{4,4},{5,20},{6,6},{7,22},{8,1},{9,17},{... | collective-permute-start | bytes 393224 | tf_op jit(solution)/shard_map/ppermute | solution.py:257
  100.0 7.9 %collective-permute-start.18 = (bf16[128,512]{1,0:T(8,128)(2,1)S(1)}, bf16[128,512]{1,0:T(8,128)(2,1)S(1)}, u32[]{:S(2)}, u32[]{:S(2)}) collective-permute-start(bf16[128,512]{1,0:T(8,128)(2,1)S(1)} %get-tuple-element.19), channel_id=1, source_target_pairs={{0,2},{1,18},{2,0},{3,16},{4,6},{5,22},{6,4},{7,20},{8,3},{9,19},{... | collective-permute-start | bytes 393224 | tf_op jit(solution)/shard_map/ppermute | solution.py:257
  101.6 17.1 %collective-permute-start.19 = (bf16[128,512]{1,0:T(8,128)(2,1)S(1)}, bf16[128,512]{1,0:T(8,128)(2,1)S(1)}, u32[]{:S(2)}, u32[]{:S(2)}) collective-permute-start(bf16[128,512]{1,0:T(8,128)(2,1)S(1)} %get-tuple-element.20), channel_id=1, source_target_pairs={{0,4},{1,20},{2,6},{3,22},{4,0},{5,16},{6,2},{7,18},{8,5},{9,21},{... | collective-permute-start | bytes 393224 | tf_op jit(solution)/shard_map/ppermute | solution.py:257
  102.4 22.4 %collective-permute-start.20 = (bf16[128,512]{1,0:T(8,128)(2,1)S(1)}, bf16[128,512]{1,0:T(8,128)(2,1)S(1)}, u32[]{:S(2)}, u32[]{:S(2)}) collective-permute-start(bf16[128,512]{1,0:T(8,128)(2,1)S(1)} %get-tuple-element.21), channel_id=1, source_target_pairs={{0,6},{1,22},{2,4},{3,20},{4,2},{5,18},{6,0},{7,16},{8,7},{9,23},{... | collective-permute-start | bytes 393224 | tf_op jit(solution)/shard_map/ppermute | solution.py:257
  103.6 21.5 %collective-permute-start.21 = (bf16[128,512]{1,0:T(8,128)(2,1)S(1)}, bf16[128,512]{1,0:T(8,128)(2,1)S(1)}, u32[]{:S(2)}, u32[]{:S(2)}) collective-permute-start(bf16[128,512]{1,0:T(8,128)(2,1)S(1)} %get-tuple-element.22), channel_id=1, source_target_pairs={{0,8},{1,24},{2,10},{3,26},{4,12},{5,28},{6,14},{7,30},{8,9},{9,25... | collective-permute-start | bytes 393224 | tf_op jit(solution)/shard_map/ppermute | solution.py:257
  107.9 17.2 %collective-permute-start.22 = (bf16[128,512]{1,0:T(8,128)(2,1)S(1)}, bf16[128,512]{1,0:T(8,128)(2,1)S(1)}, u32[]{:S(2)}, u32[]{:S(2)}) collective-permute-start(bf16[128,512]{1,0:T(8,128)(2,1)S(1)} %get-tuple-element.23), channel_id=1, source_target_pairs={{0,10},{1,26},{2,8},{3,24},{4,14},{5,30},{6,12},{7,28},{8,11},{9,2... | collective-permute-start | bytes 393224 | tf_op jit(solution)/shard_map/ppermute | solution.py:257
  118.7 17.5 %collective-permute-start.23 = (bf16[128,512]{1,0:T(8,128)(2,1)S(1)}, bf16[128,512]{1,0:T(8,128)(2,1)S(1)}, u32[]{:S(2)}, u32[]{:S(2)}) collective-permute-start(bf16[128,512]{1,0:T(8,128)(2,1)S(1)} %get-tuple-element.24), channel_id=1, source_target_pairs={{0,12},{1,28},{2,14},{3,30},{4,8},{5,24},{6,10},{7,26},{8,13},{9,2... | collective-permute-start | bytes 393224 | tf_op jit(solution)/shard_map/ppermute | solution.py:257
  124.8 16.7 %collective-permute-start.24 = (bf16[128,512]{1,0:T(8,128)(2,1)S(1)}, bf16[128,512]{1,0:T(8,128)(2,1)S(1)}, u32[]{:S(2)}, u32[]{:S(2)}) collective-permute-start(bf16[128,512]{1,0:T(8,128)(2,1)S(1)} %get-tuple-element.25), channel_id=1, source_target_pairs={{0,14},{1,30},{2,12},{3,28},{4,10},{5,26},{6,8},{7,24},{8,15},{9,3... | collective-permute-start | bytes 393224 | tf_op jit(solution)/shard_map/ppermute | solution.py:257

commit v2 on v0

v2 whole, which is shorter than its diff:
```python
import functools

import jax
import jax.numpy as jnp
from jax import lax
from jax.experimental import pallas as pl
from jax.experimental.pallas import tpu as pltpu
from jax.sharding import PartitionSpec as P

AXES = ("grp", "anim", "mark")
VMEM_LIMIT = 16 * 1024 * 1024
PARTS = 2
SHORT = pl.CostEstimate(flops=0, bytes_accessed=0, transcendentals=0)


def whole():
    return pl.BlockSpec(memory_space=pltpu.VMEM)


def anywhere():
    return pl.BlockSpec(memory_space=pl.ANY)


def in_hbm(array):
    return pltpu.with_memory_space_constraint(array, pltpu.HBM)


def params(**more):
    return pltpu.CompilerParams(vmem_limit_bytes=VMEM_LIMIT, **more)


def shape(dims, dtype=jnp.bfloat16):
    return jax.ShapeDtypeStruct(dims, dtype)


def expected_dot(left, right):
    return lax.dot_general(
        left, right, (((0,), (0,)), ((), ())), precision=lax.Precision.HIGHEST,
        preferred_element_type=jnp.float32,
    )


def matmul(left, right):
    return jnp.dot(left, right, preferred_element_type=jnp.float32)


def centre_value(genotypes, breed_codes, breed_freqs):
    fractions = breed_codes.astype(jnp.float32) / 32.0
    expected = expected_dot(fractions, breed_freqs)
    return (genotypes.astype(jnp.float32) - 2.0 * expected).astype(jnp.bfloat16)


def gather_body(noncore_geno, noncore_codes, core_geno, core_codes, breed_freqs, core_inverse, *, n_mark):
    slab = breed_freqs.shape[1] * n_mark
    noncore_z = centre_value(noncore_geno, noncore_codes, breed_freqs)
    core_z = centre_value(core_geno, core_codes, breed_freqs)
    shard_rows = lax.all_gather(core_z, "anim", axis=0, tiled=True)
    related = (
        lax.dot_general(
            noncore_z, shard_rows, (((1,), (1,)), ((), ())), preferred_element_type=jnp.float32
        )
        / slab
    )
    loading = lax.dot_general(
        shard_rows, core_inverse, (((0,), (0,)), ((), ())), preferred_element_type=jnp.float32
    ).astype(jnp.bfloat16)
    scores = matmul(noncore_z, lax.all_gather(loading, "anim", axis=1, tiled=True)) / slab
    return tuple(
        lax.psum_scatter(part.astype(jnp.bfloat16), "mark", scatter_dimension=1, tiled=True)
        for part in (related, scores)
    )


def centre_kernel(
    place, geno, codes, freqs, noncore_geno, noncore_codes, piece, noncore, *scratch
):
    rows, markers = geno.shape[0] // 2, geno.shape[1]
    mine = pl.ds(pl.multiple_of(place[0] * rows, rows), rows)
    here, sem = scratch[:-1], scratch[-1]
    sources = [codes, freqs, noncore_codes, noncore_geno, geno.at[mine, :]]
    copies = [
        pltpu.make_async_copy(source, target, sem.at[i])
        for i, (source, target) in enumerate(zip(sources, here))
    ]
    for copy in copies:
        copy.start()
    for copy in copies[:3]:
        copy.wait()
    codes, freqs, noncore_codes, noncore_geno, geno = here
    expected = expected_dot(freqs[...], codes[:, mine].astype(jnp.float32) / 32.0)
    noncore_expected = expected_dot(noncore_codes[...].astype(jnp.float32) / 32.0, freqs[...])
    copies[3].wait()
    centred = (noncore_geno[...].astype(jnp.float32) - 2.0 * noncore_expected).astype(jnp.bfloat16)
    noncore[...] = centred
    height = piece.shape[0] - markers
    for i in range(rows // markers):
        piece[markers:, i * markers:(i + 1) * markers] = centred[i * height:(i + 1) * height, :]
    copies[4].wait()
    dosage = geno[...].astype(jnp.float32).T
    piece[:markers, :] = (dosage - 2.0 * expected).astype(jnp.bfloat16)


def centre(part, core_geno, core_codes, breed_freqs, noncore_geno, noncore_codes):
    rows, markers = core_geno.shape[0] // 2, core_geno.shape[1]
    noncore = noncore_geno.shape[0]
    operands = [core_geno, core_codes, breed_freqs, noncore_geno, noncore_codes]
    return pl.pallas_call(
        centre_kernel,
        in_specs=[pl.BlockSpec(memory_space=pltpu.SMEM)] + [anywhere()] * 5,
        out_specs=[whole()] * 2,
        out_shape=[shape((markers + noncore * markers // rows, rows)), shape((noncore, markers))],
        scratch_shapes=[
            pltpu.VMEM(core_codes.shape, jnp.int32),
            pltpu.VMEM(breed_freqs.shape, jnp.float32),
            pltpu.VMEM(noncore_codes.shape, jnp.int32),
            pltpu.VMEM(noncore_geno.shape, jnp.int32),
            pltpu.VMEM((rows, markers), jnp.int32),
            pltpu.SemaphoreType.DMA((5,)),
        ],
        compiler_params=params(),
        cost_estimate=SHORT,
        name="centre",
    )(part[None], *[in_hbm(operand) for operand in operands])


def unfold_kernel(count, flag, *refs):
    markers = refs[-1].shape[1]
    pieces, outs = refs[:-2], refs[-2:]
    height = pieces[0].shape[0] - markers
    folds = pieces[0].shape[1] // markers
    for b in range(count):
        for i in range(folds):
            spot = slice((b * folds + i) * height, (b * folds + i + 1) * height)
            for j in range(2):
                @pl.when(flag[0] == j)
                def _(b=b, i=i, j=j, spot=spot):
                    for k in range(2):
                        piece = pieces[b + count * (j ^ k)]
                        outs[k][spot, :] = piece[markers:, i * markers:(i + 1) * markers]


def unfold(pieces, noncore_shape, flag):
    rows, markers = noncore_shape
    count = len(pieces) // 2
    return pl.pallas_call(
        functools.partial(unfold_kernel, count),
        in_specs=[pl.BlockSpec(memory_space=pltpu.SMEM)] + [whole()] * len(pieces),
        out_specs=[whole()] * 2,
        out_shape=[shape((rows * count, markers))] * 2,
        compiler_params=params(),
        cost_estimate=SHORT,
        name="unfold",
    )(flag.astype(jnp.int32)[None], *pieces)


def absorb_kernel(count, pairs, ahead, first, scale, place, *refs):
    refs = list(refs)
    pieces = [refs.pop(0) for _ in range(count)]
    inverse = refs.pop(0)
    related = [(refs.pop(0), refs.pop(0)) for _ in range(pairs)]
    noncore = refs.pop(0) if pairs else None
    before = None if first else refs.pop(0)
    fetched = inverse.ndim == 3
    slabs, sem = (inverse, None) if fetched else refs[-2:]
    outs = refs if fetched else refs[:-2]
    later = outs.pop() if ahead else None
    own, send = (outs.pop(-2), outs.pop(-1)) if pairs else (None, None)
    rows, columns = pieces[0].shape[1], inverse.shape[-1]

    copies = []
    for i in range(0 if fetched else count + ahead):
        block = pl.ds(pl.multiple_of(place[i] * rows, rows), rows)
        target = slabs.at[i] if i < count else later.at[i - count]
        copies.append(pltpu.make_async_copy(inverse.at[block, :], target, sem.at[i]))
        copies[-1].start()
    for i, pair in enumerate(related):
        values = [
            (matmul(noncore[...], p[:noncore.shape[1], :]) * scale).astype(jnp.bfloat16)
            for p in pair
        ]
        for j in range(2):
            @pl.when(place[count + ahead] == j)
            def _(i=i, j=j, values=values):
                own[:, i * rows:(i + 1) * rows] = values[j]
                send[:, i * rows:(i + 1) * rows] = values[1 - j]

    for copy in copies[:count]:
        copy.wait()
    for start in range(0, columns, 256):
        part = slice(start, start + 256)
        total = None if first else before[:, part]
        for i in range(count):
            product = matmul(pieces[i][:outs[0].shape[0], :], slabs[i, :, part])
            total = product if total is None else total + product
        outs[0][:, part] = total
        for i, out in enumerate(outs[1:]):
            width = out.shape[1]
            if i * width <= start < (i + 1) * width:
                out[:, start - i * width:start - i * width + 256] = total.astype(out.dtype)
    for copy in copies[count:]:
        copy.wait()


def absorb(pieces, blocks, inverse, before, noncore, pairs, flag, scale, parts=0):
    count, rows, columns, markers = len(pieces), pieces[0].shape[1], inverse.shape[-1], noncore.shape[1]
    ahead, fetched = len(blocks) - count, inverse.ndim == 3
    operands = [*pieces, inverse] + [piece for pair in pairs for piece in pair]
    operands += [noncore] if pairs else []
    operands += [] if before is None else [before]
    outs = [shape((markers, columns), jnp.float32)]
    outs += [shape((markers, columns // parts)) for _ in range(parts)]
    outs += [shape((noncore.shape[0], rows * len(pairs)))] * 2 if pairs else []
    outs += [shape((ahead, rows, columns))] if ahead else []
    specs = [whole()] * len(operands)
    specs[count] = whole() if fetched else anywhere()
    return pl.pallas_call(
        functools.partial(absorb_kernel, count, len(pairs), ahead, before is None, scale),
        in_specs=[pl.BlockSpec(memory_space=pltpu.SMEM)] + specs,
        out_specs=[whole()] * len(outs),
        out_shape=outs,
        scratch_shapes=[] if fetched else [
            pltpu.VMEM((count, rows, columns), jnp.bfloat16),
            pltpu.SemaphoreType.DMA((count + ahead,)),
        ],
        compiler_params=params(),
        cost_estimate=SHORT,
        name="absorb",
    )(jnp.stack(blocks + [flag]).astype(jnp.int32), *operands)


def add_kernel(start, total, other, out):
    width = out.shape[1]
    out[...] = (total[:, start:start + width] + other[...].astype(jnp.float32)).astype(out.dtype)


def add_part(total, other, start):
    return pl.pallas_call(
        functools.partial(add_kernel, start),
        in_specs=[whole()] * 2,
        out_specs=whole(),
        out_shape=shape(other.shape),
        compiler_params=params(),
        cost_estimate=SHORT,
        name="add_part",
    )(total, other)


def relation_kernel(count, scale, flag, done, noncore, *refs):
    pieces, (own, send) = refs[:2 * count], refs[2 * count:]
    width = pieces[0].shape[1]
    for i in range(count):
        columns = slice(i * width, (i + 1) * width)
        values = [
            (matmul(noncore[...], pieces[2 * i + j][:noncore.shape[1], :]) * scale).astype(jnp.bfloat16)
            for j in range(2)
        ]
        for j in range(2):
            @pl.when(flag[0] == j)
            def _(j=j):
                own[:, columns] = values[j]
                send[:, columns] = values[1 - j]


def relate(noncore, pairs, flag, scale, after):
    rows, width = noncore.shape[0], pairs[0][0].shape[1]
    out = shape((rows, width * len(pairs)))
    return pl.pallas_call(
        functools.partial(relation_kernel, len(pairs), scale),
        in_specs=[pl.BlockSpec(memory_space=pltpu.SMEM), anywhere()]
        + [whole()] * (2 * len(pairs) + 1),
        out_specs=(whole(), whole()),
        out_shape=(out, out),
        compiler_params=params(),
        cost_estimate=SHORT,
        name="relate",
    )(flag.astype(jnp.int32)[None], after, noncore, *[piece for pair in pairs for piece in pair])


def regression_kernel(count, scale, kept, got, mine, other, *outs):
    rows = outs[0].shape[0]
    for k in range(count):
        block = slice(k * rows, (k + 1) * rows)
        value = matmul(kept[block, :], mine[...]) + matmul(got[block, :], other[...])
        outs[k][...] = (value * scale).astype(jnp.bfloat16)


def regress(kept, got, mine, other, count, scale):
    rows, width = kept.shape[0] // count, mine.shape[1]
    return pl.pallas_call(
        functools.partial(regression_kernel, count, scale),
        in_specs=[whole()] * 4,
        out_specs=[whole()] * count,
        out_shape=[shape((rows, width))] * count,
        compiler_params=params(),
        cost_estimate=SHORT,
        name="regress",
    )(kept, got, mine, other)


def assemble_kernel(jobs, place, *refs):
    refs, sem = list(refs[:-1]), refs[-1]
    outs = refs[-len(jobs):]
    copies = []
    for (count, width), out in zip(jobs, outs):
        for _ in range(count):
            part = refs.pop(0)
            for start in range(0, part.shape[1], width):
                slot = len(copies)
                columns = pl.ds(pl.multiple_of(place[slot] * width, width), width)
                copies.append(
                    pltpu.make_async_copy(
                        part.at[:, start:start + width], out.at[:, columns], sem.at[slot]
                    )
                )
                copies[-1].start()
    for copy in copies:
        copy.wait()


def assemble(jobs):
    parts = [part for job in jobs for part in job[0]]
    slots = [slot for job in jobs for slot in job[1]]
    return pl.pallas_call(
        functools.partial(assemble_kernel, [(len(job[0]), job[2]) for job in jobs]),
        in_specs=[pl.BlockSpec(memory_space=pltpu.SMEM)] + [anywhere()] * len(parts),
        out_specs=[anywhere()] * len(jobs),
        out_shape=[shape((job[0][0].shape[0], job[2] * len(job[1]))) for job in jobs],
        scratch_shapes=[pltpu.SemaphoreType.DMA((len(slots),))],
        compiler_params=params(),
        cost_estimate=SHORT,
        name="assemble",
    )(jnp.stack(slots).astype(jnp.int32), *parts)


def permute_body(
    noncore_geno, noncore_codes, core_geno, core_codes, breed_freqs, core_inverse, *, n_anim, n_mark
):
    markers = breed_freqs.shape[1]
    scale = 1.0 / (markers * n_mark)
    top = n_anim // 2
    grp, anim, mark = (lax.axis_index(name) for name in AXES)

    def move(array, target):
        pairs = []
        for g in range(2):
            for a in range(n_anim):
                for m in range(2):
                    tg, ta, tm = target(g, a, m)
                    pairs.append(((g * n_anim + a) * 2 + m, (tg * n_anim + ta) * 2 + tm))
        return lax.ppermute(array, AXES, pairs)

    def along_anim(array, bits):
        return move(array, lambda g, a, m: (g, a ^ bits, m))

    def across_grp(array):
        return move(array, lambda g, a, m: (1 - g, a, m))

    def across_mark(array):
        return move(array, lambda g, a, m: (g, a, 1 - m))

    own, noncore = centre(
        grp, core_geno, core_codes, breed_freqs, noncore_geno, noncore_codes
    )
    rows = noncore.shape[0]
    both = jnp.concatenate([noncore, across_grp(noncore)], axis=0)
    at_home = mark == anim // top
    flag = jnp.where(at_home, 0, 1)
    inverse = in_hbm(core_inverse)
    pieces, related = {0: own}, []

    def take(chosen, total, pairs=(), ahead=(), parts=0, rows_of=inverse):
        result = absorb(
            [pieces[b] for b in chosen], [(anim ^ b) * 2 + grp for b in [*chosen, *ahead]], rows_of,
            total, both, [(pieces[b], pieces[b + top]) for b in pairs], flag, scale, parts,
        )
        if pairs:
            related.extend(result[1 + parts:3 + parts])
        return [result[0], *result[1:1 + parts]] + list(result[3 + parts if pairs else 1 + parts:])

    low = list(range(2, top, 2))
    for bits in low + [top, 1]:
        pieces[bits] = along_anim(own, bits)
    for bits in low:
        pieces[bits + 1] = along_anim(pieces[bits], 1)
    held = [top, 1] + [b + 1 for b in low]
    for b, piece in zip(held, lax.optimization_barrier([pieces[b] for b in held])):
        pieces[b] = piece
    for bits in low:
        pieces[top + bits] = along_anim(pieces[top], bits)
    for bits in [0] + low:
        pieces[top + bits + 1] = along_anim(pieces[top + bits], 1)
    (total,) = take([0, 1] + low, None)
    last = [top + bits + i for bits in low for i in range(2)]
    total, slabs = take([b + 1 for b in low] + [top, top + 1], total, [0, 1], last)
    total, *send = take(last, total, parts=PARTS, rows_of=slabs)

    kept, got = unfold([pieces[b] for b in range(n_anim)], noncore.shape, flag)
    got = across_mark(got)
    from_other = [across_grp(part) for part in send]

    arrived, slots = [], []
    for i, part in enumerate(from_other):
        width = part.shape[1]
        mine = add_part(total, part, i * width)
        other = across_mark(mine)
        if i + 1 < PARTS:
            other, from_other[i + 1] = lax.optimization_barrier((other, from_other[i + 1]))
        results = regress(kept, got, mine, other, top, scale)
        if i == 0:
            begun = results[0]
        for k in range(top):
            arrived.append(
                move(results[k], lambda g, a, m, k=k: (g, m * top + (a % top ^ k), a // top))
            )
            slots.append((anim ^ k) % top * PARTS + i)

    related += relate(both, [(pieces[b - top], pieces[b]) for b in last], flag, scale, begun)
    received = [across_mark(part) for part in related[1::2]]
    sums = [
        jnp.concatenate(
            [
                (mine[part].astype(jnp.float32) + yours[part].astype(jnp.float32)).astype(
                    jnp.bfloat16
                )
                for mine, yours in zip(related[::2], received)
            ],
            axis=1,
        )
        for part in (slice(0, rows), slice(rows, 2 * rows))
    ]
    swapped = across_grp(sums[1])

    width_of_piece = own.shape[1]
    order = [0, 1] + [b - top for b in last]
    places = [2 * ((anim ^ b) % top) + g for g in (grp, 1 - grp) for b in order]
    return tuple(
        assemble([([sums[0], swapped], places, width_of_piece), (arrived, slots, width)])
    )


def solution(mesh):
    in_specs = (
        P(("grp", "anim"), "mark"),
        P(None, ("grp", "anim")),
        P("anim", "mark"),
        P(None, "anim"),
        P(None, "mark"),
        P(None, "anim"),
    )
    out_specs = (P(("grp", "anim"), "mark"), P(("grp", "anim"), "mark"))
    n_grp, n_anim, n_mark = (mesh.shape[name] for name in AXES)
    if n_grp == 2 and n_mark == 2 and n_anim in (8, 16):
        body = functools.partial(permute_body, n_anim=n_anim, n_mark=n_mark)
    else:
        body = functools.partial(gather_body, n_mark=n_mark)
    return jax.shard_map(body, mesh=mesh, in_specs=in_specs, out_specs=out_specs, check_vma=False)
```

time: 203 us -> 90.6 us (0.45)
  the two profiles are of different devices: /device:TPU:0 before, /device:TPU:9 now
where the time goes in v2:
time: 90.6 us; the launch traced here: 90.4 us
  starting transfers between devices  38.4 us (42%)
  waiting for transfers between devices  35.8 us (40%)
  Pallas kernels  13.7 us (15%)
  other arithmetic  1.39 us (2%)
    ppermute x24, starting transfers between devices, move(): return lax.ppermute(array, AXES, pairs)  38.4 us
    ppermute x24, waiting for transfers between devices, move(): return lax.ppermute(array, AXES, pairs)  35.8 us
    pallas_call x3, Pallas kernels, absorb(): pl.pallas_call(functools.partial(absorb_kernel, count, len(pairs), ahead,...  8.15 us
    pallas_call x1, Pallas kernels, assemble(): pl.pallas_call(functools.partial(assemble_kernel, [(len(job[0]), job[2])...  1.98 us
  transfers between devices with their start and end apart: 24, of which 13 were waited for; matrix products, arithmetic and copies ran while one was open for 2% of the time, Pallas kernels for 10%

profile of v2, /device:TPU:9, one launch (start us, length us, event | category | flops | bytes accessed | tf_op | source)
XLA Modules:
  0.0 90.4 jit_solution(777852789784045094)
XLA Ops:
  0.6 1.8 %centre.1 = (bf16[320,512]{1,0:T(8,128)(2,1)S(1)}, bf16[128,256]{1,0:T(8,128)(2,1)S(1)}) custom-call(s32[1]{0:T(128)} %bitcast.22.place, s32[1024,256]{1,0:T(8,128)} %geno.1, s32[5,1024]{1,0:T(8,128)} %codes.1, f32[5,256]{1,0:T(8,128)} %freqs.1, s32[128,256]{1,0:T(8,128)} %noncore_geno.1, s32[5,128]{1,0:T(8,128)} %noncore_codes.1), custom_call_target="tpu_custom_call" | custom-call | tf_op jit(solution)/shard_map/centre/pallas_call | solution.py:107
  2.5 1.4 %collective-permute-start.1 = (bf16[320,512]{1,0:T(8,128)(2,1)S(1)}, bf16[320,512]{1,0:T(8,128)(2,1)S(1)}, u32[]{:S(2)}, u32[]{:S(2)}) collective-permute-start(bf16[320,512]{1,0:T(8,128)(2,1)S(1)} %get-tuple-element.28.refs_0_.refs_4_), channel_id=1, source_target_pairs={{0,2},{1,3},{2,0},{3,1},{4,6},{5,7},{6,4},{7,5},{8,10},{9,11},{10,... | collective-permute-start | bytes 983048 | tf_op jit(solution)/shard_map/ppermute | solution.py:350
  3.8 2.3 %collective-permute-start = (bf16[320,512]{1,0:T(8,128)(2,1)S(1)}, bf16[320,512]{1,0:T(8,128)(2,1)S(1)}, u32[]{:S(2)}, u32[]{:S(2)}) collective-permute-start(bf16[320,512]{1,0:T(8,128)(2,1)S(1)} %get-tuple-element.28.refs_0_.refs_4_), channel_id=1, source_target_pairs={{0,8},{1,9},{2,10},{3,11},{4,12},{5,13},{6,14},{7,15},{8,0},{9,1},... | collective-permute-start | bytes 983048 | tf_op jit(solution)/shard_map/ppermute | solution.py:350
  6.2 8.7 %collective-permute-done.2.refs_2_.refs_0_ = bf16[320,512]{1,0:T(8,128)(2,1)S(1)} collective-permute-done((bf16[320,512]{1,0:T(8,128)(2,1)S(1)}, bf16[320,512]{1,0:T(8,128)(2,1)S(1)}, u32[]{:S(2)}, u32[]{:S(2)}) %collective-permute-start.2) | collective-permute-done | bytes 327712 | tf_op jit(solution)/shard_map/ppermute | solution.py:350
  14.9 2.0 %collective-permute-start.3 = (bf16[320,512]{1,0:T(8,128)(2,1)S(1)}, bf16[320,512]{1,0:T(8,128)(2,1)S(1)}, u32[]{:S(2)}, u32[]{:S(2)}) collective-permute-start(bf16[320,512]{1,0:T(8,128)(2,1)S(1)} %collective-permute-done.2.refs_2_.refs_0_), channel_id=1, source_target_pairs={{0,2},{1,3},{2,0},{3,1},{4,6},{5,7},{6,4},{7,5},{8,10},{9,11},{10,... | collective-permute-start | bytes 983048 | tf_op jit(solution)/shard_map/ppermute | solution.py:350
  16.9 2.2 %collective-permute-done.refs_1_.refs_5_.refs_4_ = bf16[320,512]{1,0:T(8,128)(2,1)S(1)} collective-permute-done((bf16[320,512]{1,0:T(8,128)(2,1)S(1)}, bf16[320,512]{1,0:T(8,128)(2,1)S(1)}, u32[]{:S(2)}, u32[]{:S(2)}) %collective-permute-start) | collective-permute-done | bytes 327712 | tf_op jit(solution)/shard_map/ppermute | solution.py:350
  19.1 4.2 %collective-permute-done.3.refs_0_.refs_3_.refs_2_ = bf16[320,512]{1,0:T(8,128)(2,1)S(1)} collective-permute-done((bf16[320,512]{1,0:T(8,128)(2,1)S(1)}, bf16[320,512]{1,0:T(8,128)(2,1)S(1)}, u32[]{:S(2)}, u32[]{:S(2)}) %collective-permute-start.3) | collective-permute-done | bytes 327712 | tf_op jit(solution)/shard_map/ppermute | solution.py:350
  23.3 2.2 %collective-permute-start.7 = (bf16[320,512]{1,0:T(8,128)(2,1)S(1)}, bf16[320,512]{1,0:T(8,128)(2,1)S(1)}, u32[]{:S(2)}, u32[]{:S(2)}) collective-permute-start(bf16[320,512]{1,0:T(8,128)(2,1)S(1)} %collective-permute-done.refs_1_.refs_5_.refs_4_), channel_id=1, source_target_pairs={{0,4},{1,5},{2,6},{3,7},{4,0},{5,1},{6,2},{7,3},{8,12},{9,13},{10,... | collective-permute-start | bytes 983048 | tf_op jit(solution)/shard_map/ppermute | solution.py:350
  25.5 1.2 %collective-permute-start.5 = (bf16[128,256]{1,0:T(8,128)(2,1)S(1)}, bf16[128,256]{1,0:T(8,128)(2,1)S(1)}, u32[]{:S(2)}, u32[]{:S(2)}) collective-permute-start(bf16[128,256]{1,0:T(8,128)(2,1)S(1)} %get-tuple-element.32), channel_id=1, source_target_pairs={{0,16},{1,17},{2,18},{3,19},{4,20},{5,21},{6,22},{7,23},{8,24},{9,... | collective-permute-start | bytes 196616 | tf_op jit(solution)/shard_map/ppermute | solution.py:350
  26.9 1.2 %collective-permute-start.4 = (bf16[320,512]{1,0:T(8,128)(2,1)S(1)}, bf16[320,512]{1,0:T(8,128)(2,1)S(1)}, u32[]{:S(2)}, u32[]{:S(2)}) collective-permute-start(bf16[320,512]{1,0:T(8,128)(2,1)S(1)} %collective-permute-done.refs_1_.refs_5_.refs_4_), channel_id=1, source_target_pairs={{0,2},{1,3},{2,0},{3,1},{4,6},{5,7},{6,4},{7,5},{8,10},{9,11},{10,... | collective-permute-start | bytes 983048 | tf_op jit(solution)/shard_map/ppermute | solution.py:350
  28.1 3.2 %collective-permute-done.7.refs_6_.refs_0_.refs_1_ = bf16[320,512]{1,0:T(8,128)(2,1)S(1)} collective-permute-done((bf16[320,512]{1,0:T(8,128)(2,1)S(1)}, bf16[320,512]{1,0:T(8,128)(2,1)S(1)}, u32[]{:S(2)}, u32[]{:S(2)}) %collective-permute-start.7) | collective-permute-done | bytes 327712 | tf_op jit(solution)/shard_map/ppermute | solution.py:350
  31.4 0.9 collective-permute-start.8
  32.4 3.4 %absorb.3.refs_9_ = f32[256,1024]{1,0:T(8,128)S(1)} custom-call(s32[4]{0:T(128)S(1)} %pad_add_fusion.place, bf16[320,512]{1,0:T(8,128)(2,1)S(1)} %get-tuple-element.28.refs_0_.refs_4_, bf16[320,512]{1,0:T(8,128)(2,1)S(1)} %collective-permute-done.1.refs_1_.refs_6_, bf16[320,512]{1,0:T(8,128)(2,1)S(1)} %collective-permute-done.2.refs_2_.refs_0_, ...), custom_call_target="tpu_custom_call" | custom-call | tf_op jit(solution)/shard_map/absorb/pallas_call | solution.py:216
  35.9 3.5 %absorb.4 = (f32[256,1024]{1,0:T(8,128)S(1)}, bf16[256,1024]{1,0:T(8,128)(2,1)S(1)}, bf16[256,1024]{1,0:T(8,128)(2,1)S(1)}, bf16[2,512,1024]{2,1,0:T(8,128)(2,1)S(1)}) custom-call(s32[6]{0:T(128)S(1)} %stack.114.place, bf16[320,512]{1,0:T(8,128)(2,1)S(1)} %collective-permute-done.3.refs_0_.refs_3_.refs_2_, ...), custom_call_target="tpu_custom_call" | custom-call | tf_op jit(solution)/shard_map/absorb/pallas_call | solution.py:216
  39.4 1.8 %collective-permute-done.8.refs_7_.refs_1_.refs_3_ = bf16[320,512]{1,0:T(8,128)(2,1)S(1)} collective-permute-done((bf16[320,512]{1,0:T(8,128)(2,1)S(1)}, bf16[320,512]{1,0:T(8,128)(2,1)S(1)}, u32[]{:S(2)}, u32[]{:S(2)}) %collective-permute-start.8) | collective-permute-done | bytes 327712 | tf_op jit(solution)/shard_map/ppermute | solution.py:350
  41.1 1.3 %absorb.5 = (f32[256,1024]{1,0:T(8,128)S(1)}, bf16[256,512]{1,0:T(8,128)(2,1)S(1)}, bf16[256,512]{1,0:T(8,128)(2,1)S(1)}) custom-call(s32[3]{0:T(128)S(1)} %pad_add_fusion.1.place, bf16[320,512]{1,0:T(8,128)(2,1)S(1)} %collective-permute-done.7.refs_6_.refs_0_.refs_1_, bf16[320,512]{1,0:T(8,128)(2,1)S(1)} %collective-permute-done.8.refs_7_.refs_1_.refs_3_, ...), custom_call_target="tpu_custom_call" | custom-call | tf_op jit(solution)/shard_map/absorb/pallas_call | solution.py:216
  42.4 1.1 %collective-permute-start.10 = (bf16[256,512]{1,0:T(8,128)(2,1)S(1)}, bf16[256,512]{1,0:T(8,128)(2,1)S(1)}, u32[]{:S(2)}, u32[]{:S(2)}) collective-permute-start(bf16[256,512]{1,0:T(8,128)(2,1)S(1)} %get-tuple-element.40), channel_id=1, source_target_pairs={{0,16},{1,17},{2,18},{3,19},{4,20},{5,21},{6,22},{7,23},{8,24},{9,... | collective-permute-start | bytes 786440 | tf_op jit(solution)/shard_map/ppermute | solution.py:350
  44.0 3.8 %collective-permute-done.10.other = bf16[256,512]{1,0:T(8,128)(2,1)S(1)} collective-permute-done((bf16[256,512]{1,0:T(8,128)(2,1)S(1)}, bf16[256,512]{1,0:T(8,128)(2,1)S(1)}, u32[]{:S(2)}, u32[]{:S(2)}) %collective-permute-start.10) | collective-permute-done | bytes 262176 | tf_op jit(solution)/shard_map/ppermute | solution.py:350
  47.8 6.4 %collective-permute-start.11 = (bf16[256,512]{1,0:T(8,128)(2,1)S(1)}, bf16[256,512]{1,0:T(8,128)(2,1)S(1)}, u32[]{:S(2)}, u32[]{:S(2)}) collective-permute-start(bf16[256,512]{1,0:T(8,128)(2,1)S(1)} %add_part.2.mine), channel_id=1, source_target_pairs={{0,1},{1,0},{2,3},{3,2},{4,5},{5,4},{6,7},{7,6},{8,9},{9,8},{10,11... | collective-permute-start | bytes 786440 | tf_op jit(solution)/shard_map/ppermute | solution.py:350
  57.0 1.1 %collective-permute-start.13 = (bf16[256,1024]{1,0:T(8,128)(2,1)S(1)}, bf16[256,1024]{1,0:T(8,128)(2,1)S(1)}, u32[]{:S(2)}, u32[]{:S(2)}) collective-permute-start(bf16[256,1024]{1,0:T(8,128)(2,1)S(1)} %get-tuple-element.45), channel_id=1, source_target_pairs={{0,1},{1,0},{2,3},{3,2},{4,5},{5,4},{6,7},{7,6},{8,9},{9,8},{10,11... | collective-permute-start | bytes 1572872 | tf_op jit(solution)/shard_map/ppermute | solution.py:350
  58.4 1.2 %collective-permute-done.13 = bf16[256,1024]{1,0:T(8,128)(2,1)S(1)} collective-permute-done((bf16[256,1024]{1,0:T(8,128)(2,1)S(1)}, bf16[256,1024]{1,0:T(8,128)(2,1)S(1)}, u32[]{:S(2)}, u32[]{:S(2)}) %collective-permute-start.13) | collective-permute-done | bytes 524320 | tf_op jit(solution)/shard_map/ppermute | solution.py:350
  60.6 1.0 %collective-permute-start.14 = (bf16[128,2048]{1,0:T(8,128)(2,1)}, bf16[128,2048]{1,0:T(8,128)(2,1)S(1)}, u32[]{:S(2)}, u32[]{:S(2)}) collective-permute-start(bf16[128,2048]{1,0:T(8,128)(2,1)} %pad_maximum_fusion.1), channel_id=1, source_target_pairs={{0,16},{1,17},{2,18},{3,19},{4,20},{5,21},{6,22},{7,23},{8,24},{9,... | collective-permute-start | bytes 1572872 | tf_op jit(solution)/shard_map/ppermute | solution.py:350
  61.6 1.8 %collective-permute-start.16 = (bf16[128,512]{1,0:T(8,128)(2,1)S(1)}, bf16[128,512]{1,0:T(8,128)(2,1)S(1)}, u32[]{:S(2)}, u32[]{:S(2)}) collective-permute-start(bf16[128,512]{1,0:T(8,128)(2,1)S(1)} %get-tuple-element.46), channel_id=1, source_target_pairs={{0,2},{1,10},{2,0},{3,8},{4,6},{5,14},{6,4},{7,12},{8,3},{9,11},{1... | collective-permute-start | bytes 393224 | tf_op jit(solution)/shard_map/ppermute | solution.py:350
  63.5 2.0 %collective-permute-start.18 = (bf16[128,512]{1,0:T(8,128)(2,1)S(1)}, bf16[128,512]{1,0:T(8,128)(2,1)S(1)}, u32[]{:S(2)}, u32[]{:S(2)}) collective-permute-start(bf16[128,512]{1,0:T(8,128)(2,1)S(1)} %get-tuple-element.48), channel_id=1, source_target_pairs={{0,6},{1,14},{2,4},{3,12},{4,2},{5,10},{6,0},{7,8},{8,7},{9,15},{1... | collective-permute-start | bytes 393224 | tf_op jit(solution)/shard_map/ppermute | solution.py:350
  65.5 5.1 %collective-permute-start.15 = (bf16[128,512]{1,0:T(8,128)(2,1)S(1)}, bf16[128,512]{1,0:T(8,128)(2,1)S(1)}, u32[]{:S(2)}, u32[]{:S(2)}) collective-permute-start(bf16[128,512]{1,0:T(8,128)(2,1)S(1)} %get-tuple-element.43.done), channel_id=1, source_target_pairs={{0,0},{1,8},{2,2},{3,10},{4,4},{5,12},{6,6},{7,14},{8,1},{9,9},{10... | collective-permute-start | bytes 393224 | tf_op jit(solution)/shard_map/ppermute | solution.py:350
  71.3 1.9 %collective-permute-start.20 = (bf16[128,512]{1,0:T(8,128)(2,1)S(1)}, bf16[128,512]{1,0:T(8,128)(2,1)S(1)}, u32[]{:S(2)}, u32[]{:S(2)}) collective-permute-start(bf16[128,512]{1,0:T(8,128)(2,1)S(1)} %get-tuple-element.50), channel_id=1, source_target_pairs={{0,0},{1,8},{2,2},{3,10},{4,4},{5,12},{6,6},{7,14},{8,1},{9,9},{10... | collective-permute-start | bytes 393224 | tf_op jit(solution)/shard_map/ppermute | solution.py:350
  73.2 3.6 %collective-permute-start.21 = (bf16[128,512]{1,0:T(8,128)(2,1)S(1)}, bf16[128,512]{1,0:T(8,128)(2,1)S(1)}, u32[]{:S(2)}, u32[]{:S(2)}) collective-permute-start(bf16[128,512]{1,0:T(8,128)(2,1)S(1)} %get-tuple-element.51), channel_id=1, source_target_pairs={{0,2},{1,10},{2,0},{3,8},{4,6},{5,14},{6,4},{7,12},{8,3},{9,11},{1... | collective-permute-start | bytes 393224 | tf_op jit(solution)/shard_map/ppermute | solution.py:350
  76.8 1.8 %collective-permute-start.22 = (bf16[128,512]{1,0:T(8,128)(2,1)S(1)}, bf16[128,512]{1,0:T(8,128)(2,1)S(1)}, u32[]{:S(2)}, u32[]{:S(2)}) collective-permute-start(bf16[128,512]{1,0:T(8,128)(2,1)S(1)} %get-tuple-element.52), channel_id=1, source_target_pairs={{0,4},{1,12},{2,6},{3,14},{4,0},{5,8},{6,2},{7,10},{8,5},{9,13},{1... | collective-permute-start | bytes 393224 | tf_op jit(solution)/shard_map/ppermute | solution.py:350
  79.3 4.6 %collective-permute-done.21.refs_7_ = bf16[128,512]{1,0:T(8,128)(2,1)S(1)} collective-permute-done((bf16[128,512]{1,0:T(8,128)(2,1)S(1)}, bf16[128,512]{1,0:T(8,128)(2,1)S(1)}, u32[]{:S(2)}, u32[]{:S(2)}) %collective-permute-start.21) | collective-permute-done | bytes 131104 | tf_op jit(solution)/shard_map/ppermute | solution.py:350
  83.9 2.2 %collective-permute-done.22.refs_8_ = bf16[128,512]{1,0:T(8,128)(2,1)S(1)} collective-permute-done((bf16[128,512]{1,0:T(8,128)(2,1)S(1)}, bf16[128,512]{1,0:T(8,128)(2,1)S(1)}, u32[]{:S(2)}, u32[]{:S(2)}) %collective-permute-start.22) | collective-permute-done | bytes 131104 | tf_op jit(solution)/shard_map/ppermute | solution.py:350
  86.1 2.3 %collective-permute-done.23.refs_9_ = bf16[128,512]{1,0:T(8,128)(2,1)S(1)} collective-permute-done((bf16[128,512]{1,0:T(8,128)(2,1)S(1)}, bf16[128,512]{1,0:T(8,128)(2,1)S(1)}, u32[]{:S(2)}, u32[]{:S(2)}) %collective-permute-start.23) | collective-permute-done | bytes 131104 | tf_op jit(solution)/shard_map/ppermute | solution.py:350
  88.4 2.0 %assemble.1 = (bf16[128,4096]{1,0:T(8,128)(2,1)}, bf16[128,4096]{1,0:T(8,128)(2,1)}) custom-call(s32[16]{0:T(128)S(1)} %stack.107.place, bf16[128,2048]{1,0:T(8,128)(2,1)S(1)} %pad_maximum_fusion.refs_0_, bf16[128,2048]{1,0:T(8,128)(2,1)S(1)} %collective-permute-done.14.refs_1_, bf16[128,512]{1,0:T(8,128)(2,1)S(1)} %collective-permute-done.15.refs_2_, ...), custom_call_target="tpu_custom_call" | custom-call | tf_op jit(solution)/shard_map/assemble/pallas_call | solution.py:323
  (37 shorter events, 6.3 us)
Async XLA Ops:
  2.4 12.5 %collective-permute-start.2 = (bf16[320,512]{1,0:T(8,128)(2,1)S(1)}, bf16[320,512]{1,0:T(8,128)(2,1)S(1)}, u32[]{:S(2)}, u32[]{:S(2)}) collective-permute-start(bf16[320,512]{1,0:T(8,128)(2,1)S(1)} %get-tuple-element.28.refs_0_.refs_4_), channel_id=1, source_target_pairs={{0,4},{1,5},{2,6},{3,7},{4,0},{5,1},{6,2},{7,3},{8,12},{9,13},{10,... | collective-permute-start | bytes 983048 | tf_op jit(solution)/shard_map/ppermute | solution.py:350
  2.5 14.4 %collective-permute-start.1 = (bf16[320,512]{1,0:T(8,128)(2,1)S(1)}, bf16[320,512]{1,0:T(8,128)(2,1)S(1)}, u32[]{:S(2)}, u32[]{:S(2)}) collective-permute-start(bf16[320,512]{1,0:T(8,128)(2,1)S(1)} %get-tuple-element.28.refs_0_.refs_4_), channel_id=1, source_target_pairs={{0,2},{1,3},{2,0},{3,1},{4,6},{5,7},{6,4},{7,5},{8,10},{9,11},{10,... | collective-permute-start | bytes 983048 | tf_op jit(solution)/shard_map/ppermute | solution.py:350
  3.8 15.3 %collective-permute-start = (bf16[320,512]{1,0:T(8,128)(2,1)S(1)}, bf16[320,512]{1,0:T(8,128)(2,1)S(1)}, u32[]{:S(2)}, u32[]{:S(2)}) collective-permute-start(bf16[320,512]{1,0:T(8,128)(2,1)S(1)} %get-tuple-element.28.refs_0_.refs_4_), channel_id=1, source_target_pairs={{0,8},{1,9},{2,10},{3,11},{4,12},{5,13},{6,14},{7,15},{8,0},{9,1},... | collective-permute-start | bytes 983048 | tf_op jit(solution)/shard_map/ppermute | solution.py:350
  14.9 8.5 %collective-permute-start.3 = (bf16[320,512]{1,0:T(8,128)(2,1)S(1)}, bf16[320,512]{1,0:T(8,128)(2,1)S(1)}, u32[]{:S(2)}, u32[]{:S(2)}) collective-permute-start(bf16[320,512]{1,0:T(8,128)(2,1)S(1)} %collective-permute-done.2.refs_2_.refs_0_), channel_id=1, source_target_pairs={{0,2},{1,3},{2,0},{3,1},{4,6},{5,7},{6,4},{7,5},{8,10},{9,11},{10,... | collective-permute-start | bytes 983048 | tf_op jit(solution)/shard_map/ppermute | solution.py:350
  23.3 8.0 %collective-permute-start.7 = (bf16[320,512]{1,0:T(8,128)(2,1)S(1)}, bf16[320,512]{1,0:T(8,128)(2,1)S(1)}, u32[]{:S(2)}, u32[]{:S(2)}) collective-permute-start(bf16[320,512]{1,0:T(8,128)(2,1)S(1)} %collective-permute-done.refs_1_.refs_5_.refs_4_), channel_id=1, source_target_pairs={{0,4},{1,5},{2,6},{3,7},{4,0},{5,1},{6,2},{7,3},{8,12},{9,13},{10,... | collective-permute-start | bytes 983048 | tf_op jit(solution)/shard_map/ppermute | solution.py:350
  25.5 6.9 %collective-permute-start.5 = (bf16[128,256]{1,0:T(8,128)(2,1)S(1)}, bf16[128,256]{1,0:T(8,128)(2,1)S(1)}, u32[]{:S(2)}, u32[]{:S(2)}) collective-permute-start(bf16[128,256]{1,0:T(8,128)(2,1)S(1)} %get-tuple-element.32), channel_id=1, source_target_pairs={{0,16},{1,17},{2,18},{3,19},{4,20},{5,21},{6,22},{7,23},{8,24},{9,... | collective-permute-start | bytes 196616 | tf_op jit(solution)/shard_map/ppermute | solution.py:350
  26.9 9.0 %collective-permute-start.4 = (bf16[320,512]{1,0:T(8,128)(2,1)S(1)}, bf16[320,512]{1,0:T(8,128)(2,1)S(1)}, u32[]{:S(2)}, u32[]{:S(2)}) collective-permute-start(bf16[320,512]{1,0:T(8,128)(2,1)S(1)} %collective-permute-done.refs_1_.refs_5_.refs_4_), channel_id=1, source_target_pairs={{0,2},{1,3},{2,0},{3,1},{4,6},{5,7},{6,4},{7,5},{8,10},{9,11},{10,... | collective-permute-start | bytes 983048 | tf_op jit(solution)/shard_map/ppermute | solution.py:350
  31.4 9.8 %collective-permute-start.8 = (bf16[320,512]{1,0:T(8,128)(2,1)S(1)}, bf16[320,512]{1,0:T(8,128)(2,1)S(1)}, u32[]{:S(2)}, u32[]{:S(2)}) collective-permute-start(bf16[320,512]{1,0:T(8,128)(2,1)S(1)} %collective-permute-done.7.refs_6_.refs_0_.refs_1_), channel_id=1, source_target_pairs={{0,2},{1,3},{2,0},{3,1},{4,6},{5,7},{6,4},{7,5},{8,10},{9,11},{10,... | collective-permute-start | bytes 983048 | tf_op jit(solution)/shard_map/ppermute | solution.py:350
  42.4 5.3 %collective-permute-start.10 = (bf16[256,512]{1,0:T(8,128)(2,1)S(1)}, bf16[256,512]{1,0:T(8,128)(2,1)S(1)}, u32[]{:S(2)}, u32[]{:S(2)}) collective-permute-start(bf16[256,512]{1,0:T(8,128)(2,1)S(1)} %get-tuple-element.40), channel_id=1, source_target_pairs={{0,16},{1,17},{2,18},{3,19},{4,20},{5,21},{6,22},{7,23},{8,24},{9,... | collective-permute-start | bytes 786440 | tf_op jit(solution)/shard_map/ppermute | solution.py:350
  43.5 11.4 %collective-permute-start.12 = (bf16[256,512]{1,0:T(8,128)(2,1)S(1)}, bf16[256,512]{1,0:T(8,128)(2,1)S(1)}, u32[]{:S(2)}, u32[]{:S(2)}) collective-permute-start(bf16[256,512]{1,0:T(8,128)(2,1)S(1)} %get-tuple-element.41), channel_id=1, source_target_pairs={{0,16},{1,17},{2,18},{3,19},{4,20},{5,21},{6,22},{7,23},{8,24},{9,... | collective-permute-start | bytes 786440 | tf_op jit(solution)/shard_map/ppermute | solution.py:350
  47.8 7.5 %collective-permute-start.11 = (bf16[256,512]{1,0:T(8,128)(2,1)S(1)}, bf16[256,512]{1,0:T(8,128)(2,1)S(1)}, u32[]{:S(2)}, u32[]{:S(2)}) collective-permute-start(bf16[256,512]{1,0:T(8,128)(2,1)S(1)} %add_part.2.mine), channel_id=1, source_target_pairs={{0,1},{1,0},{2,3},{3,2},{4,5},{5,4},{6,7},{7,6},{8,9},{9,8},{10,11... | collective-permute-start | bytes 786440 | tf_op jit(solution)/shard_map/ppermute | solution.py:350
  54.3 1.6 %collective-permute-start.9 = (bf16[512,256]{1,0:T(8,128)(2,1)S(1)}, bf16[512,256]{1,0:T(8,128)(2,1)S(1)}, u32[]{:S(2)}, u32[]{:S(2)}) collective-permute-start(bf16[512,256]{1,0:T(8,128)(2,1)S(1)} %get-tuple-element.36), channel_id=1, source_target_pairs={{0,1},{1,0},{2,3},{3,2},{4,5},{5,4},{6,7},{7,6},{8,9},{9,8},{10,11... | collective-permute-start | bytes 786440 | tf_op jit(solution)/shard_map/ppermute | solution.py:350
  54.4 3.7 %collective-permute-start.6 = (bf16[256,1024]{1,0:T(8,128)(2,1)S(1)}, bf16[256,1024]{1,0:T(8,128)(2,1)S(1)}, u32[]{:S(2)}, u32[]{:S(2)}) collective-permute-start(bf16[256,1024]{1,0:T(8,128)(2,1)S(1)} %get-tuple-element.34), channel_id=1, source_target_pairs={{0,1},{1,0},{2,3},{3,2},{4,5},{5,4},{6,7},{7,6},{8,9},{9,8},{10,11... | collective-permute-start | bytes 1572872 | tf_op jit(solution)/shard_map/ppermute | solution.py:350
  57.0 2.6 %collective-permute-start.13 = (bf16[256,1024]{1,0:T(8,128)(2,1)S(1)}, bf16[256,1024]{1,0:T(8,128)(2,1)S(1)}, u32[]{:S(2)}, u32[]{:S(2)}) collective-permute-start(bf16[256,1024]{1,0:T(8,128)(2,1)S(1)} %get-tuple-element.45), channel_id=1, source_target_pairs={{0,1},{1,0},{2,3},{3,2},{4,5},{5,4},{6,7},{7,6},{8,9},{9,8},{10,11... | collective-permute-start | bytes 1572872 | tf_op jit(solution)/shard_map/ppermute | solution.py:350
  58.3 7.2 %collective-permute-start.19 = (bf16[256,512]{1,0:T(8,128)(2,1)S(1)}, bf16[256,512]{1,0:T(8,128)(2,1)S(1)}, u32[]{:S(2)}, u32[]{:S(2)}) collective-permute-start(bf16[256,512]{1,0:T(8,128)(2,1)S(1)} %add_part.3.mine), channel_id=1, source_target_pairs={{0,1},{1,0},{2,3},{3,2},{4,5},{5,4},{6,7},{7,6},{8,9},{9,8},{10,11... | collective-permute-start | bytes 786440 | tf_op jit(solution)/shard_map/ppermute | solution.py:350
  60.6 27.8 %collective-permute-start.14 = (bf16[128,2048]{1,0:T(8,128)(2,1)}, bf16[128,2048]{1,0:T(8,128)(2,1)S(1)}, u32[]{:S(2)}, u32[]{:S(2)}) collective-permute-start(bf16[128,2048]{1,0:T(8,128)(2,1)} %pad_maximum_fusion.1), channel_id=1, source_target_pairs={{0,16},{1,17},{2,18},{3,19},{4,20},{5,21},{6,22},{7,23},{8,24},{9,... | collective-permute-start | bytes 1572872 | tf_op jit(solution)/shard_map/ppermute | solution.py:350
  61.6 9.6 %collective-permute-start.16 = (bf16[128,512]{1,0:T(8,128)(2,1)S(1)}, bf16[128,512]{1,0:T(8,128)(2,1)S(1)}, u32[]{:S(2)}, u32[]{:S(2)}) collective-permute-start(bf16[128,512]{1,0:T(8,128)(2,1)S(1)} %get-tuple-element.46), channel_id=1, source_target_pairs={{0,2},{1,10},{2,0},{3,8},{4,6},{5,14},{6,4},{7,12},{8,3},{9,11},{1... | collective-permute-start | bytes 393224 | tf_op jit(solution)/shard_map/ppermute | solution.py:350
  63.4 9.8 %collective-permute-start.17 = (bf16[128,512]{1,0:T(8,128)(2,1)S(1)}, bf16[128,512]{1,0:T(8,128)(2,1)S(1)}, u32[]{:S(2)}, u32[]{:S(2)}) collective-permute-start(bf16[128,512]{1,0:T(8,128)(2,1)S(1)} %get-tuple-element.47), channel_id=1, source_target_pairs={{0,4},{1,12},{2,6},{3,14},{4,0},{5,8},{6,2},{7,10},{8,5},{9,13},{1... | collective-permute-start | bytes 393224 | tf_op jit(solution)/shard_map/ppermute | solution.py:350
  63.5 13.4 %collective-permute-start.18 = (bf16[128,512]{1,0:T(8,128)(2,1)S(1)}, bf16[128,512]{1,0:T(8,128)(2,1)S(1)}, u32[]{:S(2)}, u32[]{:S(2)}) collective-permute-start(bf16[128,512]{1,0:T(8,128)(2,1)S(1)} %get-tuple-element.48), channel_id=1, source_target_pairs={{0,6},{1,14},{2,4},{3,12},{4,2},{5,10},{6,0},{7,8},{8,7},{9,15},{1... | collective-permute-start | bytes 393224 | tf_op jit(solution)/shard_map/ppermute | solution.py:350
  65.5 13.2 %collective-permute-start.15 = (bf16[128,512]{1,0:T(8,128)(2,1)S(1)}, bf16[128,512]{1,0:T(8,128)(2,1)S(1)}, u32[]{:S(2)}, u32[]{:S(2)}) collective-permute-start(bf16[128,512]{1,0:T(8,128)(2,1)S(1)} %get-tuple-element.43.done), channel_id=1, source_target_pairs={{0,0},{1,8},{2,2},{3,10},{4,4},{5,12},{6,6},{7,14},{8,1},{9,9},{10... | collective-permute-start | bytes 393224 | tf_op jit(solution)/shard_map/ppermute | solution.py:350
  71.3 8.0 %collective-permute-start.20 = (bf16[128,512]{1,0:T(8,128)(2,1)S(1)}, bf16[128,512]{1,0:T(8,128)(2,1)S(1)}, u32[]{:S(2)}, u32[]{:S(2)}) collective-permute-start(bf16[128,512]{1,0:T(8,128)(2,1)S(1)} %get-tuple-element.50), channel_id=1, source_target_pairs={{0,0},{1,8},{2,2},{3,10},{4,4},{5,12},{6,6},{7,14},{8,1},{9,9},{10... | collective-permute-start | bytes 393224 | tf_op jit(solution)/shard_map/ppermute | solution.py:350
  73.2 10.7 %collective-permute-start.21 = (bf16[128,512]{1,0:T(8,128)(2,1)S(1)}, bf16[128,512]{1,0:T(8,128)(2,1)S(1)}, u32[]{:S(2)}, u32[]{:S(2)}) collective-permute-start(bf16[128,512]{1,0:T(8,128)(2,1)S(1)} %get-tuple-element.51), channel_id=1, source_target_pairs={{0,2},{1,10},{2,0},{3,8},{4,6},{5,14},{6,4},{7,12},{8,3},{9,11},{1... | collective-permute-start | bytes 393224 | tf_op jit(solution)/shard_map/ppermute | solution.py:350
  76.8 9.3 %collective-permute-start.22 = (bf16[128,512]{1,0:T(8,128)(2,1)S(1)}, bf16[128,512]{1,0:T(8,128)(2,1)S(1)}, u32[]{:S(2)}, u32[]{:S(2)}) collective-permute-start(bf16[128,512]{1,0:T(8,128)(2,1)S(1)} %get-tuple-element.52), channel_id=1, source_target_pairs={{0,4},{1,12},{2,6},{3,14},{4,0},{5,8},{6,2},{7,10},{8,5},{9,13},{1... | collective-permute-start | bytes 393224 | tf_op jit(solution)/shard_map/ppermute | solution.py:350
  78.7 9.7 %collective-permute-start.23 = (bf16[128,512]{1,0:T(8,128)(2,1)S(1)}, bf16[128,512]{1,0:T(8,128)(2,1)S(1)}, u32[]{:S(2)}, u32[]{:S(2)}) collective-permute-start(bf16[128,512]{1,0:T(8,128)(2,1)S(1)} %get-tuple-element.53), channel_id=1, source_target_pairs={{0,6},{1,14},{2,4},{3,12},{4,2},{5,10},{6,0},{7,8},{8,7},{9,15},{1... | collective-permute-start | bytes 393224 | tf_op jit(solution)/shard_map/ppermute | solution.py:350

commit v3 on v2

--- a/solution.py
+++ b/solution.py
@@ -9,7 +9,6 @@
 
 AXES = ("grp", "anim", "mark")
 VMEM_LIMIT = 16 * 1024 * 1024
-PARTS = 2
 SHORT = pl.CostEstimate(flops=0, bytes_accessed=0, transcendentals=0)
 
 
@@ -92,12 +91,9 @@
     copies[3].wait()
     centred = (noncore_geno[...].astype(jnp.float32) - 2.0 * noncore_expected).astype(jnp.bfloat16)
     noncore[...] = centred
-    height = piece.shape[0] - markers
-    for i in range(rows // markers):
-        piece[markers:, i * markers:(i + 1) * markers] = centred[i * height:(i + 1) * height, :]
     copies[4].wait()
     dosage = geno[...].astype(jnp.float32).T
-    piece[:markers, :] = (dosage - 2.0 * expected).astype(jnp.bfloat16)
+    piece[...] = (dosage - 2.0 * expected).astype(jnp.bfloat16)
 
 
 def centre(part, core_geno, core_codes, breed_freqs, noncore_geno, noncore_codes):
@@ -108,7 +104,7 @@
         centre_kernel,
         in_specs=[pl.BlockSpec(memory_space=pltpu.SMEM)] + [anywhere()] * 5,
         out_specs=[whole()] * 2,
-        out_shape=[shape((markers + noncore * markers // rows, rows)), shape((noncore, markers))],
+        out_shape=[shape((markers, rows)), shape((noncore, markers))],
         scratch_shapes=[
             pltpu.VMEM(core_codes.shape, jnp.int32),
             pltpu.VMEM(breed_freqs.shape, jnp.float32),
@@ -121,36 +117,6 @@
         cost_estimate=SHORT,
         name="centre",
     )(part[None], *[in_hbm(operand) for operand in operands])
-
-
-def unfold_kernel(count, flag, *refs):
-    markers = refs[-1].shape[1]
-    pieces, outs = refs[:-2], refs[-2:]
-    height = pieces[0].shape[0] - markers
-    folds = pieces[0].shape[1] // markers
-    for b in range(count):
-        for i in range(folds):
-            spot = slice((b * folds + i) * height, (b * folds + i + 1) * height)
-            for j in range(2):
-                @pl.when(flag[0] == j)
-                def _(b=b, i=i, j=j, spot=spot):
-                    for k in range(2):
-                        piece = pieces[b + count * (j ^ k)]
-                        outs[k][spot, :] = piece[markers:, i * markers:(i + 1) * markers]
-
-
-def unfold(pieces, noncore_shape, flag):
-    rows, markers = noncore_shape
-    count = len(pieces) // 2
-    return pl.pallas_call(
-        functools.partial(unfold_kernel, count),
-        in_specs=[pl.BlockSpec(memory_space=pltpu.SMEM)] + [whole()] * len(pieces),
-        out_specs=[whole()] * 2,
-        out_shape=[shape((rows * count, markers))] * 2,
-        compiler_params=params(),
-        cost_estimate=SHORT,
-        name="unfold",
-    )(flag.astype(jnp.int32)[None], *pieces)
 
 
 def absorb_kernel(count, pairs, ahead, first, scale, place, *refs):
@@ -168,14 +134,21 @@
     rows, columns = pieces[0].shape[1], inverse.shape[-1]
 
     copies = []
+    half = columns // 2
     for i in range(0 if fetched else count + ahead):
         block = pl.ds(pl.multiple_of(place[i] * rows, rows), rows)
         target = slabs.at[i] if i < count else later.at[i - count]
-        copies.append(pltpu.make_async_copy(inverse.at[block, :], target, sem.at[i]))
-        copies[-1].start()
+        for j, side in enumerate((place[count + ahead + 1], 1 - place[count + ahead + 1])):
+            source = inverse.at[block, pl.ds(pl.multiple_of(side * half, half), half)]
+            copies.append(
+                pltpu.make_async_copy(
+                    source, target.at[:, j * half:(j + 1) * half], sem.at[2 * i + j]
+                )
+            )
+            copies[-1].start()
     for i, pair in enumerate(related):
         values = [
-            (matmul(noncore[...], p[:noncore.shape[1], :]) * scale).astype(jnp.bfloat16)
+            (matmul(noncore[...], p[...]) * scale).astype(jnp.bfloat16)
             for p in pair
         ]
         for j in range(2):
@@ -184,31 +157,34 @@
                 own[:, i * rows:(i + 1) * rows] = values[j]
                 send[:, i * rows:(i + 1) * rows] = values[1 - j]
 
-    for copy in copies[:count]:
+    for copy in copies[:2 * count]:
         copy.wait()
     for start in range(0, columns, 256):
         part = slice(start, start + 256)
         total = None if first else before[:, part]
         for i in range(count):
-            product = matmul(pieces[i][:outs[0].shape[0], :], slabs[i, :, part])
+            product = matmul(pieces[i][...], slabs[i, :, part])
             total = product if total is None else total + product
-        outs[0][:, part] = total
-        for i, out in enumerate(outs[1:]):
-            width = out.shape[1]
-            if i * width <= start < (i + 1) * width:
-                out[:, start - i * width:start - i * width + 256] = total.astype(out.dtype)
-    for copy in copies[count:]:
+        if len(outs) == 1:
+            outs[0][:, part] = total
+        else:
+            outs[start // half][:, start % half:start % half + 256] = total.astype(
+                outs[start // half].dtype
+            )
+    for copy in copies[2 * count:]:
         copy.wait()
 
 
-def absorb(pieces, blocks, inverse, before, noncore, pairs, flag, scale, parts=0):
+def absorb(pieces, blocks, inverse, before, noncore, pairs, flag, side, scale, final=False):
     count, rows, columns, markers = len(pieces), pieces[0].shape[1], inverse.shape[-1], noncore.shape[1]
     ahead, fetched = len(blocks) - count, inverse.ndim == 3
     operands = [*pieces, inverse] + [piece for pair in pairs for piece in pair]
     operands += [noncore] if pairs else []
     operands += [] if before is None else [before]
-    outs = [shape((markers, columns), jnp.float32)]
-    outs += [shape((markers, columns // parts)) for _ in range(parts)]
+    if final:
+        outs = [shape((markers, columns // 2), kind) for kind in (jnp.float32, jnp.bfloat16)]
+    else:
+        outs = [shape((markers, columns), jnp.float32)]
     outs += [shape((noncore.shape[0], rows * len(pairs)))] * 2 if pairs else []
     outs += [shape((ahead, rows, columns))] if ahead else []
     specs = [whole()] * len(operands)
@@ -220,29 +196,12 @@
         out_shape=outs,
         scratch_shapes=[] if fetched else [
             pltpu.VMEM((count, rows, columns), jnp.bfloat16),
-            pltpu.SemaphoreType.DMA((count + ahead,)),
+            pltpu.SemaphoreType.DMA((2 * (count + ahead),)),
         ],
         compiler_params=params(),
         cost_estimate=SHORT,
         name="absorb",
-    )(jnp.stack(blocks + [flag]).astype(jnp.int32), *operands)
-
-
-def add_kernel(start, total, other, out):
-    width = out.shape[1]
-    out[...] = (total[:, start:start + width] + other[...].astype(jnp.float32)).astype(out.dtype)
-
-
-def add_part(total, other, start):
-    return pl.pallas_call(
-        functools.partial(add_kernel, start),
-        in_specs=[whole()] * 2,
-        out_specs=whole(),
-        out_shape=shape(other.shape),
-        compiler_params=params(),
-        cost_estimate=SHORT,
-        name="add_part",
-    )(total, other)
+    )(jnp.stack(blocks + [flag, side]).astype(jnp.int32), *operands)
 
 
 def relation_kernel(count, scale, flag, done, noncore, *refs):
@@ -251,7 +210,7 @@
     for i in range(count):
         columns = slice(i * width, (i + 1) * width)
         values = [
-            (matmul(noncore[...], pieces[2 * i + j][:noncore.shape[1], :]) * scale).astype(jnp.bfloat16)
+            (matmul(noncore[...], pieces[2 * i + j][...]) * scale).astype(jnp.bfloat16)
             for j in range(2)
         ]
         for j in range(2):
@@ -276,25 +235,30 @@
     )(flag.astype(jnp.int32)[None], after, noncore, *[piece for pair in pairs for piece in pair])
 
 
-def regression_kernel(count, scale, kept, got, mine, other, *outs):
+def regression_kernel(count, scale, flag, kept, got, mine, one, two, *outs):
     rows = outs[0].shape[0]
-    for k in range(count):
-        block = slice(k * rows, (k + 1) * rows)
-        value = matmul(kept[block, :], mine[...]) + matmul(got[block, :], other[...])
-        outs[k][...] = (value * scale).astype(jnp.bfloat16)
-
-
-def regress(kept, got, mine, other, count, scale):
+    for j in range(2):
+        left, right = ((mine, one), (one, two))[j]
+
+        @pl.when(flag[0] == j)
+        def _(left=left, right=right):
+            for k in range(count):
+                block = slice(k * rows, (k + 1) * rows)
+                value = matmul(kept[block, :], left[...]) + matmul(got[block, :], right[...])
+                outs[k][...] = (value * scale).astype(jnp.bfloat16)
+
+
+def regress(kept, got, mine, one, two, flag, count, scale):
     rows, width = kept.shape[0] // count, mine.shape[1]
     return pl.pallas_call(
         functools.partial(regression_kernel, count, scale),
-        in_specs=[whole()] * 4,
+        in_specs=[pl.BlockSpec(memory_space=pltpu.SMEM)] + [whole()] * 5,
         out_specs=[whole()] * count,
         out_shape=[shape((rows, width))] * count,
         compiler_params=params(),
         cost_estimate=SHORT,
         name="regress",
-    )(kept, got, mine, other)
+    )(flag.astype(jnp.int32)[None], kept, got, mine, one, two)
 
 
 def assemble_kernel(jobs, place, *refs):
@@ -345,8 +309,10 @@
         for g in range(2):
             for a in range(n_anim):
                 for m in range(2):
-                    tg, ta, tm = target(g, a, m)
-                    pairs.append(((g * n_anim + a) * 2 + m, (tg * n_anim + ta) * 2 + tm))
+                    if to := target(g, a, m):
+                        pairs.append(
+                            ((g * n_anim + a) * 2 + m, (to[0] * n_anim + to[1]) * 2 + to[2])
+                        )
         return lax.ppermute(array, AXES, pairs)
 
     def along_anim(array, bits):
@@ -357,6 +323,9 @@
 
     def across_mark(array):
         return move(array, lambda g, a, m: (g, a, 1 - m))
+
+    def after(*arrays):
+        return lax.optimization_barrier(arrays)
 
     own, noncore = centre(
         grp, core_geno, core_codes, breed_freqs, noncore_geno, noncore_codes
@@ -368,53 +337,47 @@
     inverse = in_hbm(core_inverse)
     pieces, related = {0: own}, []
 
-    def take(chosen, total, pairs=(), ahead=(), parts=0, rows_of=inverse):
+    def take(chosen, total, pairs=(), ahead=(), rows_of=inverse, final=False):
         result = absorb(
             [pieces[b] for b in chosen], [(anim ^ b) * 2 + grp for b in [*chosen, *ahead]], rows_of,
-            total, both, [(pieces[b], pieces[b + top]) for b in pairs], flag, scale, parts,
+            total, both, [(pieces[b], pieces[b + top]) for b in pairs], flag, grp,
+            scale, final,
         )
         if pairs:
-            related.extend(result[1 + parts:3 + parts])
-        return [result[0], *result[1:1 + parts]] + list(result[3 + parts if pairs else 1 + parts:])
+            related.extend(result[1:3])
+        return [result[0], *result[3 if pairs else 1:]]
 
     low = list(range(2, top, 2))
-    for bits in low + [top, 1]:
+    for bits in [top] + low + [1]:
         pieces[bits] = along_anim(own, bits)
+    held = [top, 1]
+    *moved, both = after(*[pieces[b] for b in held], both)
+    pieces.update(zip(held, moved))
+    for bits in low:
+        pieces[top + bits] = along_anim(pieces[top], bits)
+    pieces[top + 1] = along_anim(pieces[top], 1)
     for bits in low:
         pieces[bits + 1] = along_anim(pieces[bits], 1)
-    held = [top, 1] + [b + 1 for b in low]
-    for b, piece in zip(held, lax.optimization_barrier([pieces[b] for b in held])):
-        pieces[b] = piece
+    (total,) = take([0, 1, top] + low, None, [0])
+    pieces[top + 1], total = after(pieces[top + 1], total)
     for bits in low:
-        pieces[top + bits] = along_anim(pieces[top], bits)
-    for bits in [0] + low:
-        pieces[top + bits + 1] = along_anim(pieces[top + bits], 1)
-    (total,) = take([0, 1] + low, None)
-    last = [top + bits + i for bits in low for i in range(2)]
-    total, slabs = take([b + 1 for b in low] + [top, top + 1], total, [0, 1], last)
-    total, *send = take(last, total, parts=PARTS, rows_of=slabs)
-
-    kept, got = unfold([pieces[b] for b in range(n_anim)], noncore.shape, flag)
-    got = across_mark(got)
-    from_other = [across_grp(part) for part in send]
-
-    arrived, slots = [], []
-    for i, part in enumerate(from_other):
-        width = part.shape[1]
-        mine = add_part(total, part, i * width)
-        other = across_mark(mine)
-        if i + 1 < PARTS:
-            other, from_other[i + 1] = lax.optimization_barrier((other, from_other[i + 1]))
-        results = regress(kept, got, mine, other, top, scale)
-        if i == 0:
-            begun = results[0]
-        for k in range(top):
-            arrived.append(
-                move(results[k], lambda g, a, m, k=k: (g, m * top + (a % top ^ k), a // top))
-            )
-            slots.append((anim ^ k) % top * PARTS + i)
-
-    related += relate(both, [(pieces[b - top], pieces[b]) for b in last], flag, scale, begun)
+        pieces[top + bits + 1] = along_anim(pieces[top + 1], bits)
+
+    kept, pieces[top + low[-1]] = after(both, pieces[top + low[-1]])
+    beside = along_anim(kept, 1)
+
+    last = [bits + i for bits in low for i in (1, top + 1)]
+    total, slabs = take([top + 1] + [top + b for b in low], total, [1] + low, last)
+    keep, send = take(last, total, rows_of=slabs, final=True)
+    from_other = across_grp(send)
+
+    related += relate(both, [(pieces[b + 1], pieces[top + b + 1]) for b in low], flag, scale, keep)
+    beside, related[-1] = after(beside, related[-1])
+    kept = jnp.concatenate([kept, beside], axis=0)
+    bit = 2
+    while bit < top:
+        kept = jnp.concatenate([kept, along_anim(kept, bit)], axis=0)
+        bit *= 2
     received = [across_mark(part) for part in related[1::2]]
     sums = [
         jnp.concatenate(
@@ -428,10 +391,25 @@
         )
         for part in (slice(0, rows), slice(rows, 2 * rows))
     ]
+
+    sums[1], from_other = after(sums[1], from_other)
     swapped = across_grp(sums[1])
 
+    mine = (keep + from_other.astype(jnp.float32)).astype(jnp.bfloat16)
+    one = move(mine, lambda g, a, m: (g, a ^ top, m) if m == a // top else (g, a, 1 - m))
+    two = move(mine, lambda g, a, m: None if m == a // top else (g, a ^ top, 1 - m))
+
+    results = regress(kept, across_mark(kept), mine, one, two, flag, 2 * top, scale)
+    step = lambda k: k >> 1
+    arrived = [
+        results[k] if k == 0 else move(results[k], lambda g, a, m, k=k: (g ^ k & 1, a ^ step(k), m))
+        for k in range(2 * top)
+    ]
+    slots = [((anim ^ step(k)) % top) * 2 + (grp ^ k & 1) for k in range(2 * top)]
+    width = mine.shape[1]
+
     width_of_piece = own.shape[1]
-    order = [0, 1] + [b - top for b in last]
+    order = [0, 1] + low + [b + 1 for b in low]
     places = [2 * ((anim ^ b) % top) + g for g in (grp, 1 - grp) for b in order]
     return tuple(
         assemble([([sums[0], swapped], places, width_of_piece), (arrived, slots, width)])
@@ -449,7 +427,7 @@
     )
     out_specs = (P(("grp", "anim"), "mark"), P(("grp", "anim"), "mark"))
     n_grp, n_anim, n_mark = (mesh.shape[name] for name in AXES)
-    if n_grp == 2 and n_mark == 2 and n_anim in (8, 16):
+    if n_grp == 2 and n_mark == 2 and n_anim in (4, 8, 16):
         body = functools.partial(permute_body, n_anim=n_anim, n_mark=n_mark)
     else:
         body = functools.partial(gather_body, n_mark=n_mark)

time: 90.6 us -> 82.9 us (0.915)
  the two profiles are of different devices: /device:TPU:9 before, /device:TPU:0 now
where the time goes in v3:
time: 82.9 us; the launch traced here: 82.7 us
  starting transfers between devices  36.2 us (44%)
  waiting for transfers between devices  30.7 us (37%)
  Pallas kernels  13.1 us (16%)
  other arithmetic  1.55 us (2%)
  between operations  0.84 us (1%)
    ppermute x25, starting transfers between devices, move(): return lax.ppermute(array, AXES, pairs)  36.2 us
    ppermute x25, waiting for transfers between devices, move(): return lax.ppermute(array, AXES, pairs)  30.7 us
    pallas_call x3, Pallas kernels, absorb(): pl.pallas_call(functools.partial(absorb_kernel, count, len(pairs), ahead,...  8.24 us
    pallas_call x1, Pallas kernels, assemble(): pl.pallas_call(functools.partial(assemble_kernel, [(len(job[0]), job[2])...  1.98 us
    pallas_call x1, Pallas kernels, centre(): pl.pallas_call(centre_kernel, in_specs=[pl.BlockSpec(memory_space=pltpu.S...  1.75 us
  transfers between devices with their start and end apart: 25, of which 11 were waited for; matrix products, arithmetic and copies ran while one was open for 2% of the time, Pallas kernels for 11%

profile of v3, /device:TPU:0, one launch (start us, length us, event | category | flops | bytes accessed | tf_op | source)
XLA Modules:
  0.0 82.7 jit_solution(17141334111380148763)
XLA Ops:
  0.6 1.8 %centre.1 = (bf16[256,512]{1,0:T(8,128)(2,1)S(1)}, bf16[128,256]{1,0:T(8,128)(2,1)S(1)}) custom-call(s32[1]{0:T(128)} %bitcast.17.place, s32[1024,256]{1,0:T(8,128)} %geno.1, s32[5,1024]{1,0:T(8,128)} %codes.1, f32[5,256]{1,0:T(8,128)} %freqs.1, s32[128,256]{1,0:T(8,128)} %noncore_geno.1, s32[5,128]{1,0:T(8,128)} %noncore_codes.1), custom_call_target="tpu_custom_call" | custom-call | tf_op jit(solution)/shard_map/centre/pallas_call | solution.py:103
  2.4 4.1 %collective-permute-start = (bf16[256,512]{1,0:T(8,128)(2,1)S(1)}, bf16[256,512]{1,0:T(8,128)(2,1)S(1)}, u32[]{:S(2)}, u32[]{:S(2)}) collective-permute-start(bf16[256,512]{1,0:T(8,128)(2,1)S(1)} %get-tuple-element.34.refs_0_.refs_5_), channel_id=1, source_target_pairs={{0,8},{1,9},{2,10},{3,11},{4,12},{5,13},{6,14},{7,15},{8,0},{9,1},... | collective-permute-start | bytes 786440 | tf_op jit(solution)/shard_map/ppermute | solution.py:316
  6.5 1.5 %collective-permute-start.1 = (bf16[256,512]{1,0:T(8,128)(2,1)S(1)}, bf16[256,512]{1,0:T(8,128)(2,1)S(1)}, u32[]{:S(2)}, u32[]{:S(2)}) collective-permute-start(bf16[256,512]{1,0:T(8,128)(2,1)S(1)} %get-tuple-element.34.refs_0_.refs_5_), channel_id=1, source_target_pairs={{0,2},{1,3},{2,0},{3,1},{4,6},{5,7},{6,4},{7,5},{8,10},{9,11},{10,... | collective-permute-start | bytes 786440 | tf_op jit(solution)/shard_map/ppermute | solution.py:316
  8.0 1.5 %collective-permute-start.2 = (bf16[128,256]{1,0:T(8,128)(2,1)S(1)}, bf16[128,256]{1,0:T(8,128)(2,1)S(1)}, u32[]{:S(2)}, u32[]{:S(2)}) collective-permute-start(bf16[128,256]{1,0:T(8,128)(2,1)S(1)} %get-tuple-element.35), channel_id=1, source_target_pairs={{0,16},{1,17},{2,18},{3,19},{4,20},{5,21},{6,22},{7,23},{8,24},{9,... | collective-permute-start | bytes 196616 | tf_op jit(solution)/shard_map/ppermute | solution.py:316
  9.5 1.6 %collective-permute-start.3 = (bf16[256,512]{1,0:T(8,128)(2,1)S(1)}, bf16[256,512]{1,0:T(8,128)(2,1)S(1)}, u32[]{:S(2)}, u32[]{:S(2)}) collective-permute-start(bf16[256,512]{1,0:T(8,128)(2,1)S(1)} %get-tuple-element.34.refs_0_.refs_5_), channel_id=1, source_target_pairs={{0,4},{1,5},{2,6},{3,7},{4,0},{5,1},{6,2},{7,3},{8,12},{9,13},{10,... | collective-permute-start | bytes 786440 | tf_op jit(solution)/shard_map/ppermute | solution.py:316
  11.1 1.2 %collective-permute-done.2 = bf16[128,256]{1,0:T(8,128)(2,1)S(1)} collective-permute-done((bf16[128,256]{1,0:T(8,128)(2,1)S(1)}, bf16[128,256]{1,0:T(8,128)(2,1)S(1)}, u32[]{:S(2)}, u32[]{:S(2)}) %collective-permute-start.2) | collective-permute-done | bytes 65568 | tf_op jit(solution)/shard_map/ppermute | solution.py:316
  12.3 6.3 %collective-permute-done.refs_2_.refs_6_ = bf16[256,512]{1,0:T(8,128)(2,1)S(1)} collective-permute-done((bf16[256,512]{1,0:T(8,128)(2,1)S(1)}, bf16[256,512]{1,0:T(8,128)(2,1)S(1)}, u32[]{:S(2)}, u32[]{:S(2)}) %collective-permute-start) | collective-permute-done | bytes 262176 | tf_op jit(solution)/shard_map/ppermute | solution.py:316
  18.5 1.5 %collective-permute-start.5 = (bf16[256,512]{1,0:T(8,128)(2,1)S(1)}, bf16[256,512]{1,0:T(8,128)(2,1)S(1)}, u32[]{:S(2)}, u32[]{:S(2)}) collective-permute-start(bf16[256,512]{1,0:T(8,128)(2,1)S(1)} %collective-permute-done.refs_2_.refs_6_), channel_id=1, source_target_pairs={{0,2},{1,3},{2,0},{3,1},{4,6},{5,7},{6,4},{7,5},{8,10},{9,11},{10,... | collective-permute-start | bytes 786440 | tf_op jit(solution)/shard_map/ppermute | solution.py:316
  21.8 4.1 %absorb.3 = (f32[256,1024]{1,0:T(8,128)S(1)}, bf16[256,512]{1,0:T(8,128)(2,1)S(1)}, bf16[256,512]{1,0:T(8,128)(2,1)S(1)}) custom-call(s32[6]{0:T(128)S(1)} %stack.107.place, bf16[256,512]{1,0:T(8,128)(2,1)S(1)} %get-tuple-element.34.refs_0_.refs_5_, bf16[256,512]{1,0:T(8,128)(2,1)S(1)} %collective-permute-done.1.refs_1_.refs_3_, ...), custom_call_target="tpu_custom_call" | custom-call | tf_op jit(solution)/shard_map/absorb/pallas_call | solution.py:192
  25.8 1.9 %collective-permute-done.5.refs_0_.refs_4_ = bf16[256,512]{1,0:T(8,128)(2,1)S(1)} collective-permute-done((bf16[256,512]{1,0:T(8,128)(2,1)S(1)}, bf16[256,512]{1,0:T(8,128)(2,1)S(1)}, u32[]{:S(2)}, u32[]{:S(2)}) %collective-permute-start.5) | collective-permute-done | bytes 262176 | tf_op jit(solution)/shard_map/ppermute | solution.py:316
  28.4 1.5 %collective-permute-start.10 = (bf16[256,256]{1,0:T(8,128)(2,1)S(1)}, bf16[256,256]{1,0:T(8,128)(2,1)S(1)}, u32[]{:S(2)}, u32[]{:S(2)}) collective-permute-start(bf16[256,256]{1,0:T(8,128)(2,1)S(1)} %pad_maximum_fusion.3.refs_7_.noncore), channel_id=1, source_target_pairs={{0,2},{1,3},{2,0},{3,1},{4,6},{5,7},{6,4},{7,5},{8,10},{9,11},{10,... | collective-permute-start | bytes 393224 | tf_op jit(solution)/shard_map/ppermute | solution.py:316
  30.0 2.9 %absorb.4 = (f32[256,1024]{1,0:T(8,128)S(1)}, bf16[256,1024]{1,0:T(8,128)(2,1)S(1)}, bf16[256,1024]{1,0:T(8,128)(2,1)S(1)}, bf16[2,512,1024]{2,1,0:T(8,128)(2,1)S(1)}) custom-call(s32[6]{0:T(128)S(1)} %stack.112.place, bf16[256,512]{1,0:T(8,128)(2,1)S(1)} %collective-permute-done.5.refs_0_.refs_4_, ...), custom_call_target="tpu_custom_call" | custom-call | tf_op jit(solution)/shard_map/absorb/pallas_call | solution.py:192
  33.2 0.9 %collective-permute-done.9.refs_1_ = bf16[256,512]{1,0:T(8,128)(2,1)S(1)} collective-permute-done((bf16[256,512]{1,0:T(8,128)(2,1)S(1)}, bf16[256,512]{1,0:T(8,128)(2,1)S(1)}, u32[]{:S(2)}, u32[]{:S(2)}) %collective-permute-start.9) | collective-permute-done | bytes 262176 | tf_op jit(solution)/shard_map/ppermute | solution.py:316
  34.2 1.3 %absorb.5 = (f32[256,512]{1,0:T(8,128)S(1)}, bf16[256,512]{1,0:T(8,128)(2,1)S(1)}) custom-call(s32[4]{0:T(128)S(1)} %pad_add_fusion.place, bf16[256,512]{1,0:T(8,128)(2,1)S(1)} %collective-permute-done.8.refs_0_, bf16[256,512]{1,0:T(8,128)(2,1)S(1)} %collective-permute-done.9.refs_1_, bf16[2,512,1024]{2,1,0:T(8,128)(2,1)S(1)} %get-tuple-element.47.refs_2_, ...), custom_call_target="tpu_custom_call" | custom-call | tf_op jit(solution)/shard_map/absorb/pallas_call | solution.py:192
  35.9 0.7 collective-permute-start.14
  36.6 1.0 %add_convert_fusion.4 = (bf16[128,512]{1,0:T(8,128)(2,1)S(1)}, bf16[128,512]{1,0:T(8,128)(2,1)S(1)}) fusion(bf16[256,512]{1,0:T(8,128)(2,1)} %collective-permute-done.4, bf16[256,512]{1,0:T(8,128)(2,1)S(1)} %get-tuple-element.39), kind=kLoop, calls=%fused_computation.7 | loop fusion | flops 524288 | bytes 786432 | tf_op jit(solution)/shard_map/convert_element_type | solution.py:385
  37.7 1.6 %collective-permute-start.12 = (bf16[256,512]{1,0:T(8,128)(2,1)S(1)}, bf16[256,512]{1,0:T(8,128)(2,1)S(1)}, u32[]{:S(2)}, u32[]{:S(2)}) collective-permute-start(bf16[256,512]{1,0:T(8,128)(2,1)S(1)} %get-tuple-element.54), channel_id=1, source_target_pairs={{0,16},{1,17},{2,18},{3,19},{4,20},{5,21},{6,22},{7,23},{8,24},{9,... | collective-permute-start | bytes 786440 | tf_op jit(solution)/shard_map/ppermute | solution.py:316
  39.3 4.2 %collective-permute-done.14 = bf16[512,256]{1,0:T(8,128)(2,1)S(1)} collective-permute-done((bf16[512,256]{1,0:T(8,128)(2,1)S(1)}, bf16[512,256]{1,0:T(8,128)(2,1)S(1)}, u32[]{:S(2)}, u32[]{:S(2)}) %collective-permute-start.14) | collective-permute-done | bytes 262176 | tf_op jit(solution)/shard_map/ppermute | solution.py:316
  43.9 2.5 %collective-permute-done.12 = bf16[256,512]{1,0:T(8,128)(2,1)S(1)} collective-permute-done((bf16[256,512]{1,0:T(8,128)(2,1)S(1)}, bf16[256,512]{1,0:T(8,128)(2,1)S(1)}, u32[]{:S(2)}, u32[]{:S(2)}) %collective-permute-start.12) | collective-permute-done | bytes 262176 | tf_op jit(solution)/shard_map/ppermute | solution.py:316
  46.4 1.5 %collective-permute-start.13 = (bf16[128,2048]{1,0:T(8,128)(2,1)S(1)}, bf16[128,2048]{1,0:T(8,128)(2,1)S(1)}, u32[]{:S(2)}, u32[]{:S(2)}) collective-permute-start(bf16[128,2048]{1,0:T(8,128)(2,1)S(1)} %pad_maximum_fusion.1), channel_id=1, source_target_pairs={{0,16},{1,17},{2,18},{3,19},{4,20},{5,21},{6,22},{7,23},{8,24},{9,... | collective-permute-start | bytes 1572872 | tf_op jit(solution)/shard_map/ppermute | solution.py:316
  48.0 3.4 %collective-permute-start.16 = (bf16[256,512]{1,0:T(8,128)(2,1)S(1)}, bf16[256,512]{1,0:T(8,128)(2,1)S(1)}, u32[]{:S(2)}, u32[]{:S(2)}) collective-permute-start(bf16[256,512]{1,0:T(8,128)(2,1)S(1)} %add_convert_fusion.mine), channel_id=1, source_target_pairs={{0,8},{1,0},{2,10},{3,2},{4,12},{5,4},{6,14},{7,6},{8,9},{9,1},{10... | collective-permute-start | bytes 786440 | tf_op jit(solution)/shard_map/ppermute | solution.py:316
  52.1 4.7 %collective-permute-done.16.one = bf16[256,512]{1,0:T(8,128)(2,1)S(1)} collective-permute-done((bf16[256,512]{1,0:T(8,128)(2,1)S(1)}, bf16[256,512]{1,0:T(8,128)(2,1)S(1)}, u32[]{:S(2)}, u32[]{:S(2)}) %collective-permute-start.16) | collective-permute-done | bytes 262176 | tf_op jit(solution)/shard_map/ppermute | solution.py:316
  56.9 0.7 regress.1
  58.2 1.5 %collective-permute-start.19 = (bf16[128,512]{1,0:T(8,128)(2,1)S(1)}, bf16[128,512]{1,0:T(8,128)(2,1)S(1)}, u32[]{:S(2)}, u32[]{:S(2)}) collective-permute-start(bf16[128,512]{1,0:T(8,128)(2,1)S(1)} %get-tuple-element.60), channel_id=1, source_target_pairs={{0,2},{1,3},{2,0},{3,1},{4,6},{5,7},{6,4},{7,5},{8,10},{9,11},{10,... | collective-permute-start | bytes 393224 | tf_op jit(solution)/shard_map/ppermute | solution.py:316
  59.8 1.6 %collective-permute-start.20 = (bf16[128,512]{1,0:T(8,128)(2,1)S(1)}, bf16[128,512]{1,0:T(8,128)(2,1)S(1)}, u32[]{:S(2)}, u32[]{:S(2)}) collective-permute-start(bf16[128,512]{1,0:T(8,128)(2,1)S(1)} %get-tuple-element.61), channel_id=1, source_target_pairs={{0,18},{1,19},{2,16},{3,17},{4,22},{5,23},{6,20},{7,21},{8,26},{9,... | collective-permute-start | bytes 393224 | tf_op jit(solution)/shard_map/ppermute | solution.py:316
  61.3 6.1 %collective-permute-start.21 = (bf16[128,512]{1,0:T(8,128)(2,1)S(1)}, bf16[128,512]{1,0:T(8,128)(2,1)S(1)}, u32[]{:S(2)}, u32[]{:S(2)}) collective-permute-start(bf16[128,512]{1,0:T(8,128)(2,1)S(1)} %get-tuple-element.62), channel_id=1, source_target_pairs={{0,4},{1,5},{2,6},{3,7},{4,0},{5,1},{6,2},{7,3},{8,12},{9,13},{10,... | collective-permute-start | bytes 393224 | tf_op jit(solution)/shard_map/ppermute | solution.py:316
  67.6 2.8 %collective-permute-start.23 = (bf16[128,512]{1,0:T(8,128)(2,1)S(1)}, bf16[128,512]{1,0:T(8,128)(2,1)S(1)}, u32[]{:S(2)}, u32[]{:S(2)}) collective-permute-start(bf16[128,512]{1,0:T(8,128)(2,1)S(1)} %get-tuple-element.64), channel_id=1, source_target_pairs={{0,6},{1,7},{2,4},{3,5},{4,2},{5,3},{6,0},{7,1},{8,14},{9,15},{10,... | collective-permute-start | bytes 393224 | tf_op jit(solution)/shard_map/ppermute | solution.py:316
  70.4 1.7 %collective-permute-start.24 = (bf16[128,512]{1,0:T(8,128)(2,1)S(1)}, bf16[128,512]{1,0:T(8,128)(2,1)S(1)}, u32[]{:S(2)}, u32[]{:S(2)}) collective-permute-start(bf16[128,512]{1,0:T(8,128)(2,1)S(1)} %get-tuple-element.65), channel_id=1, source_target_pairs={{0,22},{1,23},{2,20},{3,21},{4,18},{5,19},{6,16},{7,17},{8,30},{9,... | collective-permute-start | bytes 393224 | tf_op jit(solution)/shard_map/ppermute | solution.py:316
  72.1 2.6 %collective-permute-done.22.refs_7_ = bf16[128,512]{1,0:T(8,128)(2,1)S(1)} collective-permute-done((bf16[128,512]{1,0:T(8,128)(2,1)S(1)}, bf16[128,512]{1,0:T(8,128)(2,1)S(1)}, u32[]{:S(2)}, u32[]{:S(2)}) %collective-permute-start.22) | collective-permute-done | bytes 131104 | tf_op jit(solution)/shard_map/ppermute | solution.py:316
  74.8 3.0 %collective-permute-done.23.refs_8_ = bf16[128,512]{1,0:T(8,128)(2,1)S(1)} collective-permute-done((bf16[128,512]{1,0:T(8,128)(2,1)S(1)}, bf16[128,512]{1,0:T(8,128)(2,1)S(1)}, u32[]{:S(2)}, u32[]{:S(2)}) %collective-permute-start.23) | collective-permute-done | bytes 131104 | tf_op jit(solution)/shard_map/ppermute | solution.py:316
  77.8 2.9 %collective-permute-done.24.refs_9_ = bf16[128,512]{1,0:T(8,128)(2,1)S(1)} collective-permute-done((bf16[128,512]{1,0:T(8,128)(2,1)S(1)}, bf16[128,512]{1,0:T(8,128)(2,1)S(1)}, u32[]{:S(2)}, u32[]{:S(2)}) %collective-permute-start.24) | collective-permute-done | bytes 131104 | tf_op jit(solution)/shard_map/ppermute | solution.py:316
  80.7 2.0 %assemble.1 = (bf16[128,4096]{1,0:T(8,128)(2,1)}, bf16[128,4096]{1,0:T(8,128)(2,1)}) custom-call(s32[16]{0:T(128)S(1)} %stack.100.place, bf16[128,2048]{1,0:T(8,128)(2,1)S(1)} %pad_maximum_fusion.refs_0_, bf16[128,2048]{1,0:T(8,128)(2,1)S(1)} %collective-permute-done.13.refs_1_, bf16[128,512]{1,0:T(8,128)(2,1)S(1)} %get-tuple-element.58.refs_2_, ...), custom_call_target="tpu_custom_call" | custom-call | tf_op jit(solution)/shard_map/assemble/pallas_call | solution.py:287
  (40 shorter events, 5.2 us)
Async XLA Ops:
  2.4 16.1 %collective-permute-start = (bf16[256,512]{1,0:T(8,128)(2,1)S(1)}, bf16[256,512]{1,0:T(8,128)(2,1)S(1)}, u32[]{:S(2)}, u32[]{:S(2)}) collective-permute-start(bf16[256,512]{1,0:T(8,128)(2,1)S(1)} %get-tuple-element.34.refs_0_.refs_5_), channel_id=1, source_target_pairs={{0,8},{1,9},{2,10},{3,11},{4,12},{5,13},{6,14},{7,15},{8,0},{9,1},... | collective-permute-start | bytes 786440 | tf_op jit(solution)/shard_map/ppermute | solution.py:316
  6.5 12.0 %collective-permute-start.1 = (bf16[256,512]{1,0:T(8,128)(2,1)S(1)}, bf16[256,512]{1,0:T(8,128)(2,1)S(1)}, u32[]{:S(2)}, u32[]{:S(2)}) collective-permute-start(bf16[256,512]{1,0:T(8,128)(2,1)S(1)} %get-tuple-element.34.refs_0_.refs_5_), channel_id=1, source_target_pairs={{0,2},{1,3},{2,0},{3,1},{4,6},{5,7},{6,4},{7,5},{8,10},{9,11},{10,... | collective-permute-start | bytes 786440 | tf_op jit(solution)/shard_map/ppermute | solution.py:316
  8.0 4.3 %collective-permute-start.2 = (bf16[128,256]{1,0:T(8,128)(2,1)S(1)}, bf16[128,256]{1,0:T(8,128)(2,1)S(1)}, u32[]{:S(2)}, u32[]{:S(2)}) collective-permute-start(bf16[128,256]{1,0:T(8,128)(2,1)S(1)} %get-tuple-element.35), channel_id=1, source_target_pairs={{0,16},{1,17},{2,18},{3,19},{4,20},{5,21},{6,22},{7,23},{8,24},{9,... | collective-permute-start | bytes 196616 | tf_op jit(solution)/shard_map/ppermute | solution.py:316
  9.5 11.7 %collective-permute-start.3 = (bf16[256,512]{1,0:T(8,128)(2,1)S(1)}, bf16[256,512]{1,0:T(8,128)(2,1)S(1)}, u32[]{:S(2)}, u32[]{:S(2)}) collective-permute-start(bf16[256,512]{1,0:T(8,128)(2,1)S(1)} %get-tuple-element.34.refs_0_.refs_5_), channel_id=1, source_target_pairs={{0,4},{1,5},{2,6},{3,7},{4,0},{5,1},{6,2},{7,3},{8,12},{9,13},{10,... | collective-permute-start | bytes 786440 | tf_op jit(solution)/shard_map/ppermute | solution.py:316
  18.5 9.2 %collective-permute-start.5 = (bf16[256,512]{1,0:T(8,128)(2,1)S(1)}, bf16[256,512]{1,0:T(8,128)(2,1)S(1)}, u32[]{:S(2)}, u32[]{:S(2)}) collective-permute-start(bf16[256,512]{1,0:T(8,128)(2,1)S(1)} %collective-permute-done.refs_2_.refs_6_), channel_id=1, source_target_pairs={{0,2},{1,3},{2,0},{3,1},{4,6},{5,7},{6,4},{7,5},{8,10},{9,11},{10,... | collective-permute-start | bytes 786440 | tf_op jit(solution)/shard_map/ppermute | solution.py:316
  20.1 8.3 %collective-permute-start.6 = (bf16[256,512]{1,0:T(8,128)(2,1)S(1)}, bf16[256,512]{1,0:T(8,128)(2,1)S(1)}, u32[]{:S(2)}, u32[]{:S(2)}) collective-permute-start(bf16[256,512]{1,0:T(8,128)(2,1)S(1)} %collective-permute-done.refs_2_.refs_6_), channel_id=1, source_target_pairs={{0,4},{1,5},{2,6},{3,7},{4,0},{5,1},{6,2},{7,3},{8,12},{9,13},{10,... | collective-permute-start | bytes 786440 | tf_op jit(solution)/shard_map/ppermute | solution.py:316
  21.2 12.0 %collective-permute-start.8 = (bf16[256,512]{1,0:T(8,128)(2,1)S(1)}, bf16[256,512]{1,0:T(8,128)(2,1)S(1)}, u32[]{:S(2)}, u32[]{:S(2)}) collective-permute-start(bf16[256,512]{1,0:T(8,128)(2,1)S(1)} %collective-permute-done.3.refs_3_.refs_5_), channel_id=1, source_target_pairs={{0,2},{1,3},{2,0},{3,1},{4,6},{5,7},{6,4},{7,5},{8,10},{9,11},{10,... | collective-permute-start | bytes 786440 | tf_op jit(solution)/shard_map/ppermute | solution.py:316
  27.8 6.4 %collective-permute-start.9 = (bf16[256,512]{1,0:T(8,128)(2,1)S(1)}, bf16[256,512]{1,0:T(8,128)(2,1)S(1)}, u32[]{:S(2)}, u32[]{:S(2)}) collective-permute-start(bf16[256,512]{1,0:T(8,128)(2,1)S(1)} %collective-permute-done.5.refs_0_.refs_4_), channel_id=1, source_target_pairs={{0,4},{1,5},{2,6},{3,7},{4,0},{5,1},{6,2},{7,3},{8,12},{9,13},{10,... | collective-permute-start | bytes 786440 | tf_op jit(solution)/shard_map/ppermute | solution.py:316
  28.4 8.2 %collective-permute-start.4 = (bf16[256,512]{1,0:T(8,128)(2,1)S(1)}, bf16[256,512]{1,0:T(8,128)(2,1)}, u32[]{:S(2)}, u32[]{:S(2)}) collective-permute-start(bf16[256,512]{1,0:T(8,128)(2,1)S(1)} %get-tuple-element.40), channel_id=1, source_target_pairs={{0,1},{1,0},{2,3},{3,2},{4,5},{5,4},{6,7},{7,6},{8,9},{9,8},{10,11... | collective-permute-start | bytes 786440 | tf_op jit(solution)/shard_map/ppermute | solution.py:316
  28.4 7.4 %collective-permute-start.10 = (bf16[256,256]{1,0:T(8,128)(2,1)S(1)}, bf16[256,256]{1,0:T(8,128)(2,1)S(1)}, u32[]{:S(2)}, u32[]{:S(2)}) collective-permute-start(bf16[256,256]{1,0:T(8,128)(2,1)S(1)} %pad_maximum_fusion.3.refs_7_.noncore), channel_id=1, source_target_pairs={{0,2},{1,3},{2,0},{3,1},{4,6},{5,7},{6,4},{7,5},{8,10},{9,11},{10,... | collective-permute-start | bytes 393224 | tf_op jit(solution)/shard_map/ppermute | solution.py:316
  32.9 10.7 %collective-permute-start.7 = (bf16[256,1024]{1,0:T(8,128)(2,1)S(1)}, bf16[256,1024]{1,0:T(8,128)(2,1)S(1)}, u32[]{:S(2)}, u32[]{:S(2)}) collective-permute-start(bf16[256,1024]{1,0:T(8,128)(2,1)S(1)} %get-tuple-element.46), channel_id=1, source_target_pairs={{0,1},{1,0},{2,3},{3,2},{4,5},{5,4},{6,7},{7,6},{8,9},{9,8},{10,11... | collective-permute-start | bytes 1572872 | tf_op jit(solution)/shard_map/ppermute | solution.py:316
  35.9 7.6 %collective-permute-start.14 = (bf16[512,256]{1,0:T(8,128)(2,1)S(1)}, bf16[512,256]{1,0:T(8,128)(2,1)S(1)}, u32[]{:S(2)}, u32[]{:S(2)}) collective-permute-start(bf16[512,256]{1,0:T(8,128)(2,1)S(1)} %pad_maximum_fusion.2), channel_id=1, source_target_pairs={{0,4},{1,5},{2,6},{3,7},{4,0},{5,1},{6,2},{7,3},{8,12},{9,13},{10,... | collective-permute-start | bytes 786440 | tf_op jit(solution)/shard_map/ppermute | solution.py:316
  37.6 6.2 %collective-permute-start.11 = (bf16[256,512]{1,0:T(8,128)(2,1)S(1)}, bf16[256,512]{1,0:T(8,128)(2,1)S(1)}, u32[]{:S(2)}, u32[]{:S(2)}) collective-permute-start(bf16[256,512]{1,0:T(8,128)(2,1)S(1)} %get-tuple-element.53), channel_id=1, source_target_pairs={{0,1},{1,0},{2,3},{3,2},{4,5},{5,4},{6,7},{7,6},{8,9},{9,8},{10,11... | collective-permute-start | bytes 786440 | tf_op jit(solution)/shard_map/ppermute | solution.py:316
  37.7 8.7 %collective-permute-start.12 = (bf16[256,512]{1,0:T(8,128)(2,1)S(1)}, bf16[256,512]{1,0:T(8,128)(2,1)S(1)}, u32[]{:S(2)}, u32[]{:S(2)}) collective-permute-start(bf16[256,512]{1,0:T(8,128)(2,1)S(1)} %get-tuple-element.54), channel_id=1, source_target_pairs={{0,16},{1,17},{2,18},{3,19},{4,20},{5,21},{6,22},{7,23},{8,24},{9,... | collective-permute-start | bytes 786440 | tf_op jit(solution)/shard_map/ppermute | solution.py:316
  43.5 13.4 %collective-permute-start.15 = (bf16[1024,256]{1,0:T(8,128)(2,1)S(1)}, bf16[1024,256]{1,0:T(8,128)(2,1)S(1)}, u32[]{:S(2)}, u32[]{:S(2)}) collective-permute-start(bf16[1024,256]{1,0:T(8,128)(2,1)S(1)} %constant_dynamic-update-slice_fusion.kept), channel_id=1, source_target_pairs={{0,1},{1,0},{2,3},{3,2},{4,5},{5,4},{6,7},{7,6},{8,9},{9,8},{10,11... | collective-permute-start | bytes 1572872 | tf_op jit(solution)/shard_map/ppermute | solution.py:316
  46.4 21.0 %collective-permute-start.13 = (bf16[128,2048]{1,0:T(8,128)(2,1)S(1)}, bf16[128,2048]{1,0:T(8,128)(2,1)S(1)}, u32[]{:S(2)}, u32[]{:S(2)}) collective-permute-start(bf16[128,2048]{1,0:T(8,128)(2,1)S(1)} %pad_maximum_fusion.1), channel_id=1, source_target_pairs={{0,16},{1,17},{2,18},{3,19},{4,20},{5,21},{6,22},{7,23},{8,24},{9,... | collective-permute-start | bytes 1572872 | tf_op jit(solution)/shard_map/ppermute | solution.py:316
  48.0 8.8 %collective-permute-start.16 = (bf16[256,512]{1,0:T(8,128)(2,1)S(1)}, bf16[256,512]{1,0:T(8,128)(2,1)S(1)}, u32[]{:S(2)}, u32[]{:S(2)}) collective-permute-start(bf16[256,512]{1,0:T(8,128)(2,1)S(1)} %add_convert_fusion.mine), channel_id=1, source_target_pairs={{0,8},{1,0},{2,10},{3,2},{4,12},{5,4},{6,14},{7,6},{8,9},{9,1},{10... | collective-permute-start | bytes 786440 | tf_op jit(solution)/shard_map/ppermute | solution.py:316
  51.5 5.4 %collective-permute-start.17 = (bf16[256,512]{1,0:T(8,128)(2,1)S(1)}, bf16[256,512]{1,0:T(8,128)(2,1)S(1)}, u32[]{:S(2)}, u32[]{:S(2)}) collective-permute-start(bf16[256,512]{1,0:T(8,128)(2,1)S(1)} %add_convert_fusion.mine), channel_id=1, source_target_pairs={{1,8},{3,10},{5,12},{7,14},{8,1},{10,3},{12,5},{14,7},{17,24},{19,... | collective-permute-start | bytes 786440 | tf_op jit(solution)/shard_map/ppermute | solution.py:316
  57.6 10.0 %collective-permute-start.18 = (bf16[128,512]{1,0:T(8,128)(2,1)S(1)}, bf16[128,512]{1,0:T(8,128)(2,1)S(1)}, u32[]{:S(2)}, u32[]{:S(2)}) collective-permute-start(bf16[128,512]{1,0:T(8,128)(2,1)S(1)} %get-tuple-element.59), channel_id=1, source_target_pairs={{0,16},{1,17},{2,18},{3,19},{4,20},{5,21},{6,22},{7,23},{8,24},{9,... | collective-permute-start | bytes 393224 | tf_op jit(solution)/shard_map/ppermute | solution.py:316
  58.2 12.2 %collective-permute-start.19 = (bf16[128,512]{1,0:T(8,128)(2,1)S(1)}, bf16[128,512]{1,0:T(8,128)(2,1)S(1)}, u32[]{:S(2)}, u32[]{:S(2)}) collective-permute-start(bf16[128,512]{1,0:T(8,128)(2,1)S(1)} %get-tuple-element.60), channel_id=1, source_target_pairs={{0,2},{1,3},{2,0},{3,1},{4,6},{5,7},{6,4},{7,5},{8,10},{9,11},{10,... | collective-permute-start | bytes 393224 | tf_op jit(solution)/shard_map/ppermute | solution.py:316
  59.8 12.4 %collective-permute-start.20 = (bf16[128,512]{1,0:T(8,128)(2,1)S(1)}, bf16[128,512]{1,0:T(8,128)(2,1)S(1)}, u32[]{:S(2)}, u32[]{:S(2)}) collective-permute-start(bf16[128,512]{1,0:T(8,128)(2,1)S(1)} %get-tuple-element.61), channel_id=1, source_target_pairs={{0,18},{1,19},{2,16},{3,17},{4,22},{5,23},{6,20},{7,21},{8,26},{9,... | collective-permute-start | bytes 393224 | tf_op jit(solution)/shard_map/ppermute | solution.py:316
  61.3 10.8 %collective-permute-start.21 = (bf16[128,512]{1,0:T(8,128)(2,1)S(1)}, bf16[128,512]{1,0:T(8,128)(2,1)S(1)}, u32[]{:S(2)}, u32[]{:S(2)}) collective-permute-start(bf16[128,512]{1,0:T(8,128)(2,1)S(1)} %get-tuple-element.62), channel_id=1, source_target_pairs={{0,4},{1,5},{2,6},{3,7},{4,0},{5,1},{6,2},{7,3},{8,12},{9,13},{10,... | collective-permute-start | bytes 393224 | tf_op jit(solution)/shard_map/ppermute | solution.py:316
  67.4 7.3 %collective-permute-start.22 = (bf16[128,512]{1,0:T(8,128)(2,1)S(1)}, bf16[128,512]{1,0:T(8,128)(2,1)S(1)}, u32[]{:S(2)}, u32[]{:S(2)}) collective-permute-start(bf16[128,512]{1,0:T(8,128)(2,1)S(1)} %get-tuple-element.63), channel_id=1, source_target_pairs={{0,20},{1,21},{2,22},{3,23},{4,16},{5,17},{6,18},{7,19},{8,28},{9,... | collective-permute-start | bytes 393224 | tf_op jit(solution)/shard_map/ppermute | solution.py:316
  67.6 10.2 %collective-permute-start.23 = (bf16[128,512]{1,0:T(8,128)(2,1)S(1)}, bf16[128,512]{1,0:T(8,128)(2,1)S(1)}, u32[]{:S(2)}, u32[]{:S(2)}) collective-permute-start(bf16[128,512]{1,0:T(8,128)(2,1)S(1)} %get-tuple-element.64), channel_id=1, source_target_pairs={{0,6},{1,7},{2,4},{3,5},{4,2},{5,3},{6,0},{7,1},{8,14},{9,15},{10,... | collective-permute-start | bytes 393224 | tf_op jit(solution)/shard_map/ppermute | solution.py:316
  70.4 10.3 %collective-permute-start.24 = (bf16[128,512]{1,0:T(8,128)(2,1)S(1)}, bf16[128,512]{1,0:T(8,128)(2,1)S(1)}, u32[]{:S(2)}, u32[]{:S(2)}) collective-permute-start(bf16[128,512]{1,0:T(8,128)(2,1)S(1)} %get-tuple-element.65), channel_id=1, source_target_pairs={{0,22},{1,23},{2,20},{3,21},{4,18},{5,19},{6,16},{7,17},{8,30},{9,... | collective-permute-start | bytes 393224 | tf_op jit(solution)/shard_map/ppermute | solution.py:316

commit v4 on v3

--- a/solution.py
+++ b/solution.py
@@ -204,41 +204,10 @@
     )(jnp.stack(blocks + [flag, side]).astype(jnp.int32), *operands)
 
 
-def relation_kernel(count, scale, flag, done, noncore, *refs):
-    pieces, (own, send) = refs[:2 * count], refs[2 * count:]
-    width = pieces[0].shape[1]
-    for i in range(count):
-        columns = slice(i * width, (i + 1) * width)
-        values = [
-            (matmul(noncore[...], pieces[2 * i + j][...]) * scale).astype(jnp.bfloat16)
-            for j in range(2)
-        ]
-        for j in range(2):
-            @pl.when(flag[0] == j)
-            def _(j=j):
-                own[:, columns] = values[j]
-                send[:, columns] = values[1 - j]
-
-
-def relate(noncore, pairs, flag, scale, after):
-    rows, width = noncore.shape[0], pairs[0][0].shape[1]
-    out = shape((rows, width * len(pairs)))
-    return pl.pallas_call(
-        functools.partial(relation_kernel, len(pairs), scale),
-        in_specs=[pl.BlockSpec(memory_space=pltpu.SMEM), anywhere()]
-        + [whole()] * (2 * len(pairs) + 1),
-        out_specs=(whole(), whole()),
-        out_shape=(out, out),
-        compiler_params=params(),
-        cost_estimate=SHORT,
-        name="relate",
-    )(flag.astype(jnp.int32)[None], after, noncore, *[piece for pair in pairs for piece in pair])
-
-
-def regression_kernel(count, scale, flag, kept, got, mine, one, two, *outs):
+def regression_kernel(count, scale, flag, kept, got, mine, mine_other, twin, twin_other, *outs):
     rows = outs[0].shape[0]
     for j in range(2):
-        left, right = ((mine, one), (one, two))[j]
+        left, right = ((mine, mine_other), (twin, twin_other))[j]
 
         @pl.when(flag[0] == j)
         def _(left=left, right=right):
@@ -248,17 +217,17 @@
                 outs[k][...] = (value * scale).astype(jnp.bfloat16)
 
 
-def regress(kept, got, mine, one, two, flag, count, scale):
+def regress(kept, got, mine, mine_other, twin, twin_other, flag, count, scale):
     rows, width = kept.shape[0] // count, mine.shape[1]
     return pl.pallas_call(
         functools.partial(regression_kernel, count, scale),
-        in_specs=[pl.BlockSpec(memory_space=pltpu.SMEM)] + [whole()] * 5,
+        in_specs=[pl.BlockSpec(memory_space=pltpu.SMEM)] + [whole()] * 6,
         out_specs=[whole()] * count,
         out_shape=[shape((rows, width))] * count,
         compiler_params=params(),
         cost_estimate=SHORT,
         name="regress",
-    )(flag.astype(jnp.int32)[None], kept, got, mine, one, two)
+    )(flag.astype(jnp.int32)[None], kept, got, mine, mine_other, twin, twin_other)
 
 
 def assemble_kernel(jobs, place, *refs):
@@ -343,76 +312,78 @@
             total, both, [(pieces[b], pieces[b + top]) for b in pairs], flag, grp,
             scale, final,
         )
+        head = 2 if final else 1
         if pairs:
-            related.extend(result[1:3])
-        return [result[0], *result[3 if pairs else 1:]]
+            related.extend(result[head:head + 2])
+        return [*result[:head], *result[head + 2 if pairs else head:]]
 
     low = list(range(2, top, 2))
-    for bits in [top] + low + [1]:
+    for bits in [*low, 1, top]:
         pieces[bits] = along_anim(own, bits)
-    held = [top, 1]
-    *moved, both = after(*[pieces[b] for b in held], both)
-    pieces.update(zip(held, moved))
+    pieces[top], pieces[1], both = after(pieces[top], pieces[1], both)
     for bits in low:
         pieces[top + bits] = along_anim(pieces[top], bits)
-    pieces[top + 1] = along_anim(pieces[top], 1)
     for bits in low:
         pieces[bits + 1] = along_anim(pieces[bits], 1)
+    pieces[top + 1] = along_anim(pieces[top], 1)
     (total,) = take([0, 1, top] + low, None, [0])
     pieces[top + 1], total = after(pieces[top + 1], total)
     for bits in low:
         pieces[top + bits + 1] = along_anim(pieces[top + 1], bits)
 
-    kept, pieces[top + low[-1]] = after(both, pieces[top + low[-1]])
-    beside = along_anim(kept, 1)
+    waited, pieces[top + low[-1]] = after(both, pieces[top + low[-1]])
+    beside = along_anim(waited, 1)
 
     last = [bits + i for bits in low for i in (1, top + 1)]
     total, slabs = take([top + 1] + [top + b for b in low], total, [1] + low, last)
-    keep, send = take(last, total, rows_of=slabs, final=True)
+    keep, send = take(last, total, [b + 1 for b in low], rows_of=slabs, final=True)
     from_other = across_grp(send)
 
-    related += relate(both, [(pieces[b + 1], pieces[top + b + 1]) for b in low], flag, scale, keep)
-    beside, related[-1] = after(beside, related[-1])
-    kept = jnp.concatenate([kept, beside], axis=0)
+    beside, keep = after(beside, keep)
+    kept = jnp.concatenate([both, beside], axis=0)
     bit = 2
     while bit < top:
         kept = jnp.concatenate([kept, along_anim(kept, bit)], axis=0)
         bit *= 2
+
+    mine = (keep + from_other.astype(jnp.float32)).astype(jnp.bfloat16)
+    twin = along_anim(mine, top)
+    mine_other = across_mark(mine)
+
     received = [across_mark(part) for part in related[1::2]]
     sums = [
         jnp.concatenate(
             [
-                (mine[part].astype(jnp.float32) + yours[part].astype(jnp.float32)).astype(
+                (ours[part].astype(jnp.float32) + theirs[part].astype(jnp.float32)).astype(
                     jnp.bfloat16
                 )
-                for mine, yours in zip(related[::2], received)
+                for ours, theirs in zip(related[::2], received)
             ],
             axis=1,
         )
         for part in (slice(0, rows), slice(rows, 2 * rows))
     ]
-
-    sums[1], from_other = after(sums[1], from_other)
+    sums[1], mine_other = after(sums[1], mine_other)
     swapped = across_grp(sums[1])
 
-    mine = (keep + from_other.astype(jnp.float32)).astype(jnp.bfloat16)
-    one = move(mine, lambda g, a, m: (g, a ^ top, m) if m == a // top else (g, a, 1 - m))
-    two = move(mine, lambda g, a, m: None if m == a // top else (g, a ^ top, 1 - m))
-
-    results = regress(kept, across_mark(kept), mine, one, two, flag, 2 * top, scale)
-    step = lambda k: k >> 1
-    arrived = [
-        results[k] if k == 0 else move(results[k], lambda g, a, m, k=k: (g ^ k & 1, a ^ step(k), m))
-        for k in range(2 * top)
-    ]
-    slots = [((anim ^ step(k)) % top) * 2 + (grp ^ k & 1) for k in range(2 * top)]
+    kept, mine_other = after(kept, mine_other)
+    results = regress(
+        kept, across_mark(kept), mine, mine_other, twin, across_mark(twin), flag, 2 * top, scale
+    )
+    arrived = {0: results[0]}
+    for k in range(1, 2 * top):
+        arrived[k] = move(results[k], lambda g, a, m, k=k: (g ^ k & 1, a ^ k >> 1, m))
+    arrived = [arrived[k] for k in range(2 * top)]
+    slots = [((anim ^ k >> 1) % top) * 2 + (grp ^ k & 1) for k in range(2 * top)]
     width = mine.shape[1]
 
     width_of_piece = own.shape[1]
     order = [0, 1] + low + [b + 1 for b in low]
     places = [2 * ((anim ^ b) % top) + g for g in (grp, 1 - grp) for b in order]
     return tuple(
-        assemble([([sums[0], swapped], places, width_of_piece), (arrived, slots, width)])
+        assemble(
+            [([sums[0], swapped], places, width_of_piece), (arrived, slots, width)]
+        )
     )
 
 

time: 82.9 us -> 81.8 us (0.987)
  starting transfers between devices: 36.2 us -> 29.7 us
  waiting for transfers between devices: 30.7 us -> 36.2 us
    ppermute x25 -> x26, starting transfers between devices: 36.2 us -> 29.7 us  [move(): return lax.ppermute(array, AXES, pairs)]
    ppermute x25 -> x26, waiting for transfers between devices: 30.7 us -> 36.2 us  [move(): return lax.ppermute(array, AXES, pairs)]
  transfers between devices with their start and end apart: 25 -> 26, of which waited for: 11 -> 13; matrix products, arithmetic and copies ran while one was open for 2% -> 2% of each run, Pallas kernels for 11% -> 11%
where the time goes in v4:
time: 81.8 us; the launch traced here: 81.6 us
  waiting for transfers between devices  36.2 us (44%)
  starting transfers between devices  29.7 us (36%)
  Pallas kernels  13.1 us (16%)
  other arithmetic  1.57 us (2%)
    ppermute x26, waiting for transfers between devices, move(): return lax.ppermute(array, AXES, pairs)  36.2 us
    ppermute x26, starting transfers between devices, move(): return lax.ppermute(array, AXES, pairs)  29.7 us
    pallas_call x3, Pallas kernels, absorb(): pl.pallas_call(functools.partial(absorb_kernel, count, len(pairs), ahead,...  8.61 us
    pallas_call x1, Pallas kernels, assemble(): pl.pallas_call(functools.partial(assemble_kernel, [(len(job[0]), job[2])...  1.98 us
    pallas_call x1, Pallas kernels, centre(): pl.pallas_call(centre_kernel, in_specs=[pl.BlockSpec(memory_space=pltpu.S...  1.75 us
  transfers between devices with their start and end apart: 26, of which 13 were waited for; matrix products, arithmetic and copies ran while one was open for 2% of the time, Pallas kernels for 11%

profile of v4, /device:TPU:0, one launch (start us, length us, event | category | flops | bytes accessed | tf_op | source)
XLA Modules:
  0.0 81.6 jit_solution(6513036331272142653)
XLA Ops:
  0.6 1.8 %centre.1 = (bf16[256,512]{1,0:T(8,128)(2,1)S(1)}, bf16[128,256]{1,0:T(8,128)(2,1)S(1)}) custom-call(s32[1]{0:T(128)} %bitcast.17.place, s32[1024,256]{1,0:T(8,128)} %geno.1, s32[5,1024]{1,0:T(8,128)} %codes.1, f32[5,256]{1,0:T(8,128)} %freqs.1, s32[128,256]{1,0:T(8,128)} %noncore_geno.1, s32[5,128]{1,0:T(8,128)} %noncore_codes.1), custom_call_target="tpu_custom_call" | custom-call | tf_op jit(solution)/shard_map/centre/pallas_call | solution.py:103
  2.4 4.1 %collective-permute-start = (bf16[256,512]{1,0:T(8,128)(2,1)S(1)}, bf16[256,512]{1,0:T(8,128)(2,1)S(1)}, u32[]{:S(2)}, u32[]{:S(2)}) collective-permute-start(bf16[256,512]{1,0:T(8,128)(2,1)S(1)} %get-tuple-element.36.refs_0_.refs_5_), channel_id=1, source_target_pairs={{0,8},{1,9},{2,10},{3,11},{4,12},{5,13},{6,14},{7,15},{8,0},{9,1},... | collective-permute-start | bytes 786440 | tf_op jit(solution)/shard_map/ppermute | solution.py:285
  6.5 1.5 %collective-permute-start.1 = (bf16[256,512]{1,0:T(8,128)(2,1)S(1)}, bf16[256,512]{1,0:T(8,128)(2,1)S(1)}, u32[]{:S(2)}, u32[]{:S(2)}) collective-permute-start(bf16[256,512]{1,0:T(8,128)(2,1)S(1)} %get-tuple-element.36.refs_0_.refs_5_), channel_id=1, source_target_pairs={{0,2},{1,3},{2,0},{3,1},{4,6},{5,7},{6,4},{7,5},{8,10},{9,11},{10,... | collective-permute-start | bytes 786440 | tf_op jit(solution)/shard_map/ppermute | solution.py:285
  8.0 1.5 %collective-permute-start.2 = (bf16[128,256]{1,0:T(8,128)(2,1)S(1)}, bf16[128,256]{1,0:T(8,128)(2,1)S(1)}, u32[]{:S(2)}, u32[]{:S(2)}) collective-permute-start(bf16[128,256]{1,0:T(8,128)(2,1)S(1)} %get-tuple-element.37), channel_id=1, source_target_pairs={{0,16},{1,17},{2,18},{3,19},{4,20},{5,21},{6,22},{7,23},{8,24},{9,... | collective-permute-start | bytes 196616 | tf_op jit(solution)/shard_map/ppermute | solution.py:285
  9.5 1.6 %collective-permute-start.3 = (bf16[256,512]{1,0:T(8,128)(2,1)S(1)}, bf16[256,512]{1,0:T(8,128)(2,1)S(1)}, u32[]{:S(2)}, u32[]{:S(2)}) collective-permute-start(bf16[256,512]{1,0:T(8,128)(2,1)S(1)} %get-tuple-element.36.refs_0_.refs_5_), channel_id=1, source_target_pairs={{0,4},{1,5},{2,6},{3,7},{4,0},{5,1},{6,2},{7,3},{8,12},{9,13},{10,... | collective-permute-start | bytes 786440 | tf_op jit(solution)/shard_map/ppermute | solution.py:285
  11.1 1.2 %collective-permute-done.2 = bf16[128,256]{1,0:T(8,128)(2,1)S(1)} collective-permute-done((bf16[128,256]{1,0:T(8,128)(2,1)S(1)}, bf16[128,256]{1,0:T(8,128)(2,1)S(1)}, u32[]{:S(2)}, u32[]{:S(2)}) %collective-permute-start.2) | collective-permute-done | bytes 65568 | tf_op jit(solution)/shard_map/ppermute | solution.py:285
  12.3 6.3 %collective-permute-done.refs_2_.refs_6_ = bf16[256,512]{1,0:T(8,128)(2,1)S(1)} collective-permute-done((bf16[256,512]{1,0:T(8,128)(2,1)S(1)}, bf16[256,512]{1,0:T(8,128)(2,1)S(1)}, u32[]{:S(2)}, u32[]{:S(2)}) %collective-permute-start) | collective-permute-done | bytes 262176 | tf_op jit(solution)/shard_map/ppermute | solution.py:285
  18.5 1.5 %collective-permute-start.5 = (bf16[256,512]{1,0:T(8,128)(2,1)S(1)}, bf16[256,512]{1,0:T(8,128)(2,1)S(1)}, u32[]{:S(2)}, u32[]{:S(2)}) collective-permute-start(bf16[256,512]{1,0:T(8,128)(2,1)S(1)} %collective-permute-done.refs_2_.refs_6_), channel_id=1, source_target_pairs={{0,2},{1,3},{2,0},{3,1},{4,6},{5,7},{6,4},{7,5},{8,10},{9,11},{10,... | collective-permute-start | bytes 786440 | tf_op jit(solution)/shard_map/ppermute | solution.py:285
  21.8 4.1 %absorb.3 = (f32[256,1024]{1,0:T(8,128)S(1)}, bf16[256,512]{1,0:T(8,128)(2,1)S(1)}, bf16[256,512]{1,0:T(8,128)(2,1)S(1)}) custom-call(s32[6]{0:T(128)S(1)} %stack.107.place, bf16[256,512]{1,0:T(8,128)(2,1)S(1)} %get-tuple-element.36.refs_0_.refs_5_, bf16[256,512]{1,0:T(8,128)(2,1)S(1)} %collective-permute-done.1.refs_1_.refs_3_, ...), custom_call_target="tpu_custom_call" | custom-call | tf_op jit(solution)/shard_map/absorb/pallas_call | solution.py:192
  25.8 1.9 %collective-permute-done.5.refs_0_.refs_4_ = bf16[256,512]{1,0:T(8,128)(2,1)S(1)} collective-permute-done((bf16[256,512]{1,0:T(8,128)(2,1)S(1)}, bf16[256,512]{1,0:T(8,128)(2,1)S(1)}, u32[]{:S(2)}, u32[]{:S(2)}) %collective-permute-start.5) | collective-permute-done | bytes 262176 | tf_op jit(solution)/shard_map/ppermute | solution.py:285
  28.5 1.5 %collective-permute-start.11 = (bf16[256,256]{1,0:T(8,128)(2,1)S(1)}, bf16[256,256]{1,0:T(8,128)(2,1)S(1)}, u32[]{:S(2)}, u32[]{:S(2)}) collective-permute-start(bf16[256,256]{1,0:T(8,128)(2,1)S(1)} %pad_maximum_fusion.4.refs_7_.refs_5_), channel_id=1, source_target_pairs={{0,2},{1,3},{2,0},{3,1},{4,6},{5,7},{6,4},{7,5},{8,10},{9,11},{10,... | collective-permute-start | bytes 393224 | tf_op jit(solution)/shard_map/ppermute | solution.py:285
  30.0 2.9 %absorb.4 = (f32[256,1024]{1,0:T(8,128)S(1)}, bf16[256,1024]{1,0:T(8,128)(2,1)S(1)}, bf16[256,1024]{1,0:T(8,128)(2,1)S(1)}, bf16[2,512,1024]{2,1,0:T(8,128)(2,1)S(1)}) custom-call(s32[6]{0:T(128)S(1)} %stack.112.place, bf16[256,512]{1,0:T(8,128)(2,1)S(1)} %collective-permute-done.5.refs_0_.refs_4_, ...), custom_call_target="tpu_custom_call" | custom-call | tf_op jit(solution)/shard_map/absorb/pallas_call | solution.py:192
  33.2 0.9 %collective-permute-done.9.refs_1_.refs_4_ = bf16[256,512]{1,0:T(8,128)(2,1)S(1)} collective-permute-done((bf16[256,512]{1,0:T(8,128)(2,1)S(1)}, bf16[256,512]{1,0:T(8,128)(2,1)S(1)}, u32[]{:S(2)}, u32[]{:S(2)}) %collective-permute-start.9) | collective-permute-done | bytes 262176 | tf_op jit(solution)/shard_map/ppermute | solution.py:285
  34.2 1.6 %absorb.5 = (f32[256,512]{1,0:T(8,128)S(1)}, bf16[256,512]{1,0:T(8,128)(2,1)S(1)}, bf16[256,512]{1,0:T(8,128)(2,1)S(1)}, bf16[256,512]{1,0:T(8,128)(2,1)S(1)}) custom-call(s32[4]{0:T(128)S(1)} %pad_add_fusion.place, bf16[256,512]{1,0:T(8,128)(2,1)S(1)} %collective-permute-done.8.refs_0_.refs_3_, bf16[256,512]{1,0:T(8,128)(2,1)S(1)} %collective-permute-done.9.refs_1_.refs_4_, ...), custom_call_target="tpu_custom_call" | custom-call | tf_op jit(solution)/shard_map/absorb/pallas_call | solution.py:192
  35.8 1.6 %collective-permute-start.12 = (bf16[256,512]{1,0:T(8,128)(2,1)S(1)}, bf16[256,512]{1,0:T(8,128)(2,1)S(1)}, u32[]{:S(2)}, u32[]{:S(2)}) collective-permute-start(bf16[256,512]{1,0:T(8,128)(2,1)S(1)} %get-tuple-element.56), channel_id=1, source_target_pairs={{0,16},{1,17},{2,18},{3,19},{4,20},{5,21},{6,22},{7,23},{8,24},{9,... | collective-permute-start | bytes 786440 | tf_op jit(solution)/shard_map/ppermute | solution.py:285
  37.4 1.0 %add_convert_fusion.4 = (bf16[128,512]{1,0:T(8,128)(2,1)S(1)}, bf16[128,512]{1,0:T(8,128)(2,1)S(1)}) fusion(bf16[256,512]{1,0:T(8,128)(2,1)} %collective-permute-done.4, bf16[256,512]{1,0:T(8,128)(2,1)S(1)} %get-tuple-element.41), kind=kLoop, calls=%fused_computation.8 | loop fusion | flops 524288 | bytes 786432 | tf_op jit(solution)/shard_map/convert_element_type | solution.py:357
  39.3 4.2 %collective-permute-done.12 = bf16[256,512]{1,0:T(8,128)(2,1)S(1)} collective-permute-done((bf16[256,512]{1,0:T(8,128)(2,1)S(1)}, bf16[256,512]{1,0:T(8,128)(2,1)S(1)}, u32[]{:S(2)}, u32[]{:S(2)}) %collective-permute-start.12) | collective-permute-done | bytes 262176 | tf_op jit(solution)/shard_map/ppermute | solution.py:285
  43.6 3.5 %collective-permute-start.17 = (bf16[256,512]{1,0:T(8,128)(2,1)S(1)}, bf16[256,512]{1,0:T(8,128)(2,1)S(1)}, u32[]{:S(2)}, u32[]{:S(2)}) collective-permute-start(bf16[256,512]{1,0:T(8,128)(2,1)S(1)} %add_convert_fusion.mine), channel_id=1, source_target_pairs={{0,8},{1,9},{2,10},{3,11},{4,12},{5,13},{6,14},{7,15},{8,0},{9,1},... | collective-permute-start | bytes 786440 | tf_op jit(solution)/shard_map/ppermute | solution.py:285
  47.7 1.4 %collective-permute-start.14 = (bf16[128,2048]{1,0:T(8,128)(2,1)S(1)}, bf16[128,2048]{1,0:T(8,128)(2,1)S(1)}, u32[]{:S(2)}, u32[]{:S(2)}) collective-permute-start(bf16[128,2048]{1,0:T(8,128)(2,1)S(1)} %pad_maximum_fusion.1), channel_id=1, source_target_pairs={{0,16},{1,17},{2,18},{3,19},{4,20},{5,21},{6,22},{7,23},{8,24},{9,... | collective-permute-start | bytes 1572872 | tf_op jit(solution)/shard_map/ppermute | solution.py:285
  49.1 10.5 %collective-permute-done.17.twin = bf16[256,512]{1,0:T(8,128)(2,1)S(1)} collective-permute-done((bf16[256,512]{1,0:T(8,128)(2,1)S(1)}, bf16[256,512]{1,0:T(8,128)(2,1)S(1)}, u32[]{:S(2)}, u32[]{:S(2)}) %collective-permute-start.17) | collective-permute-done | bytes 262176 | tf_op jit(solution)/shard_map/ppermute | solution.py:285
  59.6 1.5 %collective-permute-done.18.twin_other = bf16[256,512]{1,0:T(8,128)(2,1)S(1)} collective-permute-done((bf16[256,512]{1,0:T(8,128)(2,1)S(1)}, bf16[256,512]{1,0:T(8,128)(2,1)S(1)}, u32[]{:S(2)}, u32[]{:S(2)}) %collective-permute-start.18) | collective-permute-done | bytes 262176 | tf_op jit(solution)/shard_map/ppermute | solution.py:285
  61.2 0.7 regress.1
  61.9 1.4 %collective-permute-start.19 = (bf16[128,512]{1,0:T(8,128)(2,1)S(1)}, bf16[128,512]{1,0:T(8,128)(2,1)S(1)}, u32[]{:S(2)}, u32[]{:S(2)}) collective-permute-start(bf16[128,512]{1,0:T(8,128)(2,1)S(1)} %get-tuple-element.63), channel_id=1, source_target_pairs={{0,16},{1,17},{2,18},{3,19},{4,20},{5,21},{6,22},{7,23},{8,24},{9,... | collective-permute-start | bytes 393224 | tf_op jit(solution)/shard_map/ppermute | solution.py:285
  64.1 1.5 %collective-permute-start.21 = (bf16[128,512]{1,0:T(8,128)(2,1)S(1)}, bf16[128,512]{1,0:T(8,128)(2,1)S(1)}, u32[]{:S(2)}, u32[]{:S(2)}) collective-permute-start(bf16[128,512]{1,0:T(8,128)(2,1)S(1)} %get-tuple-element.65), channel_id=1, source_target_pairs={{0,18},{1,19},{2,16},{3,17},{4,22},{5,23},{6,20},{7,21},{8,26},{9,... | collective-permute-start | bytes 393224 | tf_op jit(solution)/shard_map/ppermute | solution.py:285
  65.6 2.8 %collective-permute-start.23 = (bf16[128,512]{1,0:T(8,128)(2,1)S(1)}, bf16[128,512]{1,0:T(8,128)(2,1)S(1)}, u32[]{:S(2)}, u32[]{:S(2)}) collective-permute-start(bf16[128,512]{1,0:T(8,128)(2,1)S(1)} %get-tuple-element.67), channel_id=1, source_target_pairs={{0,20},{1,21},{2,22},{3,23},{4,16},{5,17},{6,18},{7,19},{8,28},{9,... | collective-permute-start | bytes 393224 | tf_op jit(solution)/shard_map/ppermute | solution.py:285
  68.6 1.2 %collective-permute-done.20.refs_4_ = bf16[128,512]{1,0:T(8,128)(2,1)S(1)} collective-permute-done((bf16[128,512]{1,0:T(8,128)(2,1)S(1)}, bf16[128,512]{1,0:T(8,128)(2,1)S(1)}, u32[]{:S(2)}, u32[]{:S(2)}) %collective-permute-start.20) | collective-permute-done | bytes 131104 | tf_op jit(solution)/shard_map/ppermute | solution.py:285
  69.7 1.7 %collective-permute-start.25 = (bf16[128,512]{1,0:T(8,128)(2,1)S(1)}, bf16[128,512]{1,0:T(8,128)(2,1)S(1)}, u32[]{:S(2)}, u32[]{:S(2)}) collective-permute-start(bf16[128,512]{1,0:T(8,128)(2,1)S(1)} %get-tuple-element.69), channel_id=1, source_target_pairs={{0,22},{1,23},{2,20},{3,21},{4,18},{5,19},{6,16},{7,17},{8,30},{9,... | collective-permute-start | bytes 393224 | tf_op jit(solution)/shard_map/ppermute | solution.py:285
  71.5 1.2 %collective-permute-done.21.refs_5_ = bf16[128,512]{1,0:T(8,128)(2,1)S(1)} collective-permute-done((bf16[128,512]{1,0:T(8,128)(2,1)S(1)}, bf16[128,512]{1,0:T(8,128)(2,1)S(1)}, u32[]{:S(2)}, u32[]{:S(2)}) %collective-permute-start.21) | collective-permute-done | bytes 131104 | tf_op jit(solution)/shard_map/ppermute | solution.py:285
  72.7 2.9 %collective-permute-done.23.refs_7_ = bf16[128,512]{1,0:T(8,128)(2,1)S(1)} collective-permute-done((bf16[128,512]{1,0:T(8,128)(2,1)S(1)}, bf16[128,512]{1,0:T(8,128)(2,1)S(1)}, u32[]{:S(2)}, u32[]{:S(2)}) %collective-permute-start.23) | collective-permute-done | bytes 131104 | tf_op jit(solution)/shard_map/ppermute | solution.py:285
  75.7 1.6 %collective-permute-done.24.refs_8_ = bf16[128,512]{1,0:T(8,128)(2,1)S(1)} collective-permute-done((bf16[128,512]{1,0:T(8,128)(2,1)S(1)}, bf16[128,512]{1,0:T(8,128)(2,1)S(1)}, u32[]{:S(2)}, u32[]{:S(2)}) %collective-permute-start.24) | collective-permute-done | bytes 131104 | tf_op jit(solution)/shard_map/ppermute | solution.py:285
  77.3 2.4 %collective-permute-done.25.refs_9_ = bf16[128,512]{1,0:T(8,128)(2,1)S(1)} collective-permute-done((bf16[128,512]{1,0:T(8,128)(2,1)S(1)}, bf16[128,512]{1,0:T(8,128)(2,1)S(1)}, u32[]{:S(2)}, u32[]{:S(2)}) %collective-permute-start.25) | collective-permute-done | bytes 131104 | tf_op jit(solution)/shard_map/ppermute | solution.py:285
  79.7 2.0 %assemble.1 = (bf16[128,4096]{1,0:T(8,128)(2,1)}, bf16[128,4096]{1,0:T(8,128)(2,1)}) custom-call(s32[16]{0:T(128)S(1)} %stack.100.place, bf16[128,2048]{1,0:T(8,128)(2,1)S(1)} %pad_maximum_fusion.refs_0_, bf16[128,2048]{1,0:T(8,128)(2,1)S(1)} %collective-permute-done.14.refs_1_, bf16[128,512]{1,0:T(8,128)(2,1)S(1)} %get-tuple-element.62.refs_2_, ...), custom_call_target="tpu_custom_call" | custom-call | tf_op jit(solution)/shard_map/assemble/pallas_call | solution.py:256
  (39 shorter events, 5.1 us)
Async XLA Ops:
  2.4 16.1 %collective-permute-start = (bf16[256,512]{1,0:T(8,128)(2,1)S(1)}, bf16[256,512]{1,0:T(8,128)(2,1)S(1)}, u32[]{:S(2)}, u32[]{:S(2)}) collective-permute-start(bf16[256,512]{1,0:T(8,128)(2,1)S(1)} %get-tuple-element.36.refs_0_.refs_5_), channel_id=1, source_target_pairs={{0,8},{1,9},{2,10},{3,11},{4,12},{5,13},{6,14},{7,15},{8,0},{9,1},... | collective-permute-start | bytes 786440 | tf_op jit(solution)/shard_map/ppermute | solution.py:285
  6.5 12.0 %collective-permute-start.1 = (bf16[256,512]{1,0:T(8,128)(2,1)S(1)}, bf16[256,512]{1,0:T(8,128)(2,1)S(1)}, u32[]{:S(2)}, u32[]{:S(2)}) collective-permute-start(bf16[256,512]{1,0:T(8,128)(2,1)S(1)} %get-tuple-element.36.refs_0_.refs_5_), channel_id=1, source_target_pairs={{0,2},{1,3},{2,0},{3,1},{4,6},{5,7},{6,4},{7,5},{8,10},{9,11},{10,... | collective-permute-start | bytes 786440 | tf_op jit(solution)/shard_map/ppermute | solution.py:285
  8.0 4.3 %collective-permute-start.2 = (bf16[128,256]{1,0:T(8,128)(2,1)S(1)}, bf16[128,256]{1,0:T(8,128)(2,1)S(1)}, u32[]{:S(2)}, u32[]{:S(2)}) collective-permute-start(bf16[128,256]{1,0:T(8,128)(2,1)S(1)} %get-tuple-element.37), channel_id=1, source_target_pairs={{0,16},{1,17},{2,18},{3,19},{4,20},{5,21},{6,22},{7,23},{8,24},{9,... | collective-permute-start | bytes 196616 | tf_op jit(solution)/shard_map/ppermute | solution.py:285
  9.5 11.7 %collective-permute-start.3 = (bf16[256,512]{1,0:T(8,128)(2,1)S(1)}, bf16[256,512]{1,0:T(8,128)(2,1)S(1)}, u32[]{:S(2)}, u32[]{:S(2)}) collective-permute-start(bf16[256,512]{1,0:T(8,128)(2,1)S(1)} %get-tuple-element.36.refs_0_.refs_5_), channel_id=1, source_target_pairs={{0,4},{1,5},{2,6},{3,7},{4,0},{5,1},{6,2},{7,3},{8,12},{9,13},{10,... | collective-permute-start | bytes 786440 | tf_op jit(solution)/shard_map/ppermute | solution.py:285
  18.5 9.2 %collective-permute-start.5 = (bf16[256,512]{1,0:T(8,128)(2,1)S(1)}, bf16[256,512]{1,0:T(8,128)(2,1)S(1)}, u32[]{:S(2)}, u32[]{:S(2)}) collective-permute-start(bf16[256,512]{1,0:T(8,128)(2,1)S(1)} %collective-permute-done.refs_2_.refs_6_), channel_id=1, source_target_pairs={{0,2},{1,3},{2,0},{3,1},{4,6},{5,7},{6,4},{7,5},{8,10},{9,11},{10,... | collective-permute-start | bytes 786440 | tf_op jit(solution)/shard_map/ppermute | solution.py:285
  20.2 8.4 %collective-permute-start.6 = (bf16[256,512]{1,0:T(8,128)(2,1)S(1)}, bf16[256,512]{1,0:T(8,128)(2,1)S(1)}, u32[]{:S(2)}, u32[]{:S(2)}) collective-permute-start(bf16[256,512]{1,0:T(8,128)(2,1)S(1)} %collective-permute-done.refs_2_.refs_6_), channel_id=1, source_target_pairs={{0,4},{1,5},{2,6},{3,7},{4,0},{5,1},{6,2},{7,3},{8,12},{9,13},{10,... | collective-permute-start | bytes 786440 | tf_op jit(solution)/shard_map/ppermute | solution.py:285
  21.2 12.1 %collective-permute-start.8 = (bf16[256,512]{1,0:T(8,128)(2,1)S(1)}, bf16[256,512]{1,0:T(8,128)(2,1)S(1)}, u32[]{:S(2)}, u32[]{:S(2)}) collective-permute-start(bf16[256,512]{1,0:T(8,128)(2,1)S(1)} %collective-permute-done.3.refs_3_.refs_5_), channel_id=1, source_target_pairs={{0,2},{1,3},{2,0},{3,1},{4,6},{5,7},{6,4},{7,5},{8,10},{9,11},{10,... | collective-permute-start | bytes 786440 | tf_op jit(solution)/shard_map/ppermute | solution.py:285
  27.8 6.4 %collective-permute-start.9 = (bf16[256,512]{1,0:T(8,128)(2,1)S(1)}, bf16[256,512]{1,0:T(8,128)(2,1)S(1)}, u32[]{:S(2)}, u32[]{:S(2)}) collective-permute-start(bf16[256,512]{1,0:T(8,128)(2,1)S(1)} %collective-permute-done.5.refs_0_.refs_4_), channel_id=1, source_target_pairs={{0,4},{1,5},{2,6},{3,7},{4,0},{5,1},{6,2},{7,3},{8,12},{9,13},{10,... | collective-permute-start | bytes 786440 | tf_op jit(solution)/shard_map/ppermute | solution.py:285
  28.4 9.1 %collective-permute-start.4 = (bf16[256,512]{1,0:T(8,128)(2,1)S(1)}, bf16[256,512]{1,0:T(8,128)(2,1)}, u32[]{:S(2)}, u32[]{:S(2)}) collective-permute-start(bf16[256,512]{1,0:T(8,128)(2,1)S(1)} %get-tuple-element.42), channel_id=1, source_target_pairs={{0,1},{1,0},{2,3},{3,2},{4,5},{5,4},{6,7},{7,6},{8,9},{9,8},{10,11... | collective-permute-start | bytes 786440 | tf_op jit(solution)/shard_map/ppermute | solution.py:285
  28.5 9.9 %collective-permute-start.11 = (bf16[256,256]{1,0:T(8,128)(2,1)S(1)}, bf16[256,256]{1,0:T(8,128)(2,1)S(1)}, u32[]{:S(2)}, u32[]{:S(2)}) collective-permute-start(bf16[256,256]{1,0:T(8,128)(2,1)S(1)} %pad_maximum_fusion.4.refs_7_.refs_5_), channel_id=1, source_target_pairs={{0,2},{1,3},{2,0},{3,1},{4,6},{5,7},{6,4},{7,5},{8,10},{9,11},{10,... | collective-permute-start | bytes 393224 | tf_op jit(solution)/shard_map/ppermute | solution.py:285
  32.9 14.3 %collective-permute-start.7 = (bf16[256,1024]{1,0:T(8,128)(2,1)S(1)}, bf16[256,1024]{1,0:T(8,128)(2,1)S(1)}, u32[]{:S(2)}, u32[]{:S(2)}) collective-permute-start(bf16[256,1024]{1,0:T(8,128)(2,1)S(1)} %get-tuple-element.48), channel_id=1, source_target_pairs={{0,1},{1,0},{2,3},{3,2},{4,5},{5,4},{6,7},{7,6},{8,9},{9,8},{10,11... | collective-permute-start | bytes 1572872 | tf_op jit(solution)/shard_map/ppermute | solution.py:285
  35.8 7.6 %collective-permute-start.12 = (bf16[256,512]{1,0:T(8,128)(2,1)S(1)}, bf16[256,512]{1,0:T(8,128)(2,1)S(1)}, u32[]{:S(2)}, u32[]{:S(2)}) collective-permute-start(bf16[256,512]{1,0:T(8,128)(2,1)S(1)} %get-tuple-element.56), channel_id=1, source_target_pairs={{0,16},{1,17},{2,18},{3,19},{4,20},{5,21},{6,22},{7,23},{8,24},{9,... | collective-permute-start | bytes 786440 | tf_op jit(solution)/shard_map/ppermute | solution.py:285
  38.5 8.6 %collective-permute-start.10 = (bf16[256,512]{1,0:T(8,128)(2,1)S(1)}, bf16[256,512]{1,0:T(8,128)(2,1)S(1)}, u32[]{:S(2)}, u32[]{:S(2)}) collective-permute-start(bf16[256,512]{1,0:T(8,128)(2,1)S(1)} %get-tuple-element.52), channel_id=1, source_target_pairs={{0,1},{1,0},{2,3},{3,2},{4,5},{5,4},{6,7},{7,6},{8,9},{9,8},{10,11... | collective-permute-start | bytes 786440 | tf_op jit(solution)/shard_map/ppermute | solution.py:285
  38.6 8.8 %collective-permute-start.15 = (bf16[512,256]{1,0:T(8,128)(2,1)S(1)}, bf16[512,256]{1,0:T(8,128)(2,1)S(1)}, u32[]{:S(2)}, u32[]{:S(2)}) collective-permute-start(bf16[512,256]{1,0:T(8,128)(2,1)S(1)} %pad_maximum_fusion.3), channel_id=1, source_target_pairs={{0,4},{1,5},{2,6},{3,7},{4,0},{5,1},{6,2},{7,3},{8,12},{9,13},{10,... | collective-permute-start | bytes 786440 | tf_op jit(solution)/shard_map/ppermute | solution.py:285
  43.5 4.0 %collective-permute-start.13 = (bf16[256,512]{1,0:T(8,128)(2,1)S(1)}, bf16[256,512]{1,0:T(8,128)(2,1)S(1)}, u32[]{:S(2)}, u32[]{:S(2)}) collective-permute-start(bf16[256,512]{1,0:T(8,128)(2,1)S(1)} %add_convert_fusion.mine), channel_id=1, source_target_pairs={{0,1},{1,0},{2,3},{3,2},{4,5},{5,4},{6,7},{7,6},{8,9},{9,8},{10,11... | collective-permute-start | bytes 786440 | tf_op jit(solution)/shard_map/ppermute | solution.py:285
  43.6 16.0 %collective-permute-start.17 = (bf16[256,512]{1,0:T(8,128)(2,1)S(1)}, bf16[256,512]{1,0:T(8,128)(2,1)S(1)}, u32[]{:S(2)}, u32[]{:S(2)}) collective-permute-start(bf16[256,512]{1,0:T(8,128)(2,1)S(1)} %add_convert_fusion.mine), channel_id=1, source_target_pairs={{0,8},{1,9},{2,10},{3,11},{4,12},{5,13},{6,14},{7,15},{8,0},{9,1},... | collective-permute-start | bytes 786440 | tf_op jit(solution)/shard_map/ppermute | solution.py:285
  47.5 13.7 %collective-permute-start.16 = (bf16[1024,256]{1,0:T(8,128)(2,1)S(1)}, bf16[1024,256]{1,0:T(8,128)(2,1)S(1)}, u32[]{:S(2)}, u32[]{:S(2)}) collective-permute-start(bf16[1024,256]{1,0:T(8,128)(2,1)S(1)} %pad_maximum_fusion.2.kept), channel_id=1, source_target_pairs={{0,1},{1,0},{2,3},{3,2},{4,5},{5,4},{6,7},{7,6},{8,9},{9,8},{10,11... | collective-permute-start | bytes 1572872 | tf_op jit(solution)/shard_map/ppermute | solution.py:285
  47.7 17.9 %collective-permute-start.14 = (bf16[128,2048]{1,0:T(8,128)(2,1)S(1)}, bf16[128,2048]{1,0:T(8,128)(2,1)S(1)}, u32[]{:S(2)}, u32[]{:S(2)}) collective-permute-start(bf16[128,2048]{1,0:T(8,128)(2,1)S(1)} %pad_maximum_fusion.1), channel_id=1, source_target_pairs={{0,16},{1,17},{2,18},{3,19},{4,20},{5,21},{6,22},{7,23},{8,24},{9,... | collective-permute-start | bytes 1572872 | tf_op jit(solution)/shard_map/ppermute | solution.py:285
  59.6 1.5 %collective-permute-start.18 = (bf16[256,512]{1,0:T(8,128)(2,1)S(1)}, bf16[256,512]{1,0:T(8,128)(2,1)S(1)}, u32[]{:S(2)}, u32[]{:S(2)}) collective-permute-start(bf16[256,512]{1,0:T(8,128)(2,1)S(1)} %collective-permute-done.17.twin), channel_id=1, source_target_pairs={{0,1},{1,0},{2,3},{3,2},{4,5},{5,4},{6,7},{7,6},{8,9},{9,8},{10,11... | collective-permute-start | bytes 786440 | tf_op jit(solution)/shard_map/ppermute | solution.py:285
  61.9 6.6 %collective-permute-start.19 = (bf16[128,512]{1,0:T(8,128)(2,1)S(1)}, bf16[128,512]{1,0:T(8,128)(2,1)S(1)}, u32[]{:S(2)}, u32[]{:S(2)}) collective-permute-start(bf16[128,512]{1,0:T(8,128)(2,1)S(1)} %get-tuple-element.63), channel_id=1, source_target_pairs={{0,16},{1,17},{2,18},{3,19},{4,20},{5,21},{6,22},{7,23},{8,24},{9,... | collective-permute-start | bytes 393224 | tf_op jit(solution)/shard_map/ppermute | solution.py:285
  63.4 6.4 %collective-permute-start.20 = (bf16[128,512]{1,0:T(8,128)(2,1)S(1)}, bf16[128,512]{1,0:T(8,128)(2,1)S(1)}, u32[]{:S(2)}, u32[]{:S(2)}) collective-permute-start(bf16[128,512]{1,0:T(8,128)(2,1)S(1)} %get-tuple-element.64), channel_id=1, source_target_pairs={{0,2},{1,3},{2,0},{3,1},{4,6},{5,7},{6,4},{7,5},{8,10},{9,11},{10,... | collective-permute-start | bytes 393224 | tf_op jit(solution)/shard_map/ppermute | solution.py:285
  64.1 8.6 %collective-permute-start.21 = (bf16[128,512]{1,0:T(8,128)(2,1)S(1)}, bf16[128,512]{1,0:T(8,128)(2,1)S(1)}, u32[]{:S(2)}, u32[]{:S(2)}) collective-permute-start(bf16[128,512]{1,0:T(8,128)(2,1)S(1)} %get-tuple-element.65), channel_id=1, source_target_pairs={{0,18},{1,19},{2,16},{3,17},{4,22},{5,23},{6,20},{7,21},{8,26},{9,... | collective-permute-start | bytes 393224 | tf_op jit(solution)/shard_map/ppermute | solution.py:285
  65.6 7.1 %collective-permute-start.22 = (bf16[128,512]{1,0:T(8,128)(2,1)S(1)}, bf16[128,512]{1,0:T(8,128)(2,1)S(1)}, u32[]{:S(2)}, u32[]{:S(2)}) collective-permute-start(bf16[128,512]{1,0:T(8,128)(2,1)S(1)} %get-tuple-element.66), channel_id=1, source_target_pairs={{0,4},{1,5},{2,6},{3,7},{4,0},{5,1},{6,2},{7,3},{8,12},{9,13},{10,... | collective-permute-start | bytes 393224 | tf_op jit(solution)/shard_map/ppermute | solution.py:285
  65.6 10.1 %collective-permute-start.23 = (bf16[128,512]{1,0:T(8,128)(2,1)S(1)}, bf16[128,512]{1,0:T(8,128)(2,1)S(1)}, u32[]{:S(2)}, u32[]{:S(2)}) collective-permute-start(bf16[128,512]{1,0:T(8,128)(2,1)S(1)} %get-tuple-element.67), channel_id=1, source_target_pairs={{0,20},{1,21},{2,22},{3,23},{4,16},{5,17},{6,18},{7,19},{8,28},{9,... | collective-permute-start | bytes 393224 | tf_op jit(solution)/shard_map/ppermute | solution.py:285
  68.5 8.8 %collective-permute-start.24 = (bf16[128,512]{1,0:T(8,128)(2,1)S(1)}, bf16[128,512]{1,0:T(8,128)(2,1)S(1)}, u32[]{:S(2)}, u32[]{:S(2)}) collective-permute-start(bf16[128,512]{1,0:T(8,128)(2,1)S(1)} %get-tuple-element.68), channel_id=1, source_target_pairs={{0,6},{1,7},{2,4},{3,5},{4,2},{5,3},{6,0},{7,1},{8,14},{9,15},{10,... | collective-permute-start | bytes 393224 | tf_op jit(solution)/shard_map/ppermute | solution.py:285
  69.7 9.9 %collective-permute-start.25 = (bf16[128,512]{1,0:T(8,128)(2,1)S(1)}, bf16[128,512]{1,0:T(8,128)(2,1)S(1)}, u32[]{:S(2)}, u32[]{:S(2)}) collective-permute-start(bf16[128,512]{1,0:T(8,128)(2,1)S(1)} %get-tuple-element.69), channel_id=1, source_target_pairs={{0,22},{1,23},{2,20},{3,21},{4,18},{5,19},{6,16},{7,17},{8,30},{9,... | collective-permute-start | bytes 393224 | tf_op jit(solution)/shard_map/ppermute | solution.py:285

commit v5 on v4

--- a/solution.py
+++ b/solution.py
@@ -204,21 +204,22 @@
     )(jnp.stack(blocks + [flag, side]).astype(jnp.int32), *operands)
 
 
-def regression_kernel(count, scale, flag, kept, got, mine, mine_other, twin, twin_other, *outs):
+def regression_kernel(count, scale, place, kept, got, mine, mine_other, twin, twin_other, *outs):
     rows = outs[0].shape[0]
     for j in range(2):
         left, right = ((mine, mine_other), (twin, twin_other))[j]
 
-        @pl.when(flag[0] == j)
+        @pl.when(place[count] == j)
         def _(left=left, right=right):
             for k in range(count):
-                block = slice(k * rows, (k + 1) * rows)
+                block = pl.ds(pl.multiple_of(place[k] * rows, rows), rows)
                 value = matmul(kept[block, :], left[...]) + matmul(got[block, :], right[...])
                 outs[k][...] = (value * scale).astype(jnp.bfloat16)
 
 
-def regress(kept, got, mine, mine_other, twin, twin_other, flag, count, scale):
-    rows, width = kept.shape[0] // count, mine.shape[1]
+def regress(kept, got, mine, mine_other, twin, twin_other, blocks, flag, scale):
+    count, width = len(blocks), mine.shape[1]
+    rows = kept.shape[0] // count
     return pl.pallas_call(
         functools.partial(regression_kernel, count, scale),
         in_specs=[pl.BlockSpec(memory_space=pltpu.SMEM)] + [whole()] * 6,
@@ -227,7 +228,9 @@
         compiler_params=params(),
         cost_estimate=SHORT,
         name="regress",
-    )(flag.astype(jnp.int32)[None], kept, got, mine, mine_other, twin, twin_other)
+    )(
+        jnp.stack([*blocks, flag]).astype(jnp.int32), kept, got, mine, mine_other, twin, twin_other
+    )
 
 
 def assemble_kernel(jobs, place, *refs):
@@ -366,15 +369,20 @@
     sums[1], mine_other = after(sums[1], mine_other)
     swapped = across_grp(sums[1])
 
+    size = 2 * top
+    steps = [sorted(range(size), key=lambda k: (k.bit_count(), k))]
+    steps.append([(k >> 1 | k << size.bit_length() - 2) & size - 1 for k in steps[0]])
+    step = [jnp.where(mark == 0, k, l) for k, l in zip(*steps)]
     kept, mine_other = after(kept, mine_other)
     results = regress(
-        kept, across_mark(kept), mine, mine_other, twin, across_mark(twin), flag, 2 * top, scale
-    )
-    arrived = {0: results[0]}
-    for k in range(1, 2 * top):
-        arrived[k] = move(results[k], lambda g, a, m, k=k: (g ^ k & 1, a ^ k >> 1, m))
-    arrived = [arrived[k] for k in range(2 * top)]
-    slots = [((anim ^ k >> 1) % top) * 2 + (grp ^ k & 1) for k in range(2 * top)]
+        kept, across_mark(kept), mine, mine_other, twin, across_mark(twin), step, flag, scale
+    )
+    arrived = [results[0]]
+    for i in range(1, size):
+        arrived.append(
+            move(results[i], lambda g, a, m: (g ^ steps[m][i] & 1, a ^ steps[m][i] >> 1, m))
+        )
+    slots = [((anim ^ (k >> 1)) % top) * 2 + (grp ^ (k & 1)) for k in step]
     width = mine.shape[1]
 
     width_of_piece = own.shape[1]

time: 81.8 us -> 81.2 us (level)
  waiting for transfers between devices: 36.2 us -> 28.5 us
  other arithmetic: 1.57 us -> 5.45 us
  starting transfers between devices: 29.7 us -> 31.7 us
  Pallas kernels: 13.1 us -> 14.3 us
    ppermute x26, waiting for transfers between devices: 36.2 us -> 28.5 us  [move(): return lax.ppermute(array, AXES, pairs)]
    convert_element_type x3, other arithmetic: 1.28 us -> 3.3 us  [permute_body(): (ours[part].astype(jnp.float32) + theirs[part].astype(jnp.float32)).astyp...]
    ppermute x26, starting transfers between devices: 29.7 us -> 31.7 us  [move(): return lax.ppermute(array, AXES, pairs)]
    concatenate x2, other arithmetic: 0.07 us -> 1.93 us  [permute_body(): jnp.concatenate([(ours[part].astype(jnp.float32) + theirs[part].astype(jn...]
    pallas_call x1, Pallas kernels: 0.72 us -> 1.91 us  [regress(): pl.pallas_call(functools.partial(regression_kernel, count, scale), in_spe...]
  transfers between devices with their start and end apart: 26 -> 26, of which waited for: 13 -> 11; matrix products, arithmetic and copies ran while one was open for 2% -> 7% of each run, Pallas kernels for 11% -> 13%
where the time goes in v5:
time: 81.2 us; the launch traced here: 81 us
  starting transfers between devices  31.7 us (39%)
  waiting for transfers between devices  28.5 us (35%)
  Pallas kernels  14.3 us (18%)
  other arithmetic  5.45 us (7%)
    ppermute x26, starting transfers between devices, move(): return lax.ppermute(array, AXES, pairs)  31.7 us
    ppermute x26, waiting for transfers between devices, move(): return lax.ppermute(array, AXES, pairs)  28.5 us
    pallas_call x3, Pallas kernels, absorb(): pl.pallas_call(functools.partial(absorb_kernel, count, len(pairs), ahead,...  8.61 us
    convert_element_type x3, other arithmetic, permute_body(): (ours[part].astype(jnp.float32) + theirs[part].astype(jnp.float32)).astyp...  3.3 us
    pallas_call x1, Pallas kernels, assemble(): pl.pallas_call(functools.partial(assemble_kernel, [(len(job[0]), job[2])...  1.98 us
    concatenate x2, other arithmetic, permute_body(): jnp.concatenate([(ours[part].astype(jnp.float32) + theirs[part].astype(jn...  1.93 us
    pallas_call x1, Pallas kernels, regress(): pl.pallas_call(functools.partial(regression_kernel, count, scale), in_spe...  1.91 us
    pallas_call x1, Pallas kernels, centre(): pl.pallas_call(centre_kernel, in_specs=[pl.BlockSpec(memory_space=pltpu.S...  1.75 us
  transfers between devices with their start and end apart: 26, of which 11 were waited for; matrix products, arithmetic and copies ran while one was open for 7% of the time, Pallas kernels for 13%

profile of v5, /device:TPU:0, one launch (start us, length us, event | category | flops | bytes accessed | tf_op | source)
XLA Modules:
  0.0 81.0 jit_solution(6670789542781916743)
XLA Ops:
  0.6 1.8 %centre.1 = (bf16[256,512]{1,0:T(8,128)(2,1)S(1)}, bf16[128,256]{1,0:T(8,128)(2,1)S(1)}) custom-call(s32[1]{0:T(128)} %bitcast.20.place, s32[1024,256]{1,0:T(8,128)} %geno.1, s32[5,1024]{1,0:T(8,128)} %codes.1, f32[5,256]{1,0:T(8,128)} %freqs.1, s32[128,256]{1,0:T(8,128)} %noncore_geno.1, s32[5,128]{1,0:T(8,128)} %noncore_codes.1), custom_call_target="tpu_custom_call" | custom-call | tf_op jit(solution)/shard_map/centre/pallas_call | solution.py:103
  2.4 4.1 %collective-permute-start = (bf16[256,512]{1,0:T(8,128)(2,1)S(1)}, bf16[256,512]{1,0:T(8,128)(2,1)S(1)}, u32[]{:S(2)}, u32[]{:S(2)}) collective-permute-start(bf16[256,512]{1,0:T(8,128)(2,1)S(1)} %get-tuple-element.36.refs_0_.refs_5_), channel_id=1, source_target_pairs={{0,8},{1,9},{2,10},{3,11},{4,12},{5,13},{6,14},{7,15},{8,0},{9,1},... | collective-permute-start | bytes 786440 | tf_op jit(solution)/shard_map/ppermute | solution.py:288
  6.5 1.5 %collective-permute-start.1 = (bf16[256,512]{1,0:T(8,128)(2,1)S(1)}, bf16[256,512]{1,0:T(8,128)(2,1)S(1)}, u32[]{:S(2)}, u32[]{:S(2)}) collective-permute-start(bf16[256,512]{1,0:T(8,128)(2,1)S(1)} %get-tuple-element.36.refs_0_.refs_5_), channel_id=1, source_target_pairs={{0,2},{1,3},{2,0},{3,1},{4,6},{5,7},{6,4},{7,5},{8,10},{9,11},{10,... | collective-permute-start | bytes 786440 | tf_op jit(solution)/shard_map/ppermute | solution.py:288
  8.0 1.5 %collective-permute-start.2 = (bf16[128,256]{1,0:T(8,128)(2,1)S(1)}, bf16[128,256]{1,0:T(8,128)(2,1)S(1)}, u32[]{:S(2)}, u32[]{:S(2)}) collective-permute-start(bf16[128,256]{1,0:T(8,128)(2,1)S(1)} %get-tuple-element.37), channel_id=1, source_target_pairs={{0,16},{1,17},{2,18},{3,19},{4,20},{5,21},{6,22},{7,23},{8,24},{9,... | collective-permute-start | bytes 196616 | tf_op jit(solution)/shard_map/ppermute | solution.py:288
  9.5 1.6 %collective-permute-start.3 = (bf16[256,512]{1,0:T(8,128)(2,1)S(1)}, bf16[256,512]{1,0:T(8,128)(2,1)S(1)}, u32[]{:S(2)}, u32[]{:S(2)}) collective-permute-start(bf16[256,512]{1,0:T(8,128)(2,1)S(1)} %get-tuple-element.36.refs_0_.refs_5_), channel_id=1, source_target_pairs={{0,4},{1,5},{2,6},{3,7},{4,0},{5,1},{6,2},{7,3},{8,12},{9,13},{10,... | collective-permute-start | bytes 786440 | tf_op jit(solution)/shard_map/ppermute | solution.py:288
  11.1 1.2 %collective-permute-done.2 = bf16[128,256]{1,0:T(8,128)(2,1)S(1)} collective-permute-done((bf16[128,256]{1,0:T(8,128)(2,1)S(1)}, bf16[128,256]{1,0:T(8,128)(2,1)S(1)}, u32[]{:S(2)}, u32[]{:S(2)}) %collective-permute-start.2) | collective-permute-done | bytes 65568 | tf_op jit(solution)/shard_map/ppermute | solution.py:288
  12.3 6.3 %collective-permute-done.refs_2_.refs_6_ = bf16[256,512]{1,0:T(8,128)(2,1)S(1)} collective-permute-done((bf16[256,512]{1,0:T(8,128)(2,1)S(1)}, bf16[256,512]{1,0:T(8,128)(2,1)S(1)}, u32[]{:S(2)}, u32[]{:S(2)}) %collective-permute-start) | collective-permute-done | bytes 262176 | tf_op jit(solution)/shard_map/ppermute | solution.py:288
  18.5 1.5 %collective-permute-start.5 = (bf16[256,512]{1,0:T(8,128)(2,1)S(1)}, bf16[256,512]{1,0:T(8,128)(2,1)S(1)}, u32[]{:S(2)}, u32[]{:S(2)}) collective-permute-start(bf16[256,512]{1,0:T(8,128)(2,1)S(1)} %collective-permute-done.refs_2_.refs_6_), channel_id=1, source_target_pairs={{0,2},{1,3},{2,0},{3,1},{4,6},{5,7},{6,4},{7,5},{8,10},{9,11},{10,... | collective-permute-start | bytes 786440 | tf_op jit(solution)/shard_map/ppermute | solution.py:288
  21.8 4.1 %absorb.3 = (f32[256,1024]{1,0:T(8,128)S(1)}, bf16[256,512]{1,0:T(8,128)(2,1)S(1)}, bf16[256,512]{1,0:T(8,128)(2,1)S(1)}) custom-call(s32[6]{0:T(128)S(1)} %stack.140.place, bf16[256,512]{1,0:T(8,128)(2,1)S(1)} %get-tuple-element.36.refs_0_.refs_5_, bf16[256,512]{1,0:T(8,128)(2,1)S(1)} %collective-permute-done.1.refs_1_.refs_3_, ...), custom_call_target="tpu_custom_call" | custom-call | tf_op jit(solution)/shard_map/absorb/pallas_call | solution.py:192
  25.8 1.9 %collective-permute-done.5.refs_0_.refs_4_ = bf16[256,512]{1,0:T(8,128)(2,1)S(1)} collective-permute-done((bf16[256,512]{1,0:T(8,128)(2,1)S(1)}, bf16[256,512]{1,0:T(8,128)(2,1)S(1)}, u32[]{:S(2)}, u32[]{:S(2)}) %collective-permute-start.5) | collective-permute-done | bytes 262176 | tf_op jit(solution)/shard_map/ppermute | solution.py:288
  28.5 1.5 %collective-permute-start.11 = (bf16[256,256]{1,0:T(8,128)(2,1)S(1)}, bf16[256,256]{1,0:T(8,128)(2,1)S(1)}, u32[]{:S(2)}, u32[]{:S(2)}) collective-permute-start(bf16[256,256]{1,0:T(8,128)(2,1)S(1)} %pad_maximum_fusion.4.refs_7_.refs_5_), channel_id=1, source_target_pairs={{0,2},{1,3},{2,0},{3,1},{4,6},{5,7},{6,4},{7,5},{8,10},{9,11},{10,... | collective-permute-start | bytes 393224 | tf_op jit(solution)/shard_map/ppermute | solution.py:288
  30.0 2.9 %absorb.4 = (f32[256,1024]{1,0:T(8,128)S(1)}, bf16[256,1024]{1,0:T(8,128)(2,1)S(1)}, bf16[256,1024]{1,0:T(8,128)(2,1)S(1)}, bf16[2,512,1024]{2,1,0:T(8,128)(2,1)S(1)}) custom-call(s32[6]{0:T(128)S(1)} %stack.145.place, bf16[256,512]{1,0:T(8,128)(2,1)S(1)} %collective-permute-done.5.refs_0_.refs_4_, ...), custom_call_target="tpu_custom_call" | custom-call | tf_op jit(solution)/shard_map/absorb/pallas_call | solution.py:192
  33.2 0.9 %collective-permute-done.9.refs_1_.refs_4_ = bf16[256,512]{1,0:T(8,128)(2,1)S(1)} collective-permute-done((bf16[256,512]{1,0:T(8,128)(2,1)S(1)}, bf16[256,512]{1,0:T(8,128)(2,1)S(1)}, u32[]{:S(2)}, u32[]{:S(2)}) %collective-permute-start.9) | collective-permute-done | bytes 262176 | tf_op jit(solution)/shard_map/ppermute | solution.py:288
  34.2 1.6 %absorb.5 = (f32[256,512]{1,0:T(8,128)S(1)}, bf16[256,512]{1,0:T(8,128)(2,1)S(1)}, bf16[256,512]{1,0:T(8,128)(2,1)S(1)}, bf16[256,512]{1,0:T(8,128)(2,1)S(1)}) custom-call(s32[4]{0:T(128)S(1)} %pad_add_fusion.place, bf16[256,512]{1,0:T(8,128)(2,1)S(1)} %collective-permute-done.8.refs_0_.refs_3_, bf16[256,512]{1,0:T(8,128)(2,1)S(1)} %collective-permute-done.9.refs_1_.refs_4_, ...), custom_call_target="tpu_custom_call" | custom-call | tf_op jit(solution)/shard_map/absorb/pallas_call | solution.py:192
  35.8 1.6 %collective-permute-start.12 = (bf16[256,512]{1,0:T(8,128)(2,1)S(1)}, bf16[256,512]{1,0:T(8,128)(2,1)S(1)}, u32[]{:S(2)}, u32[]{:S(2)}) collective-permute-start(bf16[256,512]{1,0:T(8,128)(2,1)S(1)} %get-tuple-element.56), channel_id=1, source_target_pairs={{0,16},{1,17},{2,18},{3,19},{4,20},{5,21},{6,22},{7,23},{8,24},{9,... | collective-permute-start | bytes 786440 | tf_op jit(solution)/shard_map/ppermute | solution.py:288
  37.4 1.7 %add_convert_fusion.4 = (bf16[128,512]{1,0:T(8,128)(2,1)S(1)}, bf16[128,512]{1,0:T(8,128)(2,1)}) fusion(bf16[256,512]{1,0:T(8,128)(2,1)} %collective-permute-done.4, bf16[256,512]{1,0:T(8,128)(2,1)S(1)} %get-tuple-element.41), kind=kLoop, calls=%fused_computation.8 | loop fusion | flops 524288 | bytes 786432 | tf_op jit(solution)/shard_map/convert_element_type | solution.py:360
  39.8 3.6 %collective-permute-done.12 = bf16[256,512]{1,0:T(8,128)(2,1)S(1)} collective-permute-done((bf16[256,512]{1,0:T(8,128)(2,1)S(1)}, bf16[256,512]{1,0:T(8,128)(2,1)S(1)}, u32[]{:S(2)}, u32[]{:S(2)}) %collective-permute-start.12) | collective-permute-done | bytes 262176 | tf_op jit(solution)/shard_map/ppermute | solution.py:288
  43.6 3.5 %collective-permute-start.17 = (bf16[256,512]{1,0:T(8,128)(2,1)S(1)}, bf16[256,512]{1,0:T(8,128)(2,1)S(1)}, u32[]{:S(2)}, u32[]{:S(2)}) collective-permute-start(bf16[256,512]{1,0:T(8,128)(2,1)S(1)} %add_convert_fusion.mine), channel_id=1, source_target_pairs={{0,8},{1,9},{2,10},{3,11},{4,12},{5,13},{6,14},{7,15},{8,0},{9,1},... | collective-permute-start | bytes 786440 | tf_op jit(solution)/shard_map/ppermute | solution.py:288
  47.9 0.9 %add_convert_fusion.1 = (bf16[128,1024]{1,0:T(8,128)(2,1)S(1)}, bf16[128,1024]{1,0:T(8,128)(2,1)}) fusion(bf16[256,1024]{1,0:T(8,128)(2,1)S(1)} %collective-permute-done.7, bf16[256,1024]{1,0:T(8,128)(2,1)S(1)} %get-tuple-element.47), kind=kLoop, calls=%fused_computation.4 | loop fusion | flops 1048576 | bytes 1572864 | tf_op jit(solution)/shard_map/convert_element_type | solution.py:360
  48.8 0.8 %pad_maximum_fusion.1 = bf16[128,2048]{1,0:T(8,128)(2,1)} fusion(bf16[128,512]{1,0:T(8,128)(2,1)S(1)} %get-tuple-element.74, bf16[128,1024]{1,0:T(8,128)(2,1)S(1)} %get-tuple-element.70, bf16[128,512]{1,0:T(8,128)(2,1)S(1)} %get-tuple-element.72), kind=kLoop, calls=%fused_computation.1 | loop fusion | flops 1572864 | bytes 1048576 | tf_op jit(solution)/shard_map/concatenate | solution.py:358
  49.8 1.4 %collective-permute-start.14 = (bf16[128,2048]{1,0:T(8,128)(2,1)}, bf16[128,2048]{1,0:T(8,128)(2,1)S(1)}, u32[]{:S(2)}, u32[]{:S(2)}) collective-permute-start(bf16[128,2048]{1,0:T(8,128)(2,1)} %pad_maximum_fusion.1), channel_id=1, source_target_pairs={{0,16},{1,17},{2,18},{3,19},{4,20},{5,21},{6,22},{7,23},{8,24},{9,... | collective-permute-start | bytes 1572872 | tf_op jit(solution)/shard_map/ppermute | solution.py:288
  51.2 8.5 %collective-permute-done.17.twin = bf16[256,512]{1,0:T(8,128)(2,1)S(1)} collective-permute-done((bf16[256,512]{1,0:T(8,128)(2,1)S(1)}, bf16[256,512]{1,0:T(8,128)(2,1)S(1)}, u32[]{:S(2)}, u32[]{:S(2)}) %collective-permute-start.17) | collective-permute-done | bytes 262176 | tf_op jit(solution)/shard_map/ppermute | solution.py:288
  59.7 1.4 %collective-permute-done.18.twin_other = bf16[256,512]{1,0:T(8,128)(2,1)S(1)} collective-permute-done((bf16[256,512]{1,0:T(8,128)(2,1)S(1)}, bf16[256,512]{1,0:T(8,128)(2,1)S(1)}, u32[]{:S(2)}, u32[]{:S(2)}) %collective-permute-start.18) | collective-permute-done | bytes 262176 | tf_op jit(solution)/shard_map/ppermute | solution.py:288
  61.2 1.9 %regress.1 = (bf16[128,512]{1,0:T(8,128)(2,1)S(1)}, bf16[128,512]{1,0:T(8,128)(2,1)}, bf16[128,512]{1,0:T(8,128)(2,1)S(1)}, bf16[128,512]{1,0:T(8,128)(2,1)S(1)}...) custom-call(s32[9]{0:T(128)S(1)} %stack.153.place, ...), custom_call_target="tpu_custom_call" | custom-call | tf_op jit(solution)/shard_map/regress/pallas_call | solution.py:223
  63.1 1.4 %collective-permute-start.19 = (bf16[128,512]{1,0:T(8,128)(2,1)}, bf16[128,512]{1,0:T(8,128)(2,1)S(1)}, u32[]{:S(2)}, u32[]{:S(2)}) collective-permute-start(bf16[128,512]{1,0:T(8,128)(2,1)} %get-tuple-element.63), channel_id=1, source_target_pairs={{0,16},{1,5},{2,18},{3,7},{4,20},{5,1},{6,22},{7,3},{8,24},{9,13},... | collective-permute-start | bytes 393224 | tf_op jit(solution)/shard_map/ppermute | solution.py:288
  65.3 1.5 %collective-permute-start.22 = (bf16[128,512]{1,0:T(8,128)(2,1)S(1)}, bf16[128,512]{1,0:T(8,128)(2,1)S(1)}, u32[]{:S(2)}, u32[]{:S(2)}) collective-permute-start(bf16[128,512]{1,0:T(8,128)(2,1)S(1)} %get-tuple-element.66), channel_id=1, source_target_pairs={{0,18},{1,21},{2,16},{3,23},{4,22},{5,17},{6,20},{7,19},{8,26},{9,... | collective-permute-start | bytes 393224 | tf_op jit(solution)/shard_map/ppermute | solution.py:288
  66.8 2.8 %collective-permute-start.23 = (bf16[128,512]{1,0:T(8,128)(2,1)S(1)}, bf16[128,512]{1,0:T(8,128)(2,1)S(1)}, u32[]{:S(2)}, u32[]{:S(2)}) collective-permute-start(bf16[128,512]{1,0:T(8,128)(2,1)S(1)} %get-tuple-element.67), channel_id=1, source_target_pairs={{0,20},{1,7},{2,22},{3,5},{4,16},{5,3},{6,18},{7,1},{8,28},{9,15},... | collective-permute-start | bytes 393224 | tf_op jit(solution)/shard_map/ppermute | solution.py:288
  69.9 3.9 %collective-permute-start.25 = (bf16[128,512]{1,0:T(8,128)(2,1)S(1)}, bf16[128,512]{1,0:T(8,128)(2,1)S(1)}, u32[]{:S(2)}, u32[]{:S(2)}) collective-permute-start(bf16[128,512]{1,0:T(8,128)(2,1)S(1)} %get-tuple-element.69), channel_id=1, source_target_pairs={{0,22},{1,23},{2,20},{3,21},{4,18},{5,19},{6,16},{7,17},{8,30},{9,... | collective-permute-start | bytes 393224 | tf_op jit(solution)/shard_map/ppermute | solution.py:288
  73.8 1.1 %pad_maximum_fusion.refs_0_ = bf16[128,2048]{1,0:T(8,128)(2,1)S(1)} fusion(bf16[128,512]{1,0:T(8,128)(2,1)} %get-tuple-element.75, bf16[128,1024]{1,0:T(8,128)(2,1)} %get-tuple-element.71, bf16[128,512]{1,0:T(8,128)(2,1)} %get-tuple-element.73), kind=kLoop, calls=%fused_computation | loop fusion | flops 1572864 | bytes 1048576 | tf_op jit(solution)/shard_map/concatenate | solution.py:358
  74.9 1.9 %collective-permute-done.24.refs_8_ = bf16[128,512]{1,0:T(8,128)(2,1)S(1)} collective-permute-done((bf16[128,512]{1,0:T(8,128)(2,1)S(1)}, bf16[128,512]{1,0:T(8,128)(2,1)S(1)}, u32[]{:S(2)}, u32[]{:S(2)}) %collective-permute-start.24) | collective-permute-done | bytes 131104 | tf_op jit(solution)/shard_map/ppermute | solution.py:288
  76.8 2.2 %collective-permute-done.25.refs_9_ = bf16[128,512]{1,0:T(8,128)(2,1)S(1)} collective-permute-done((bf16[128,512]{1,0:T(8,128)(2,1)S(1)}, bf16[128,512]{1,0:T(8,128)(2,1)S(1)}, u32[]{:S(2)}, u32[]{:S(2)}) %collective-permute-start.25) | collective-permute-done | bytes 131104 | tf_op jit(solution)/shard_map/ppermute | solution.py:288
  79.0 2.0 %assemble.1 = (bf16[128,4096]{1,0:T(8,128)(2,1)}, bf16[128,4096]{1,0:T(8,128)(2,1)}) custom-call(s32[16]{0:T(128)S(1)} %stack.133.place, bf16[128,2048]{1,0:T(8,128)(2,1)S(1)} %pad_maximum_fusion.refs_0_, bf16[128,2048]{1,0:T(8,128)(2,1)S(1)} %collective-permute-done.14.refs_1_, bf16[128,512]{1,0:T(8,128)(2,1)S(1)} %get-tuple-element.62.refs_2_, ...), custom_call_target="tpu_custom_call" | custom-call | tf_op jit(solution)/shard_map/assemble/pallas_call | solution.py:259
  (40 shorter events, 5.7 us)
Async XLA Ops:
  2.4 16.1 %collective-permute-start = (bf16[256,512]{1,0:T(8,128)(2,1)S(1)}, bf16[256,512]{1,0:T(8,128)(2,1)S(1)}, u32[]{:S(2)}, u32[]{:S(2)}) collective-permute-start(bf16[256,512]{1,0:T(8,128)(2,1)S(1)} %get-tuple-element.36.refs_0_.refs_5_), channel_id=1, source_target_pairs={{0,8},{1,9},{2,10},{3,11},{4,12},{5,13},{6,14},{7,15},{8,0},{9,1},... | collective-permute-start | bytes 786440 | tf_op jit(solution)/shard_map/ppermute | solution.py:288
  6.5 12.0 %collective-permute-start.1 = (bf16[256,512]{1,0:T(8,128)(2,1)S(1)}, bf16[256,512]{1,0:T(8,128)(2,1)S(1)}, u32[]{:S(2)}, u32[]{:S(2)}) collective-permute-start(bf16[256,512]{1,0:T(8,128)(2,1)S(1)} %get-tuple-element.36.refs_0_.refs_5_), channel_id=1, source_target_pairs={{0,2},{1,3},{2,0},{3,1},{4,6},{5,7},{6,4},{7,5},{8,10},{9,11},{10,... | collective-permute-start | bytes 786440 | tf_op jit(solution)/shard_map/ppermute | solution.py:288
  8.0 4.3 %collective-permute-start.2 = (bf16[128,256]{1,0:T(8,128)(2,1)S(1)}, bf16[128,256]{1,0:T(8,128)(2,1)S(1)}, u32[]{:S(2)}, u32[]{:S(2)}) collective-permute-start(bf16[128,256]{1,0:T(8,128)(2,1)S(1)} %get-tuple-element.37), channel_id=1, source_target_pairs={{0,16},{1,17},{2,18},{3,19},{4,20},{5,21},{6,22},{7,23},{8,24},{9,... | collective-permute-start | bytes 196616 | tf_op jit(solution)/shard_map/ppermute | solution.py:288
  9.5 11.7 %collective-permute-start.3 = (bf16[256,512]{1,0:T(8,128)(2,1)S(1)}, bf16[256,512]{1,0:T(8,128)(2,1)S(1)}, u32[]{:S(2)}, u32[]{:S(2)}) collective-permute-start(bf16[256,512]{1,0:T(8,128)(2,1)S(1)} %get-tuple-element.36.refs_0_.refs_5_), channel_id=1, source_target_pairs={{0,4},{1,5},{2,6},{3,7},{4,0},{5,1},{6,2},{7,3},{8,12},{9,13},{10,... | collective-permute-start | bytes 786440 | tf_op jit(solution)/shard_map/ppermute | solution.py:288
  18.5 9.2 %collective-permute-start.5 = (bf16[256,512]{1,0:T(8,128)(2,1)S(1)}, bf16[256,512]{1,0:T(8,128)(2,1)S(1)}, u32[]{:S(2)}, u32[]{:S(2)}) collective-permute-start(bf16[256,512]{1,0:T(8,128)(2,1)S(1)} %collective-permute-done.refs_2_.refs_6_), channel_id=1, source_target_pairs={{0,2},{1,3},{2,0},{3,1},{4,6},{5,7},{6,4},{7,5},{8,10},{9,11},{10,... | collective-permute-start | bytes 786440 | tf_op jit(solution)/shard_map/ppermute | solution.py:288
  20.2 8.4 %collective-permute-start.6 = (bf16[256,512]{1,0:T(8,128)(2,1)S(1)}, bf16[256,512]{1,0:T(8,128)(2,1)S(1)}, u32[]{:S(2)}, u32[]{:S(2)}) collective-permute-start(bf16[256,512]{1,0:T(8,128)(2,1)S(1)} %collective-permute-done.refs_2_.refs_6_), channel_id=1, source_target_pairs={{0,4},{1,5},{2,6},{3,7},{4,0},{5,1},{6,2},{7,3},{8,12},{9,13},{10,... | collective-permute-start | bytes 786440 | tf_op jit(solution)/shard_map/ppermute | solution.py:288
  21.2 12.1 %collective-permute-start.8 = (bf16[256,512]{1,0:T(8,128)(2,1)S(1)}, bf16[256,512]{1,0:T(8,128)(2,1)S(1)}, u32[]{:S(2)}, u32[]{:S(2)}) collective-permute-start(bf16[256,512]{1,0:T(8,128)(2,1)S(1)} %collective-permute-done.3.refs_3_.refs_5_), channel_id=1, source_target_pairs={{0,2},{1,3},{2,0},{3,1},{4,6},{5,7},{6,4},{7,5},{8,10},{9,11},{10,... | collective-permute-start | bytes 786440 | tf_op jit(solution)/shard_map/ppermute | solution.py:288
  27.8 6.4 %collective-permute-start.9 = (bf16[256,512]{1,0:T(8,128)(2,1)S(1)}, bf16[256,512]{1,0:T(8,128)(2,1)S(1)}, u32[]{:S(2)}, u32[]{:S(2)}) collective-permute-start(bf16[256,512]{1,0:T(8,128)(2,1)S(1)} %collective-permute-done.5.refs_0_.refs_4_), channel_id=1, source_target_pairs={{0,4},{1,5},{2,6},{3,7},{4,0},{5,1},{6,2},{7,3},{8,12},{9,13},{10,... | collective-permute-start | bytes 786440 | tf_op jit(solution)/shard_map/ppermute | solution.py:288
  28.4 9.1 %collective-permute-start.4 = (bf16[256,512]{1,0:T(8,128)(2,1)S(1)}, bf16[256,512]{1,0:T(8,128)(2,1)}, u32[]{:S(2)}, u32[]{:S(2)}) collective-permute-start(bf16[256,512]{1,0:T(8,128)(2,1)S(1)} %get-tuple-element.42), channel_id=1, source_target_pairs={{0,1},{1,0},{2,3},{3,2},{4,5},{5,4},{6,7},{7,6},{8,9},{9,8},{10,11... | collective-permute-start | bytes 786440 | tf_op jit(solution)/shard_map/ppermute | solution.py:288
  28.5 10.6 %collective-permute-start.11 = (bf16[256,256]{1,0:T(8,128)(2,1)S(1)}, bf16[256,256]{1,0:T(8,128)(2,1)S(1)}, u32[]{:S(2)}, u32[]{:S(2)}) collective-permute-start(bf16[256,256]{1,0:T(8,128)(2,1)S(1)} %pad_maximum_fusion.4.refs_7_.refs_5_), channel_id=1, source_target_pairs={{0,2},{1,3},{2,0},{3,1},{4,6},{5,7},{6,4},{7,5},{8,10},{9,11},{10,... | collective-permute-start | bytes 393224 | tf_op jit(solution)/shard_map/ppermute | solution.py:288
  32.9 14.9 %collective-permute-start.7 = (bf16[256,1024]{1,0:T(8,128)(2,1)S(1)}, bf16[256,1024]{1,0:T(8,128)(2,1)S(1)}, u32[]{:S(2)}, u32[]{:S(2)}) collective-permute-start(bf16[256,1024]{1,0:T(8,128)(2,1)S(1)} %get-tuple-element.48), channel_id=1, source_target_pairs={{0,1},{1,0},{2,3},{3,2},{4,5},{5,4},{6,7},{7,6},{8,9},{9,8},{10,11... | collective-permute-start | bytes 1572872 | tf_op jit(solution)/shard_map/ppermute | solution.py:288
  35.8 7.6 %collective-permute-start.12 = (bf16[256,512]{1,0:T(8,128)(2,1)S(1)}, bf16[256,512]{1,0:T(8,128)(2,1)S(1)}, u32[]{:S(2)}, u32[]{:S(2)}) collective-permute-start(bf16[256,512]{1,0:T(8,128)(2,1)S(1)} %get-tuple-element.56), channel_id=1, source_target_pairs={{0,16},{1,17},{2,18},{3,19},{4,20},{5,21},{6,22},{7,23},{8,24},{9,... | collective-permute-start | bytes 786440 | tf_op jit(solution)/shard_map/ppermute | solution.py:288
  39.1 8.0 %collective-permute-start.10 = (bf16[256,512]{1,0:T(8,128)(2,1)S(1)}, bf16[256,512]{1,0:T(8,128)(2,1)S(1)}, u32[]{:S(2)}, u32[]{:S(2)}) collective-permute-start(bf16[256,512]{1,0:T(8,128)(2,1)S(1)} %get-tuple-element.52), channel_id=1, source_target_pairs={{0,1},{1,0},{2,3},{3,2},{4,5},{5,4},{6,7},{7,6},{8,9},{9,8},{10,11... | collective-permute-start | bytes 786440 | tf_op jit(solution)/shard_map/ppermute | solution.py:288
  39.1 9.6 %collective-permute-start.15 = (bf16[512,256]{1,0:T(8,128)(2,1)S(1)}, bf16[512,256]{1,0:T(8,128)(2,1)S(1)}, u32[]{:S(2)}, u32[]{:S(2)}) collective-permute-start(bf16[512,256]{1,0:T(8,128)(2,1)S(1)} %pad_maximum_fusion.3), channel_id=1, source_target_pairs={{0,4},{1,5},{2,6},{3,7},{4,0},{5,1},{6,2},{7,3},{8,12},{9,13},{10,... | collective-permute-start | bytes 786440 | tf_op jit(solution)/shard_map/ppermute | solution.py:288
  43.5 6.1 %collective-permute-start.13 = (bf16[256,512]{1,0:T(8,128)(2,1)S(1)}, bf16[256,512]{1,0:T(8,128)(2,1)S(1)}, u32[]{:S(2)}, u32[]{:S(2)}) collective-permute-start(bf16[256,512]{1,0:T(8,128)(2,1)S(1)} %add_convert_fusion.mine), channel_id=1, source_target_pairs={{0,1},{1,0},{2,3},{3,2},{4,5},{5,4},{6,7},{7,6},{8,9},{9,8},{10,11... | collective-permute-start | bytes 786440 | tf_op jit(solution)/shard_map/ppermute | solution.py:288
  43.6 16.0 %collective-permute-start.17 = (bf16[256,512]{1,0:T(8,128)(2,1)S(1)}, bf16[256,512]{1,0:T(8,128)(2,1)S(1)}, u32[]{:S(2)}, u32[]{:S(2)}) collective-permute-start(bf16[256,512]{1,0:T(8,128)(2,1)S(1)} %add_convert_fusion.mine), channel_id=1, source_target_pairs={{0,8},{1,9},{2,10},{3,11},{4,12},{5,13},{6,14},{7,15},{8,0},{9,1},... | collective-permute-start | bytes 786440 | tf_op jit(solution)/shard_map/ppermute | solution.py:288
  49.6 11.5 %collective-permute-start.16 = (bf16[1024,256]{1,0:T(8,128)(2,1)S(1)}, bf16[1024,256]{1,0:T(8,128)(2,1)S(1)}, u32[]{:S(2)}, u32[]{:S(2)}) collective-permute-start(bf16[1024,256]{1,0:T(8,128)(2,1)S(1)} %pad_maximum_fusion.2.kept), channel_id=1, source_target_pairs={{0,1},{1,0},{2,3},{3,2},{4,5},{5,4},{6,7},{7,6},{8,9},{9,8},{10,11... | collective-permute-start | bytes 1572872 | tf_op jit(solution)/shard_map/ppermute | solution.py:288
  49.8 17.0 %collective-permute-start.14 = (bf16[128,2048]{1,0:T(8,128)(2,1)}, bf16[128,2048]{1,0:T(8,128)(2,1)S(1)}, u32[]{:S(2)}, u32[]{:S(2)}) collective-permute-start(bf16[128,2048]{1,0:T(8,128)(2,1)} %pad_maximum_fusion.1), channel_id=1, source_target_pairs={{0,16},{1,17},{2,18},{3,19},{4,20},{5,21},{6,22},{7,23},{8,24},{9,... | collective-permute-start | bytes 1572872 | tf_op jit(solution)/shard_map/ppermute | solution.py:288
  59.6 1.5 %collective-permute-start.18 = (bf16[256,512]{1,0:T(8,128)(2,1)S(1)}, bf16[256,512]{1,0:T(8,128)(2,1)S(1)}, u32[]{:S(2)}, u32[]{:S(2)}) collective-permute-start(bf16[256,512]{1,0:T(8,128)(2,1)S(1)} %collective-permute-done.17.twin), channel_id=1, source_target_pairs={{0,1},{1,0},{2,3},{3,2},{4,5},{5,4},{6,7},{7,6},{8,9},{9,8},{10,11... | collective-permute-start | bytes 786440 | tf_op jit(solution)/shard_map/ppermute | solution.py:288
  63.1 6.5 %collective-permute-start.19 = (bf16[128,512]{1,0:T(8,128)(2,1)}, bf16[128,512]{1,0:T(8,128)(2,1)S(1)}, u32[]{:S(2)}, u32[]{:S(2)}) collective-permute-start(bf16[128,512]{1,0:T(8,128)(2,1)} %get-tuple-element.63), channel_id=1, source_target_pairs={{0,16},{1,5},{2,18},{3,7},{4,20},{5,1},{6,22},{7,3},{8,24},{9,13},... | collective-permute-start | bytes 393224 | tf_op jit(solution)/shard_map/ppermute | solution.py:288
  64.5 5.4 %collective-permute-start.20 = (bf16[128,512]{1,0:T(8,128)(2,1)S(1)}, bf16[128,512]{1,0:T(8,128)(2,1)S(1)}, u32[]{:S(2)}, u32[]{:S(2)}) collective-permute-start(bf16[128,512]{1,0:T(8,128)(2,1)S(1)} %get-tuple-element.64), channel_id=1, source_target_pairs={{0,2},{1,17},{2,0},{3,19},{4,6},{5,21},{6,4},{7,23},{8,10},{9,25},... | collective-permute-start | bytes 393224 | tf_op jit(solution)/shard_map/ppermute | solution.py:288
  65.2 9.7 %collective-permute-start.21 = (bf16[128,512]{1,0:T(8,128)(2,1)S(1)}, bf16[128,512]{1,0:T(8,128)(2,1)S(1)}, u32[]{:S(2)}, u32[]{:S(2)}) collective-permute-start(bf16[128,512]{1,0:T(8,128)(2,1)S(1)} %get-tuple-element.65), channel_id=1, source_target_pairs={{0,4},{1,3},{2,6},{3,1},{4,0},{5,7},{6,2},{7,5},{8,12},{9,11},{10,... | collective-permute-start | bytes 393224 | tf_op jit(solution)/shard_map/ppermute | solution.py:288
  65.3 9.6 %collective-permute-start.22 = (bf16[128,512]{1,0:T(8,128)(2,1)S(1)}, bf16[128,512]{1,0:T(8,128)(2,1)S(1)}, u32[]{:S(2)}, u32[]{:S(2)}) collective-permute-start(bf16[128,512]{1,0:T(8,128)(2,1)S(1)} %get-tuple-element.66), channel_id=1, source_target_pairs={{0,18},{1,21},{2,16},{3,23},{4,22},{5,17},{6,20},{7,19},{8,26},{9,... | collective-permute-start | bytes 393224 | tf_op jit(solution)/shard_map/ppermute | solution.py:288
  66.8 8.1 %collective-permute-start.23 = (bf16[128,512]{1,0:T(8,128)(2,1)S(1)}, bf16[128,512]{1,0:T(8,128)(2,1)S(1)}, u32[]{:S(2)}, u32[]{:S(2)}) collective-permute-start(bf16[128,512]{1,0:T(8,128)(2,1)S(1)} %get-tuple-element.67), channel_id=1, source_target_pairs={{0,20},{1,7},{2,22},{3,5},{4,16},{5,3},{6,18},{7,1},{8,28},{9,15},... | collective-permute-start | bytes 393224 | tf_op jit(solution)/shard_map/ppermute | solution.py:288
  69.6 7.2 %collective-permute-start.24 = (bf16[128,512]{1,0:T(8,128)(2,1)S(1)}, bf16[128,512]{1,0:T(8,128)(2,1)S(1)}, u32[]{:S(2)}, u32[]{:S(2)}) collective-permute-start(bf16[128,512]{1,0:T(8,128)(2,1)S(1)} %get-tuple-element.68), channel_id=1, source_target_pairs={{0,6},{1,19},{2,4},{3,17},{4,2},{5,23},{6,0},{7,21},{8,14},{9,27},... | collective-permute-start | bytes 393224 | tf_op jit(solution)/shard_map/ppermute | solution.py:288
  69.9 9.1 %collective-permute-start.25 = (bf16[128,512]{1,0:T(8,128)(2,1)S(1)}, bf16[128,512]{1,0:T(8,128)(2,1)S(1)}, u32[]{:S(2)}, u32[]{:S(2)}) collective-permute-start(bf16[128,512]{1,0:T(8,128)(2,1)S(1)} %get-tuple-element.69), channel_id=1, source_target_pairs={{0,22},{1,23},{2,20},{3,21},{4,18},{5,19},{6,16},{7,17},{8,30},{9,... | collective-permute-start | bytes 393224 | tf_op jit(solution)/shard_map/ppermute | solution.py:288

commit v6 on v5

--- a/solution.py
+++ b/solution.py
@@ -92,7 +92,7 @@
     centred = (noncore_geno[...].astype(jnp.float32) - 2.0 * noncore_expected).astype(jnp.bfloat16)
     noncore[...] = centred
     copies[4].wait()
-    dosage = geno[...].astype(jnp.float32).T
+    dosage = geno[...].astype(jnp.bfloat16).T.astype(jnp.float32)
     piece[...] = (dosage - 2.0 * expected).astype(jnp.bfloat16)
 
 
@@ -204,33 +204,30 @@
     )(jnp.stack(blocks + [flag, side]).astype(jnp.int32), *operands)
 
 
-def regression_kernel(count, scale, place, kept, got, mine, mine_other, twin, twin_other, *outs):
+def regression_kernel(orders, scale, place, kept, got, mine, mine_other, twin, twin_other, *outs):
     rows = outs[0].shape[0]
-    for j in range(2):
-        left, right = ((mine, mine_other), (twin, twin_other))[j]
-
-        @pl.when(place[count] == j)
-        def _(left=left, right=right):
-            for k in range(count):
-                block = pl.ds(pl.multiple_of(place[k] * rows, rows), rows)
-                value = matmul(kept[block, :], left[...]) + matmul(got[block, :], right[...])
-                outs[k][...] = (value * scale).astype(jnp.bfloat16)
-
-
-def regress(kept, got, mine, mine_other, twin, twin_other, blocks, flag, scale):
-    count, width = len(blocks), mine.shape[1]
+    for i, order in enumerate(orders):
+        for j, (left, right) in enumerate(((mine, mine_other), (twin, twin_other))):
+            @pl.when((place[0] == i) & (place[1] == j))
+            def _(order=order, left=left, right=right):
+                for out, k in zip(outs, order):
+                    block = slice(k * rows, (k + 1) * rows)
+                    value = matmul(kept[block, :], left[...]) + matmul(got[block, :], right[...])
+                    out[...] = (value * scale).astype(jnp.bfloat16)
+
+
+def regress(kept, got, mine, mine_other, twin, twin_other, orders, core, flag, scale):
+    count, width = len(orders[0]), mine.shape[1]
     rows = kept.shape[0] // count
     return pl.pallas_call(
-        functools.partial(regression_kernel, count, scale),
+        functools.partial(regression_kernel, orders, scale),
         in_specs=[pl.BlockSpec(memory_space=pltpu.SMEM)] + [whole()] * 6,
         out_specs=[whole()] * count,
         out_shape=[shape((rows, width))] * count,
         compiler_params=params(),
         cost_estimate=SHORT,
         name="regress",
-    )(
-        jnp.stack([*blocks, flag]).astype(jnp.int32), kept, got, mine, mine_other, twin, twin_other
-    )
+    )(jnp.stack([core, flag]).astype(jnp.int32), kept, got, mine, mine_other, twin, twin_other)
 
 
 def assemble_kernel(jobs, place, *refs):
@@ -375,7 +372,7 @@
     step = [jnp.where(mark == 0, k, l) for k, l in zip(*steps)]
     kept, mine_other = after(kept, mine_other)
     results = regress(
-        kept, across_mark(kept), mine, mine_other, twin, across_mark(twin), step, flag, scale
+        kept, across_mark(kept), mine, mine_other, twin, across_mark(twin), steps, mark, flag, scale
     )
     arrived = [results[0]]
     for i in range(1, size):

time: 81.2 us -> 80.6 us (level)
  other arithmetic: 5.45 us -> 1.64 us
  waiting for transfers between devices: 28.5 us -> 32.2 us
    ppermute x26, waiting for transfers between devices: 28.5 us -> 32.2 us  [move(): return lax.ppermute(array, AXES, pairs)]
    convert_element_type x3, other arithmetic: 3.3 us -> 1.28 us  [permute_body(): (ours[part].astype(jnp.float32) + theirs[part].astype(jnp.float32)).astyp...]
    concatenate x2, other arithmetic: 1.93 us -> 0.07 us  [permute_body(): jnp.concatenate([(ours[part].astype(jnp.float32) + theirs[part].astype(jn...]
  transfers between devices with their start and end apart: 26 -> 26, of which waited for: 11 -> 12; matrix products, arithmetic and copies ran while one was open for 7% -> 2% of each run, Pallas kernels for 13% -> 12%
where the time goes in v6:
time: 80.6 us; the launch traced here: 80.4 us
  waiting for transfers between devices  32.2 us (40%)
  starting transfers between devices  31.9 us (40%)
  Pallas kernels  13.5 us (17%)
  other arithmetic  1.64 us (2%)
  between operations  0.83 us (1%)
    ppermute x26, waiting for transfers between devices, move(): return lax.ppermute(array, AXES, pairs)  32.2 us
    ppermute x26, starting transfers between devices, move(): return lax.ppermute(array, AXES, pairs)  31.9 us
    pallas_call x3, Pallas kernels, absorb(): pl.pallas_call(functools.partial(absorb_kernel, count, len(pairs), ahead,...  8.6 us
    pallas_call x1, Pallas kernels, assemble(): pl.pallas_call(functools.partial(assemble_kernel, [(len(job[0]), job[2])...  1.98 us
    pallas_call x1, Pallas kernels, centre(): pl.pallas_call(centre_kernel, in_specs=[pl.BlockSpec(memory_space=pltpu.S...  1.68 us
  transfers between devices with their start and end apart: 26, of which 12 were waited for; matrix products, arithmetic and copies ran while one was open for 2% of the time, Pallas kernels for 12%

profile of v6, /device:TPU:0, one launch (start us, length us, event | category | flops | bytes accessed | tf_op | source)
XLA Modules:
  0.0 80.4 jit_solution(7124393804019868379)
XLA Ops:
  0.6 1.7 %centre.1 = (bf16[256,512]{1,0:T(8,128)(2,1)S(1)}, bf16[128,256]{1,0:T(8,128)(2,1)S(1)}) custom-call(s32[1]{0:T(128)} %bitcast.20.place, s32[1024,256]{1,0:T(8,128)} %geno.1, s32[5,1024]{1,0:T(8,128)} %codes.1, f32[5,256]{1,0:T(8,128)} %freqs.1, s32[128,256]{1,0:T(8,128)} %noncore_geno.1, s32[5,128]{1,0:T(8,128)} %noncore_codes.1), custom_call_target="tpu_custom_call" | custom-call | tf_op jit(solution)/shard_map/centre/pallas_call | solution.py:103
  2.3 4.1 %collective-permute-start = (bf16[256,512]{1,0:T(8,128)(2,1)S(1)}, bf16[256,512]{1,0:T(8,128)(2,1)S(1)}, u32[]{:S(2)}, u32[]{:S(2)}) collective-permute-start(bf16[256,512]{1,0:T(8,128)(2,1)S(1)} %get-tuple-element.36.refs_0_.refs_5_), channel_id=1, source_target_pairs={{0,8},{1,9},{2,10},{3,11},{4,12},{5,13},{6,14},{7,15},{8,0},{9,1},... | collective-permute-start | bytes 786440 | tf_op jit(solution)/shard_map/ppermute | solution.py:285
  6.4 1.5 %collective-permute-start.1 = (bf16[256,512]{1,0:T(8,128)(2,1)S(1)}, bf16[256,512]{1,0:T(8,128)(2,1)S(1)}, u32[]{:S(2)}, u32[]{:S(2)}) collective-permute-start(bf16[256,512]{1,0:T(8,128)(2,1)S(1)} %get-tuple-element.36.refs_0_.refs_5_), channel_id=1, source_target_pairs={{0,2},{1,3},{2,0},{3,1},{4,6},{5,7},{6,4},{7,5},{8,10},{9,11},{10,... | collective-permute-start | bytes 786440 | tf_op jit(solution)/shard_map/ppermute | solution.py:285
  7.9 1.5 %collective-permute-start.2 = (bf16[128,256]{1,0:T(8,128)(2,1)S(1)}, bf16[128,256]{1,0:T(8,128)(2,1)S(1)}, u32[]{:S(2)}, u32[]{:S(2)}) collective-permute-start(bf16[128,256]{1,0:T(8,128)(2,1)S(1)} %get-tuple-element.37), channel_id=1, source_target_pairs={{0,16},{1,17},{2,18},{3,19},{4,20},{5,21},{6,22},{7,23},{8,24},{9,... | collective-permute-start | bytes 196616 | tf_op jit(solution)/shard_map/ppermute | solution.py:285
  9.4 1.6 %collective-permute-start.3 = (bf16[256,512]{1,0:T(8,128)(2,1)S(1)}, bf16[256,512]{1,0:T(8,128)(2,1)S(1)}, u32[]{:S(2)}, u32[]{:S(2)}) collective-permute-start(bf16[256,512]{1,0:T(8,128)(2,1)S(1)} %get-tuple-element.36.refs_0_.refs_5_), channel_id=1, source_target_pairs={{0,4},{1,5},{2,6},{3,7},{4,0},{5,1},{6,2},{7,3},{8,12},{9,13},{10,... | collective-permute-start | bytes 786440 | tf_op jit(solution)/shard_map/ppermute | solution.py:285
  11.0 1.2 %collective-permute-done.2 = bf16[128,256]{1,0:T(8,128)(2,1)S(1)} collective-permute-done((bf16[128,256]{1,0:T(8,128)(2,1)S(1)}, bf16[128,256]{1,0:T(8,128)(2,1)S(1)}, u32[]{:S(2)}, u32[]{:S(2)}) %collective-permute-start.2) | collective-permute-done | bytes 65568 | tf_op jit(solution)/shard_map/ppermute | solution.py:285
  12.2 6.3 %collective-permute-done.refs_2_.refs_6_ = bf16[256,512]{1,0:T(8,128)(2,1)S(1)} collective-permute-done((bf16[256,512]{1,0:T(8,128)(2,1)S(1)}, bf16[256,512]{1,0:T(8,128)(2,1)S(1)}, u32[]{:S(2)}, u32[]{:S(2)}) %collective-permute-start) | collective-permute-done | bytes 262176 | tf_op jit(solution)/shard_map/ppermute | solution.py:285
  18.5 1.5 %collective-permute-start.5 = (bf16[256,512]{1,0:T(8,128)(2,1)S(1)}, bf16[256,512]{1,0:T(8,128)(2,1)S(1)}, u32[]{:S(2)}, u32[]{:S(2)}) collective-permute-start(bf16[256,512]{1,0:T(8,128)(2,1)S(1)} %collective-permute-done.refs_2_.refs_6_), channel_id=1, source_target_pairs={{0,2},{1,3},{2,0},{3,1},{4,6},{5,7},{6,4},{7,5},{8,10},{9,11},{10,... | collective-permute-start | bytes 786440 | tf_op jit(solution)/shard_map/ppermute | solution.py:285
  21.7 4.1 %absorb.3 = (f32[256,1024]{1,0:T(8,128)S(1)}, bf16[256,512]{1,0:T(8,128)(2,1)S(1)}, bf16[256,512]{1,0:T(8,128)(2,1)S(1)}) custom-call(s32[6]{0:T(128)S(1)} %stack.123.place, bf16[256,512]{1,0:T(8,128)(2,1)S(1)} %get-tuple-element.36.refs_0_.refs_5_, bf16[256,512]{1,0:T(8,128)(2,1)S(1)} %collective-permute-done.1.refs_1_.refs_3_, ...), custom_call_target="tpu_custom_call" | custom-call | tf_op jit(solution)/shard_map/absorb/pallas_call | solution.py:192
  25.8 1.9 %collective-permute-done.5.refs_0_.refs_4_ = bf16[256,512]{1,0:T(8,128)(2,1)S(1)} collective-permute-done((bf16[256,512]{1,0:T(8,128)(2,1)S(1)}, bf16[256,512]{1,0:T(8,128)(2,1)S(1)}, u32[]{:S(2)}, u32[]{:S(2)}) %collective-permute-start.5) | collective-permute-done | bytes 262176 | tf_op jit(solution)/shard_map/ppermute | solution.py:285
  28.5 1.5 %collective-permute-start.11 = (bf16[256,256]{1,0:T(8,128)(2,1)S(1)}, bf16[256,256]{1,0:T(8,128)(2,1)S(1)}, u32[]{:S(2)}, u32[]{:S(2)}) collective-permute-start(bf16[256,256]{1,0:T(8,128)(2,1)S(1)} %pad_maximum_fusion.4.refs_7_.refs_5_), channel_id=1, source_target_pairs={{0,2},{1,3},{2,0},{3,1},{4,6},{5,7},{6,4},{7,5},{8,10},{9,11},{10,... | collective-permute-start | bytes 393224 | tf_op jit(solution)/shard_map/ppermute | solution.py:285
  30.0 2.9 %absorb.4 = (f32[256,1024]{1,0:T(8,128)S(1)}, bf16[256,1024]{1,0:T(8,128)(2,1)S(1)}, bf16[256,1024]{1,0:T(8,128)(2,1)S(1)}, bf16[2,512,1024]{2,1,0:T(8,128)(2,1)S(1)}) custom-call(s32[6]{0:T(128)S(1)} %stack.128.place, bf16[256,512]{1,0:T(8,128)(2,1)S(1)} %collective-permute-done.5.refs_0_.refs_4_, ...), custom_call_target="tpu_custom_call" | custom-call | tf_op jit(solution)/shard_map/absorb/pallas_call | solution.py:192
  33.2 0.9 %collective-permute-done.9.refs_1_.refs_4_ = bf16[256,512]{1,0:T(8,128)(2,1)S(1)} collective-permute-done((bf16[256,512]{1,0:T(8,128)(2,1)S(1)}, bf16[256,512]{1,0:T(8,128)(2,1)S(1)}, u32[]{:S(2)}, u32[]{:S(2)}) %collective-permute-start.9) | collective-permute-done | bytes 262176 | tf_op jit(solution)/shard_map/ppermute | solution.py:285
  34.1 1.6 %absorb.5 = (f32[256,512]{1,0:T(8,128)S(1)}, bf16[256,512]{1,0:T(8,128)(2,1)S(1)}, bf16[256,512]{1,0:T(8,128)(2,1)S(1)}, bf16[256,512]{1,0:T(8,128)(2,1)S(1)}) custom-call(s32[4]{0:T(128)S(1)} %pad_add_fusion.place, bf16[256,512]{1,0:T(8,128)(2,1)S(1)} %collective-permute-done.8.refs_0_.refs_3_, bf16[256,512]{1,0:T(8,128)(2,1)S(1)} %collective-permute-done.9.refs_1_.refs_4_, ...), custom_call_target="tpu_custom_call" | custom-call | tf_op jit(solution)/shard_map/absorb/pallas_call | solution.py:192
  35.7 1.6 %collective-permute-start.12 = (bf16[256,512]{1,0:T(8,128)(2,1)S(1)}, bf16[256,512]{1,0:T(8,128)(2,1)S(1)}, u32[]{:S(2)}, u32[]{:S(2)}) collective-permute-start(bf16[256,512]{1,0:T(8,128)(2,1)S(1)} %get-tuple-element.56), channel_id=1, source_target_pairs={{0,16},{1,17},{2,18},{3,19},{4,20},{5,21},{6,22},{7,23},{8,24},{9,... | collective-permute-start | bytes 786440 | tf_op jit(solution)/shard_map/ppermute | solution.py:285
  37.4 1.0 %add_convert_fusion.4 = (bf16[128,512]{1,0:T(8,128)(2,1)S(1)}, bf16[128,512]{1,0:T(8,128)(2,1)S(1)}) fusion(bf16[256,512]{1,0:T(8,128)(2,1)} %collective-permute-done.4, bf16[256,512]{1,0:T(8,128)(2,1)S(1)} %get-tuple-element.41), kind=kLoop, calls=%fused_computation.8 | loop fusion | flops 524288 | bytes 786432 | tf_op jit(solution)/shard_map/convert_element_type | solution.py:357
  38.5 0.7 collective-permute-start.15
  39.2 4.2 %collective-permute-done.12 = bf16[256,512]{1,0:T(8,128)(2,1)S(1)} collective-permute-done((bf16[256,512]{1,0:T(8,128)(2,1)S(1)}, bf16[256,512]{1,0:T(8,128)(2,1)S(1)}, u32[]{:S(2)}, u32[]{:S(2)}) %collective-permute-start.12) | collective-permute-done | bytes 262176 | tf_op jit(solution)/shard_map/ppermute | solution.py:285
  43.5 3.5 %collective-permute-start.17 = (bf16[256,512]{1,0:T(8,128)(2,1)S(1)}, bf16[256,512]{1,0:T(8,128)(2,1)S(1)}, u32[]{:S(2)}, u32[]{:S(2)}) collective-permute-start(bf16[256,512]{1,0:T(8,128)(2,1)S(1)} %add_convert_fusion.mine), channel_id=1, source_target_pairs={{0,8},{1,9},{2,10},{3,11},{4,12},{5,13},{6,14},{7,15},{8,0},{9,1},... | collective-permute-start | bytes 786440 | tf_op jit(solution)/shard_map/ppermute | solution.py:285
  47.7 1.4 %collective-permute-start.14 = (bf16[128,2048]{1,0:T(8,128)(2,1)S(1)}, bf16[128,2048]{1,0:T(8,128)(2,1)S(1)}, u32[]{:S(2)}, u32[]{:S(2)}) collective-permute-start(bf16[128,2048]{1,0:T(8,128)(2,1)S(1)} %pad_maximum_fusion.1), channel_id=1, source_target_pairs={{0,16},{1,17},{2,18},{3,19},{4,20},{5,21},{6,22},{7,23},{8,24},{9,... | collective-permute-start | bytes 1572872 | tf_op jit(solution)/shard_map/ppermute | solution.py:285
  49.0 10.5 %collective-permute-done.17.twin = bf16[256,512]{1,0:T(8,128)(2,1)S(1)} collective-permute-done((bf16[256,512]{1,0:T(8,128)(2,1)S(1)}, bf16[256,512]{1,0:T(8,128)(2,1)S(1)}, u32[]{:S(2)}, u32[]{:S(2)}) %collective-permute-start.17) | collective-permute-done | bytes 262176 | tf_op jit(solution)/shard_map/ppermute | solution.py:285
  59.6 1.5 %collective-permute-done.18.twin_other = bf16[256,512]{1,0:T(8,128)(2,1)S(1)} collective-permute-done((bf16[256,512]{1,0:T(8,128)(2,1)S(1)}, bf16[256,512]{1,0:T(8,128)(2,1)S(1)}, u32[]{:S(2)}, u32[]{:S(2)}) %collective-permute-start.18) | collective-permute-done | bytes 262176 | tf_op jit(solution)/shard_map/ppermute | solution.py:285
  61.1 1.3 %regress.1 = (bf16[128,512]{1,0:T(8,128)(2,1)S(1)}, bf16[128,512]{1,0:T(8,128)(2,1)S(1)}, bf16[128,512]{1,0:T(8,128)(2,1)S(1)}, bf16[128,512]{1,0:T(8,128)(2,1)S...) custom-call(s32[2]{0:T(128)S(1)} %pad_add_fusion.1.place, ...), custom_call_target="tpu_custom_call" | custom-call | tf_op jit(solution)/shard_map/regress/pallas_call | solution.py:222
  62.4 1.4 %collective-permute-start.19 = (bf16[128,512]{1,0:T(8,128)(2,1)S(1)}, bf16[128,512]{1,0:T(8,128)(2,1)S(1)}, u32[]{:S(2)}, u32[]{:S(2)}) collective-permute-start(bf16[128,512]{1,0:T(8,128)(2,1)S(1)} %get-tuple-element.63), channel_id=1, source_target_pairs={{0,16},{1,5},{2,18},{3,7},{4,20},{5,1},{6,22},{7,3},{8,24},{9,13},... | collective-permute-start | bytes 393224 | tf_op jit(solution)/shard_map/ppermute | solution.py:285
  63.8 0.7 collective-permute-start.20
  64.7 1.5 %collective-permute-start.22 = (bf16[128,512]{1,0:T(8,128)(2,1)S(1)}, bf16[128,512]{1,0:T(8,128)(2,1)S(1)}, u32[]{:S(2)}, u32[]{:S(2)}) collective-permute-start(bf16[128,512]{1,0:T(8,128)(2,1)S(1)} %get-tuple-element.66), channel_id=1, source_target_pairs={{0,18},{1,21},{2,16},{3,23},{4,22},{5,17},{6,20},{7,19},{8,26},{9,... | collective-permute-start | bytes 393224 | tf_op jit(solution)/shard_map/ppermute | solution.py:285
  66.2 2.8 %collective-permute-start.23 = (bf16[128,512]{1,0:T(8,128)(2,1)S(1)}, bf16[128,512]{1,0:T(8,128)(2,1)S(1)}, u32[]{:S(2)}, u32[]{:S(2)}) collective-permute-start(bf16[128,512]{1,0:T(8,128)(2,1)S(1)} %get-tuple-element.67), channel_id=1, source_target_pairs={{0,20},{1,7},{2,22},{3,5},{4,16},{5,3},{6,18},{7,1},{8,28},{9,15},... | collective-permute-start | bytes 393224 | tf_op jit(solution)/shard_map/ppermute | solution.py:285
  69.3 3.9 %collective-permute-start.25 = (bf16[128,512]{1,0:T(8,128)(2,1)S(1)}, bf16[128,512]{1,0:T(8,128)(2,1)S(1)}, u32[]{:S(2)}, u32[]{:S(2)}) collective-permute-start(bf16[128,512]{1,0:T(8,128)(2,1)S(1)} %get-tuple-element.69), channel_id=1, source_target_pairs={{0,22},{1,23},{2,20},{3,21},{4,18},{5,19},{6,16},{7,17},{8,30},{9,... | collective-permute-start | bytes 393224 | tf_op jit(solution)/shard_map/ppermute | solution.py:285
  73.3 0.7 collective-permute-done.23.refs_7_
  74.0 2.3 %collective-permute-done.24.refs_8_ = bf16[128,512]{1,0:T(8,128)(2,1)S(1)} collective-permute-done((bf16[128,512]{1,0:T(8,128)(2,1)S(1)}, bf16[128,512]{1,0:T(8,128)(2,1)S(1)}, u32[]{:S(2)}, u32[]{:S(2)}) %collective-permute-start.24) | collective-permute-done | bytes 131104 | tf_op jit(solution)/shard_map/ppermute | solution.py:285
  76.3 2.1 %collective-permute-done.25.refs_9_ = bf16[128,512]{1,0:T(8,128)(2,1)S(1)} collective-permute-done((bf16[128,512]{1,0:T(8,128)(2,1)S(1)}, bf16[128,512]{1,0:T(8,128)(2,1)S(1)}, u32[]{:S(2)}, u32[]{:S(2)}) %collective-permute-start.25) | collective-permute-done | bytes 131104 | tf_op jit(solution)/shard_map/ppermute | solution.py:285
  78.4 2.0 %assemble.1 = (bf16[128,4096]{1,0:T(8,128)(2,1)}, bf16[128,4096]{1,0:T(8,128)(2,1)}) custom-call(s32[16]{0:T(128)S(1)} %stack.116.place, bf16[128,2048]{1,0:T(8,128)(2,1)S(1)} %pad_maximum_fusion.refs_0_, bf16[128,2048]{1,0:T(8,128)(2,1)S(1)} %collective-permute-done.14.refs_1_, bf16[128,512]{1,0:T(8,128)(2,1)S(1)} %get-tuple-element.62.refs_2_, ...), custom_call_target="tpu_custom_call" | custom-call | tf_op jit(solution)/shard_map/assemble/pallas_call | solution.py:256
  (40 shorter events, 4.2 us)
Async XLA Ops:
  2.3 16.1 %collective-permute-start = (bf16[256,512]{1,0:T(8,128)(2,1)S(1)}, bf16[256,512]{1,0:T(8,128)(2,1)S(1)}, u32[]{:S(2)}, u32[]{:S(2)}) collective-permute-start(bf16[256,512]{1,0:T(8,128)(2,1)S(1)} %get-tuple-element.36.refs_0_.refs_5_), channel_id=1, source_target_pairs={{0,8},{1,9},{2,10},{3,11},{4,12},{5,13},{6,14},{7,15},{8,0},{9,1},... | collective-permute-start | bytes 786440 | tf_op jit(solution)/shard_map/ppermute | solution.py:285
  6.4 12.0 %collective-permute-start.1 = (bf16[256,512]{1,0:T(8,128)(2,1)S(1)}, bf16[256,512]{1,0:T(8,128)(2,1)S(1)}, u32[]{:S(2)}, u32[]{:S(2)}) collective-permute-start(bf16[256,512]{1,0:T(8,128)(2,1)S(1)} %get-tuple-element.36.refs_0_.refs_5_), channel_id=1, source_target_pairs={{0,2},{1,3},{2,0},{3,1},{4,6},{5,7},{6,4},{7,5},{8,10},{9,11},{10,... | collective-permute-start | bytes 786440 | tf_op jit(solution)/shard_map/ppermute | solution.py:285
  7.9 4.3 %collective-permute-start.2 = (bf16[128,256]{1,0:T(8,128)(2,1)S(1)}, bf16[128,256]{1,0:T(8,128)(2,1)S(1)}, u32[]{:S(2)}, u32[]{:S(2)}) collective-permute-start(bf16[128,256]{1,0:T(8,128)(2,1)S(1)} %get-tuple-element.37), channel_id=1, source_target_pairs={{0,16},{1,17},{2,18},{3,19},{4,20},{5,21},{6,22},{7,23},{8,24},{9,... | collective-permute-start | bytes 196616 | tf_op jit(solution)/shard_map/ppermute | solution.py:285
  9.4 11.7 %collective-permute-start.3 = (bf16[256,512]{1,0:T(8,128)(2,1)S(1)}, bf16[256,512]{1,0:T(8,128)(2,1)S(1)}, u32[]{:S(2)}, u32[]{:S(2)}) collective-permute-start(bf16[256,512]{1,0:T(8,128)(2,1)S(1)} %get-tuple-element.36.refs_0_.refs_5_), channel_id=1, source_target_pairs={{0,4},{1,5},{2,6},{3,7},{4,0},{5,1},{6,2},{7,3},{8,12},{9,13},{10,... | collective-permute-start | bytes 786440 | tf_op jit(solution)/shard_map/ppermute | solution.py:285
  18.5 9.2 %collective-permute-start.5 = (bf16[256,512]{1,0:T(8,128)(2,1)S(1)}, bf16[256,512]{1,0:T(8,128)(2,1)S(1)}, u32[]{:S(2)}, u32[]{:S(2)}) collective-permute-start(bf16[256,512]{1,0:T(8,128)(2,1)S(1)} %collective-permute-done.refs_2_.refs_6_), channel_id=1, source_target_pairs={{0,2},{1,3},{2,0},{3,1},{4,6},{5,7},{6,4},{7,5},{8,10},{9,11},{10,... | collective-permute-start | bytes 786440 | tf_op jit(solution)/shard_map/ppermute | solution.py:285
  20.1 8.4 %collective-permute-start.6 = (bf16[256,512]{1,0:T(8,128)(2,1)S(1)}, bf16[256,512]{1,0:T(8,128)(2,1)S(1)}, u32[]{:S(2)}, u32[]{:S(2)}) collective-permute-start(bf16[256,512]{1,0:T(8,128)(2,1)S(1)} %collective-permute-done.refs_2_.refs_6_), channel_id=1, source_target_pairs={{0,4},{1,5},{2,6},{3,7},{4,0},{5,1},{6,2},{7,3},{8,12},{9,13},{10,... | collective-permute-start | bytes 786440 | tf_op jit(solution)/shard_map/ppermute | solution.py:285
  21.1 12.1 %collective-permute-start.8 = (bf16[256,512]{1,0:T(8,128)(2,1)S(1)}, bf16[256,512]{1,0:T(8,128)(2,1)S(1)}, u32[]{:S(2)}, u32[]{:S(2)}) collective-permute-start(bf16[256,512]{1,0:T(8,128)(2,1)S(1)} %collective-permute-done.3.refs_3_.refs_5_), channel_id=1, source_target_pairs={{0,2},{1,3},{2,0},{3,1},{4,6},{5,7},{6,4},{7,5},{8,10},{9,11},{10,... | collective-permute-start | bytes 786440 | tf_op jit(solution)/shard_map/ppermute | solution.py:285
  27.7 6.4 %collective-permute-start.9 = (bf16[256,512]{1,0:T(8,128)(2,1)S(1)}, bf16[256,512]{1,0:T(8,128)(2,1)S(1)}, u32[]{:S(2)}, u32[]{:S(2)}) collective-permute-start(bf16[256,512]{1,0:T(8,128)(2,1)S(1)} %collective-permute-done.5.refs_0_.refs_4_), channel_id=1, source_target_pairs={{0,4},{1,5},{2,6},{3,7},{4,0},{5,1},{6,2},{7,3},{8,12},{9,13},{10,... | collective-permute-start | bytes 786440 | tf_op jit(solution)/shard_map/ppermute | solution.py:285
  28.3 9.1 %collective-permute-start.4 = (bf16[256,512]{1,0:T(8,128)(2,1)S(1)}, bf16[256,512]{1,0:T(8,128)(2,1)}, u32[]{:S(2)}, u32[]{:S(2)}) collective-permute-start(bf16[256,512]{1,0:T(8,128)(2,1)S(1)} %get-tuple-element.42), channel_id=1, source_target_pairs={{0,1},{1,0},{2,3},{3,2},{4,5},{5,4},{6,7},{7,6},{8,9},{9,8},{10,11... | collective-permute-start | bytes 786440 | tf_op jit(solution)/shard_map/ppermute | solution.py:285
  28.5 9.9 %collective-permute-start.11 = (bf16[256,256]{1,0:T(8,128)(2,1)S(1)}, bf16[256,256]{1,0:T(8,128)(2,1)S(1)}, u32[]{:S(2)}, u32[]{:S(2)}) collective-permute-start(bf16[256,256]{1,0:T(8,128)(2,1)S(1)} %pad_maximum_fusion.4.refs_7_.refs_5_), channel_id=1, source_target_pairs={{0,2},{1,3},{2,0},{3,1},{4,6},{5,7},{6,4},{7,5},{8,10},{9,11},{10,... | collective-permute-start | bytes 393224 | tf_op jit(solution)/shard_map/ppermute | solution.py:285
  32.9 14.3 %collective-permute-start.7 = (bf16[256,1024]{1,0:T(8,128)(2,1)S(1)}, bf16[256,1024]{1,0:T(8,128)(2,1)S(1)}, u32[]{:S(2)}, u32[]{:S(2)}) collective-permute-start(bf16[256,1024]{1,0:T(8,128)(2,1)S(1)} %get-tuple-element.48), channel_id=1, source_target_pairs={{0,1},{1,0},{2,3},{3,2},{4,5},{5,4},{6,7},{7,6},{8,9},{9,8},{10,11... | collective-permute-start | bytes 1572872 | tf_op jit(solution)/shard_map/ppermute | solution.py:285
  35.7 7.6 %collective-permute-start.12 = (bf16[256,512]{1,0:T(8,128)(2,1)S(1)}, bf16[256,512]{1,0:T(8,128)(2,1)S(1)}, u32[]{:S(2)}, u32[]{:S(2)}) collective-permute-start(bf16[256,512]{1,0:T(8,128)(2,1)S(1)} %get-tuple-element.56), channel_id=1, source_target_pairs={{0,16},{1,17},{2,18},{3,19},{4,20},{5,21},{6,22},{7,23},{8,24},{9,... | collective-permute-start | bytes 786440 | tf_op jit(solution)/shard_map/ppermute | solution.py:285
  38.4 8.6 %collective-permute-start.10 = (bf16[256,512]{1,0:T(8,128)(2,1)S(1)}, bf16[256,512]{1,0:T(8,128)(2,1)S(1)}, u32[]{:S(2)}, u32[]{:S(2)}) collective-permute-start(bf16[256,512]{1,0:T(8,128)(2,1)S(1)} %get-tuple-element.52), channel_id=1, source_target_pairs={{0,1},{1,0},{2,3},{3,2},{4,5},{5,4},{6,7},{7,6},{8,9},{9,8},{10,11... | collective-permute-start | bytes 786440 | tf_op jit(solution)/shard_map/ppermute | solution.py:285
  38.5 8.8 %collective-permute-start.15 = (bf16[512,256]{1,0:T(8,128)(2,1)S(1)}, bf16[512,256]{1,0:T(8,128)(2,1)S(1)}, u32[]{:S(2)}, u32[]{:S(2)}) collective-permute-start(bf16[512,256]{1,0:T(8,128)(2,1)S(1)} %pad_maximum_fusion.3), channel_id=1, source_target_pairs={{0,4},{1,5},{2,6},{3,7},{4,0},{5,1},{6,2},{7,3},{8,12},{9,13},{10,... | collective-permute-start | bytes 786440 | tf_op jit(solution)/shard_map/ppermute | solution.py:285
  43.4 4.0 %collective-permute-start.13 = (bf16[256,512]{1,0:T(8,128)(2,1)S(1)}, bf16[256,512]{1,0:T(8,128)(2,1)S(1)}, u32[]{:S(2)}, u32[]{:S(2)}) collective-permute-start(bf16[256,512]{1,0:T(8,128)(2,1)S(1)} %add_convert_fusion.mine), channel_id=1, source_target_pairs={{0,1},{1,0},{2,3},{3,2},{4,5},{5,4},{6,7},{7,6},{8,9},{9,8},{10,11... | collective-permute-start | bytes 786440 | tf_op jit(solution)/shard_map/ppermute | solution.py:285
  43.5 16.1 %collective-permute-start.17 = (bf16[256,512]{1,0:T(8,128)(2,1)S(1)}, bf16[256,512]{1,0:T(8,128)(2,1)S(1)}, u32[]{:S(2)}, u32[]{:S(2)}) collective-permute-start(bf16[256,512]{1,0:T(8,128)(2,1)S(1)} %add_convert_fusion.mine), channel_id=1, source_target_pairs={{0,8},{1,9},{2,10},{3,11},{4,12},{5,13},{6,14},{7,15},{8,0},{9,1},... | collective-permute-start | bytes 786440 | tf_op jit(solution)/shard_map/ppermute | solution.py:285
  47.4 13.7 %collective-permute-start.16 = (bf16[1024,256]{1,0:T(8,128)(2,1)S(1)}, bf16[1024,256]{1,0:T(8,128)(2,1)S(1)}, u32[]{:S(2)}, u32[]{:S(2)}) collective-permute-start(bf16[1024,256]{1,0:T(8,128)(2,1)S(1)} %pad_maximum_fusion.2.kept), channel_id=1, source_target_pairs={{0,1},{1,0},{2,3},{3,2},{4,5},{5,4},{6,7},{7,6},{8,9},{9,8},{10,11... | collective-permute-start | bytes 1572872 | tf_op jit(solution)/shard_map/ppermute | solution.py:285
  47.7 18.5 %collective-permute-start.14 = (bf16[128,2048]{1,0:T(8,128)(2,1)S(1)}, bf16[128,2048]{1,0:T(8,128)(2,1)S(1)}, u32[]{:S(2)}, u32[]{:S(2)}) collective-permute-start(bf16[128,2048]{1,0:T(8,128)(2,1)S(1)} %pad_maximum_fusion.1), channel_id=1, source_target_pairs={{0,16},{1,17},{2,18},{3,19},{4,20},{5,21},{6,22},{7,23},{8,24},{9,... | collective-permute-start | bytes 1572872 | tf_op jit(solution)/shard_map/ppermute | solution.py:285
  59.6 1.5 %collective-permute-start.18 = (bf16[256,512]{1,0:T(8,128)(2,1)S(1)}, bf16[256,512]{1,0:T(8,128)(2,1)S(1)}, u32[]{:S(2)}, u32[]{:S(2)}) collective-permute-start(bf16[256,512]{1,0:T(8,128)(2,1)S(1)} %collective-permute-done.17.twin), channel_id=1, source_target_pairs={{0,1},{1,0},{2,3},{3,2},{4,5},{5,4},{6,7},{7,6},{8,9},{9,8},{10,11... | collective-permute-start | bytes 786440 | tf_op jit(solution)/shard_map/ppermute | solution.py:285
  62.4 6.6 %collective-permute-start.19 = (bf16[128,512]{1,0:T(8,128)(2,1)S(1)}, bf16[128,512]{1,0:T(8,128)(2,1)S(1)}, u32[]{:S(2)}, u32[]{:S(2)}) collective-permute-start(bf16[128,512]{1,0:T(8,128)(2,1)S(1)} %get-tuple-element.63), channel_id=1, source_target_pairs={{0,16},{1,5},{2,18},{3,7},{4,20},{5,1},{6,22},{7,3},{8,24},{9,13},... | collective-permute-start | bytes 393224 | tf_op jit(solution)/shard_map/ppermute | solution.py:285
  63.8 5.5 %collective-permute-start.20 = (bf16[128,512]{1,0:T(8,128)(2,1)S(1)}, bf16[128,512]{1,0:T(8,128)(2,1)S(1)}, u32[]{:S(2)}, u32[]{:S(2)}) collective-permute-start(bf16[128,512]{1,0:T(8,128)(2,1)S(1)} %get-tuple-element.64), channel_id=1, source_target_pairs={{0,2},{1,17},{2,0},{3,19},{4,6},{5,21},{6,4},{7,23},{8,10},{9,25},... | collective-permute-start | bytes 393224 | tf_op jit(solution)/shard_map/ppermute | solution.py:285
  64.6 8.7 %collective-permute-start.21 = (bf16[128,512]{1,0:T(8,128)(2,1)S(1)}, bf16[128,512]{1,0:T(8,128)(2,1)S(1)}, u32[]{:S(2)}, u32[]{:S(2)}) collective-permute-start(bf16[128,512]{1,0:T(8,128)(2,1)S(1)} %get-tuple-element.65), channel_id=1, source_target_pairs={{0,4},{1,3},{2,6},{3,1},{4,0},{5,7},{6,2},{7,5},{8,12},{9,11},{10,... | collective-permute-start | bytes 393224 | tf_op jit(solution)/shard_map/ppermute | solution.py:285
  64.7 8.6 %collective-permute-start.22 = (bf16[128,512]{1,0:T(8,128)(2,1)S(1)}, bf16[128,512]{1,0:T(8,128)(2,1)S(1)}, u32[]{:S(2)}, u32[]{:S(2)}) collective-permute-start(bf16[128,512]{1,0:T(8,128)(2,1)S(1)} %get-tuple-element.66), channel_id=1, source_target_pairs={{0,18},{1,21},{2,16},{3,23},{4,22},{5,17},{6,20},{7,19},{8,26},{9,... | collective-permute-start | bytes 393224 | tf_op jit(solution)/shard_map/ppermute | solution.py:285
  66.2 7.8 %collective-permute-start.23 = (bf16[128,512]{1,0:T(8,128)(2,1)S(1)}, bf16[128,512]{1,0:T(8,128)(2,1)S(1)}, u32[]{:S(2)}, u32[]{:S(2)}) collective-permute-start(bf16[128,512]{1,0:T(8,128)(2,1)S(1)} %get-tuple-element.67), channel_id=1, source_target_pairs={{0,20},{1,7},{2,22},{3,5},{4,16},{5,3},{6,18},{7,1},{8,28},{9,15},... | collective-permute-start | bytes 393224 | tf_op jit(solution)/shard_map/ppermute | solution.py:285
  69.0 7.4 %collective-permute-start.24 = (bf16[128,512]{1,0:T(8,128)(2,1)S(1)}, bf16[128,512]{1,0:T(8,128)(2,1)S(1)}, u32[]{:S(2)}, u32[]{:S(2)}) collective-permute-start(bf16[128,512]{1,0:T(8,128)(2,1)S(1)} %get-tuple-element.68), channel_id=1, source_target_pairs={{0,6},{1,19},{2,4},{3,17},{4,2},{5,23},{6,0},{7,21},{8,14},{9,27},... | collective-permute-start | bytes 393224 | tf_op jit(solution)/shard_map/ppermute | solution.py:285
  69.3 9.1 %collective-permute-start.25 = (bf16[128,512]{1,0:T(8,128)(2,1)S(1)}, bf16[128,512]{1,0:T(8,128)(2,1)S(1)}, u32[]{:S(2)}, u32[]{:S(2)}) collective-permute-start(bf16[128,512]{1,0:T(8,128)(2,1)S(1)} %get-tuple-element.69), channel_id=1, source_target_pairs={{0,22},{1,23},{2,20},{3,21},{4,18},{5,19},{6,16},{7,17},{8,30},{9,... | collective-permute-start | bytes 393224 | tf_op jit(solution)/shard_map/ppermute | solution.py:285
